TPU v7x, 32 devices: a whole 2x2x4 slice. The times are simulated.
32 devices in a mesh: dp: 8 (over z, x), tensor: 4 (over y, core).
Axes of the slice: x: 2, y: 2, z: 4, core: 2. Of those that a mesh axis runs over, the one named last changes fastest.
Arguments:
- tokens: bfloat16 [13312, 768], P(('dp', 'tensor')), may hold values from -6 to 6
- out_grad: bfloat16 [13312, 768], P(('dp', 'tensor')), may hold values from -6 to 6
- image_lengths: int32 [16, 4], P('dp'), may hold values from 0 to 576, as said below
- norm1_gain: float32 [2, 768], replicated, may hold values from 0.5 to 1.5
- norm1_bias: float32 [2, 768], replicated, may hold values from -3 to 3
- qkv_weight: bfloat16 [2, 3, 768, 768], P(None, None, None, 'tensor'), may hold values from -0.21875 to 0.21875
- qkv_bias: float32 [2, 3, 768], P(None, None, 'tensor'), may hold values from -3 to 3
- rope_freqs: float32 [2, 2, 384], P(None, None, 'tensor'), may hold values from -1 to 1
- out_weight: bfloat16 [2, 768, 768], P(None, 'tensor'), may hold values from -1.75 to 1.75
- out_bias: float32 [2, 768], replicated, may hold values from -3 to 3
- norm2_gain: float32 [2, 768], replicated, may hold values from 0.5 to 1.5
- norm2_bias: float32 [2, 768], replicated, may hold values from -3 to 3
- up_weight: bfloat16 [2, 768, 3072], P(None, None, 'tensor'), may hold values from -0.21875 to 0.21875
- up_bias: float32 [2, 3072], P(None, 'tensor'), may hold values from -3 to 3
- down_weight: bfloat16 [2, 3072, 768], P(None, 'tensor'), may hold values from -0.109375 to 0.109375
- down_bias: float32 [2, 768], replicated, may hold values from -3 to 3
Outputs:
- activations: bfloat16 [13312, 768], P(('dp', 'tensor'))
- input_grad: float32 [13312, 768], P(('dp', 'tensor'))
- norm1_gain_grad: float32 [2, 768], replicated
- norm1_bias_grad: float32 [2, 768], replicated
- qkv_weight_grad: float32 [2, 3, 768, 768], P(None, None, None, 'tensor')
- qkv_bias_grad: float32 [2, 3, 768], P(None, None, 'tensor')
- rope_freqs_grad: float32 [2, 2, 384], P(None, None, 'tensor')
- out_weight_grad: float32 [2, 768, 768], P(None, 'tensor')
- out_bias_grad: float32 [2, 768], replicated
- norm2_gain_grad: float32 [2, 768], replicated
- norm2_bias_grad: float32 [2, 768], replicated
- up_weight_grad: float32 [2, 768, 3072], P(None, None, 'tensor')
- up_bias_grad: float32 [2, 3072], P(None, 'tensor')
- down_weight_grad: float32 [2, 3072, 768], P(None, 'tensor')
- down_bias_grad: float32 [2, 768], replicated
Inputs may be any that keep to these rules, and one draw needn't show every extreme that they name: `image_lengths`: in each row the nonzero lengths come first, each 196, 400 or 576; the first is never zero; a row sums to at most 832.
All inputs are finite; a program needn't handle non-finite values.
Results may differ from a plain program's by a relative error of at most 0.024.
Values may be sent and summed in bfloat16 or wider, within the bound.
No kernel may reach another device: no remote copies, remote signals or barrier semaphores. Data moves between devices by JAX's collectives and lax.ppermute only.
A program may use at most 192 MiB of HBM per device.

v0:
```python
from functools import partial

import jax
import jax.numpy as jnp
from jax import lax
from jax.sharding import PartitionSpec as P

HEAD_DIM = 64
LEN = 832
SIDE_S = 14
SIDE_M = 20
SIDE_L = 24
MAX_IMAGES = 4
LAYERS = 2


EPS = 1e-06
NEGATIVE = -1000000000.0


def normalize(values, gain, shift):
    average = jnp.mean(values, axis=-1, keepdims=True)
    centred = values - average
    variance = jnp.mean(centred * centred, axis=-1, keepdims=True)
    return centred * lax.rsqrt(variance + EPS) * gain + shift


def places(lengths):
    image_ends = jnp.cumsum(lengths, axis=1)
    image_starts = image_ends - lengths
    position = jnp.arange(LEN, dtype=jnp.int32)
    segment = jnp.sum((position[None, :, None] >= image_ends[:, None, :]).astype(jnp.int32), axis=2)
    belongs = segment[:, :, None] == jnp.arange(MAX_IMAGES, dtype=jnp.int32)[None, None, :]
    begin_at = jnp.sum(jnp.where(belongs, image_starts[:, None, :], 0), axis=2)
    image_size = jnp.sum(jnp.where(belongs, lengths[:, None, :], 0), axis=2)
    image_side = jnp.where(
        image_size == SIDE_S * SIDE_S,
        SIDE_S,
        jnp.where(image_size == SIDE_M * SIDE_M, SIDE_M, SIDE_L),
    ).astype(jnp.int32)
    offset = position[None, :] - begin_at
    inside = segment < MAX_IMAGES
    row_at = jnp.where(inside, offset // image_side, 0)
    column_at = jnp.where(inside, offset % image_side, 0)
    return (segment, row_at, column_at)


def rotate(values, freqs, row_at, column_at):
    half_dim = values.shape[-1] // 2
    freq_table = freqs.reshape(2, -1, half_dim)
    angles = (
        row_at.astype(jnp.float32)[..., None, None] * freq_table[0]
        + column_at.astype(jnp.float32)[..., None, None] * freq_table[1]
    )
    cosine = jnp.cos(angles)
    sine_part = jnp.sin(angles)
    first_half = values[..., :half_dim]
    second_half = values[..., half_dim:]
    return jnp.concatenate(
        [
            first_half * cosine - second_half * sine_part,
            first_half * sine_part + second_half * cosine,
        ],
        axis=-1,
    )


def spread(row_share):
    return lax.all_gather(row_share, "tensor", axis=0, tiled=True)


def spread_back(row_share):
    return lax.all_gather(row_share, "tensor", axis=0, tiled=True)


def collect(left_side, right_side):
    share_rows = left_side.shape[0] // lax.axis_size("tensor")

    def partial_term(begin_at, row_count):
        return jnp.dot(left_side, right_side, preferred_element_type=jnp.float32)

    return lax.psum_scatter(
        partial_term(jnp.int32(0), share_rows * lax.axis_size("tensor")).astype(jnp.bfloat16),
        "tensor",
        scatter_dimension=0,
        tiled=True,
    ).astype(jnp.float32)


def collect_back(grad_stack, weight_stack):
    share_rows = grad_stack.shape[1] // lax.axis_size("tensor")

    def partial_term(begin_at, row_count):
        return jnp.einsum(
            "kte,kde->td", grad_stack, weight_stack, preferred_element_type=jnp.float32
        )

    return lax.psum_scatter(
        partial_term(jnp.int32(0), share_rows * lax.axis_size("tensor")).astype(jnp.bfloat16),
        "tensor",
        scatter_dimension=0,
        tiled=True,
    ).astype(jnp.float32)


def masked_scores(turned_q, turned_k, segment):
    scaling = turned_q.shape[-1] ** (-0.5)
    scores = (
        jnp.einsum("qhe,khe->hqk", turned_q, turned_k, preferred_element_type=jnp.float32) * scaling
    )
    allowed = segment[:, None] == segment[None, :]
    return jnp.where(allowed[None], scores, NEGATIVE)


def attend(pieces):
    turned_q, turned_k, value_part, segment = pieces
    scores = masked_scores(turned_q, turned_k, segment)
    highest = jnp.max(scores, axis=-1, keepdims=True)
    exp_scores = jnp.exp(scores - highest)
    totals = jnp.sum(exp_scores, axis=-1, keepdims=True)
    attn_probs = (exp_scores / totals).astype(jnp.bfloat16)
    mixed_heads = jnp.einsum(
        "hqk,khe->qhe", attn_probs, value_part, preferred_element_type=jnp.float32
    ).astype(jnp.bfloat16)
    return (mixed_heads, (highest + jnp.log(totals))[..., 0])


def attend_back(pieces):
    turned_q, turned_k, value_part, segment, log_totals, grad_mixed = pieces
    scaling = turned_q.shape[-1] ** (-0.5)
    scores = masked_scores(turned_q, turned_k, segment)
    attn_probs = jnp.exp(scores - log_totals[..., None])
    low_probs = attn_probs.astype(jnp.bfloat16)
    grad_value = jnp.einsum(
        "hqk,qhe->khe", low_probs, grad_mixed, preferred_element_type=jnp.float32
    )
    grad_probs = jnp.einsum(
        "qhe,khe->hqk", grad_mixed, value_part, preferred_element_type=jnp.float32
    )
    grad_scores = (
        attn_probs * (grad_probs - jnp.sum(attn_probs * grad_probs, axis=-1, keepdims=True))
    ).astype(jnp.bfloat16)
    grad_turned_q = (
        jnp.einsum("hqk,khe->qhe", grad_scores, turned_k, preferred_element_type=jnp.float32)
        * scaling
    )
    grad_turned_k = (
        jnp.einsum("hqk,qhe->khe", grad_scores, turned_q, preferred_element_type=jnp.float32)
        * scaling
    )
    return (grad_turned_q, grad_turned_k, grad_value)


def transpose_dot(left_side, right_side):
    return lax.dot_general(
        left_side, right_side, (((1,), (1,)), ((), ())), preferred_element_type=jnp.float32
    )


def norm_grads(values, gain, shift, incoming):
    norm_value, norm_back = jax.vjp(normalize, values, gain, shift)
    grad_through, grad_gain, grad_shift = norm_back(incoming)
    return (grad_through, grad_gain, grad_shift)


def body(
    tokens,
    out_grad,
    image_lengths,
    norm1_gain,
    norm1_bias,
    qkv_weight,
    qkv_bias,
    rope_freqs,
    out_weight,
    out_bias,
    norm2_gain,
    norm2_bias,
    up_weight,
    up_bias,
    down_weight,
    down_bias,
):
    seqs_here = image_lengths.shape[0]
    heads_here = qkv_weight.shape[3] // HEAD_DIM
    head_shape = (seqs_here, LEN, heads_here, HEAD_DIM)
    segment, row_at, column_at = places(image_lengths)
    current = tokens.astype(jnp.float32)
    kept_layers = []
    for layer_at in range(LAYERS):
        inputs = current
        normed = spread(
            normalize(inputs, norm1_gain[layer_at], norm1_bias[layer_at]).astype(jnp.bfloat16)
        )
        projected = jnp.einsum(
            "td,kde->kte", normed, qkv_weight[layer_at], preferred_element_type=jnp.float32
        )
        projected = projected + qkv_bias[layer_at][:, None, :]
        query_part = projected[0].reshape(head_shape)
        key_part = projected[1].reshape(head_shape)
        value_part = projected[2].astype(jnp.bfloat16).reshape(head_shape)
        turned_q = rotate(query_part, rope_freqs[layer_at], row_at, column_at).astype(jnp.bfloat16)
        turned_k = rotate(key_part, rope_freqs[layer_at], row_at, column_at).astype(jnp.bfloat16)
        mixed_heads, log_totals = lax.map(attend, (turned_q, turned_k, value_part, segment))
        mixed_heads = mixed_heads.reshape(-1, heads_here * HEAD_DIM)
        middle = inputs + collect(mixed_heads, out_weight[layer_at]) + out_bias[layer_at]
        normed_mlp = spread(
            normalize(middle, norm2_gain[layer_at], norm2_bias[layer_at]).astype(jnp.bfloat16)
        )
        pre_gelu = (
            jnp.dot(normed_mlp, up_weight[layer_at], preferred_element_type=jnp.float32)
            + up_bias[layer_at]
        )
        active = jax.nn.gelu(pre_gelu, approximate=False).astype(jnp.bfloat16)
        current = middle + collect(active, down_weight[layer_at]) + down_bias[layer_at]
        kept_layers.append(
            (
                inputs,
                normed,
                query_part,
                key_part,
                turned_q,
                turned_k,
                value_part,
                log_totals,
                mixed_heads,
                middle,
                normed_mlp,
                pre_gelu,
                active,
            )
        )
    activations = current.astype(jnp.bfloat16)
    gradient = out_grad.astype(jnp.float32)
    sharded_grads = [None] * LAYERS
    shared_grads = [None] * LAYERS
    for layer_at in reversed(range(LAYERS)):
        (
            inputs,
            normed,
            query_part,
            key_part,
            turned_q,
            turned_k,
            value_part,
            log_totals,
            mixed_heads,
            middle,
            normed_mlp,
            pre_gelu,
            active,
        ) = kept_layers[layer_at]
        grad_mlp_out = gradient.astype(jnp.bfloat16)
        grad_down_bias = jnp.sum(grad_mlp_out.astype(jnp.float32), axis=0)
        grad_mlp_all = spread_back(grad_mlp_out)
        grad_down = jnp.einsum(
            "tf,td->fd", active, grad_mlp_all, preferred_element_type=jnp.float32
        )
        grad_active = transpose_dot(grad_mlp_all, down_weight[layer_at])
        gelu_value, gelu_back = jax.vjp(partial(jax.nn.gelu, approximate=False), pre_gelu)
        grad_pre_gelu = gelu_back(grad_active)[0].astype(jnp.bfloat16)
        grad_up = jnp.einsum(
            "td,tf->df", normed_mlp, grad_pre_gelu, preferred_element_type=jnp.float32
        )
        grad_up_bias = jnp.sum(grad_pre_gelu.astype(jnp.float32), axis=0)
        grad_normed_mlp = collect_back(grad_pre_gelu[None], up_weight[layer_at][None])
        grad_through, grad_gain2, grad_shift2 = norm_grads(
            middle, norm2_gain[layer_at], norm2_bias[layer_at], grad_normed_mlp
        )
        grad_middle = gradient + grad_through
        grad_attn_out = grad_middle.astype(jnp.bfloat16)
        grad_out_bias = jnp.sum(grad_attn_out.astype(jnp.float32), axis=0)
        grad_attn_all = spread_back(grad_attn_out)
        grad_out = jnp.einsum(
            "te,td->ed", mixed_heads, grad_attn_all, preferred_element_type=jnp.float32
        )
        grad_mixed = (
            transpose_dot(grad_attn_all, out_weight[layer_at])
            .astype(jnp.bfloat16)
            .reshape(head_shape)
        )
        grad_turned_q, grad_turned_k, grad_value = lax.map(
            attend_back, (turned_q, turned_k, value_part, segment, log_totals, grad_mixed)
        )

        def turn_both(query_in, key_in, freqs):
            return (
                rotate(query_in, freqs, row_at, column_at),
                rotate(key_in, freqs, row_at, column_at),
            )

        turn_value, turn_back = jax.vjp(turn_both, query_part, key_part, rope_freqs[layer_at])
        grad_query, grad_key, grad_freqs = turn_back((grad_turned_q, grad_turned_k))
        grad_proj = jnp.stack([grad_query, grad_key, grad_value]).astype(jnp.bfloat16)
        grad_proj = grad_proj.reshape(3, -1, heads_here * HEAD_DIM)
        grad_qkv = jnp.einsum("td,kte->kde", normed, grad_proj, preferred_element_type=jnp.float32)
        grad_qkv_bias = jnp.sum(grad_proj.astype(jnp.float32), axis=1)
        grad_normed = collect_back(grad_proj, qkv_weight[layer_at])
        grad_inside, grad_gain1, grad_shift1 = norm_grads(
            inputs, norm1_gain[layer_at], norm1_bias[layer_at], grad_normed
        )
        gradient = grad_middle + grad_inside
        layer_sharded = (
            grad_qkv,
            grad_qkv_bias,
            grad_freqs,
            grad_out,
            grad_up,
            grad_up_bias,
            grad_down,
        )
        layer_shared = (
            grad_gain1,
            grad_shift1,
            grad_out_bias,
            grad_gain2,
            grad_shift2,
            grad_down_bias,
        )
        sharded_grads[layer_at] = layer_sharded
        shared_grads[layer_at] = layer_shared
    sharded_stacked = tuple(
        (
            jnp.stack([sharded_grads[layer_at][item] for layer_at in range(LAYERS)])
            for item in range(7)
        )
    )
    shared_stacked = tuple(
        (
            jnp.stack([shared_grads[layer_at][item] for layer_at in range(LAYERS)])
            for item in range(6)
        )
    )
    sharded_stacked = lax.psum(sharded_stacked, "dp")
    shared_stacked = lax.psum(shared_stacked, ("dp", "tensor"))
    return (
        activations,
        gradient,
        shared_stacked[0],
        shared_stacked[1],
        sharded_stacked[0],
        sharded_stacked[1],
        sharded_stacked[2],
        sharded_stacked[3],
        shared_stacked[2],
        shared_stacked[3],
        shared_stacked[4],
        sharded_stacked[4],
        sharded_stacked[5],
        sharded_stacked[6],
        shared_stacked[5],
    )


def solution(mesh):
    in_specs = (
        P(("dp", "tensor"), None),
        P(("dp", "tensor"), None),
        P("dp", None),
        P(),
        P(),
        P(None, None, None, "tensor"),
        P(None, None, "tensor"),
        P(None, None, "tensor"),
        P(None, "tensor", None),
        P(),
        P(),
        P(),
        P(None, None, "tensor"),
        P(None, "tensor"),
        P(None, "tensor", None),
        P(),
    )
    out_specs = (
        P(("dp", "tensor"), None),
        P(("dp", "tensor"), None),
        P(),
        P(),
        P(None, None, None, "tensor"),
        P(None, None, "tensor"),
        P(None, None, "tensor"),
        P(None, "tensor", None),
        P(),
        P(),
        P(),
        P(None, None, "tensor"),
        P(None, "tensor"),
        P(None, "tensor", None),
        P(),
    )
    return jax.shard_map(body, mesh=mesh, in_specs=in_specs, out_specs=out_specs, check_vma=False)
```

profile of v0, /device:TPU:0, one launch (start us, length us, event | category | flops | bytes accessed | tf_op | source)
XLA Modules:
  0.0 1248.2 jit_solution(12349753236207467933)
XLA Ops:
  18.3 24.6 %all-gather.9.cloned.1.call-done = bf16[1664,768]{1,0:T(8,128)(2,1)} async-done(((bf16[416,768]{1,0:T(8,128)(2,1)}), bf16[1664,768]{1,0:T(8,128)(2,1)}) %all-gather.9.cloned.1.call-update) | async-done | bytes 2555920 | tf_op jit(solution)/shard_map/all_gather | solution.py:69
  57.2 14.8 %while.52 = (s32[]{:T(128)}, bf16[2,832,3,64]{1,3,2,0:T(8,128)(2,1)S(1)}, f32[2,3,832]{2,1,0:T(4,128)S(1)}, bf16[2,832,3,64]{1,3,2,0:T(8,128)(2,1)S(1)}, s32[2,8...) while((s32[]{:T(128)}, ...), condition=%wide.region_9.10_spmd, body=%wide.region_6.9_spmd.sunk | while | flops 557397568 | bytes 29924452 | solution.py:204
  79.0 32.9 %reduce-scatter.9.cloned.1.call-done = bf16[416,768]{1,0:T(8,128)(2,1)} async-done(((bf16[1664,768]{1,0:T(8,128)(2,1)}), bf16[416,768]{1,0:T(8,128)(2,1)}) %reduce-scatter.9.cloned.1.call-update) | async-done | bytes 638992 | tf_op jit(solution)/shard_map/reduce_scatter | solution.py:82
  116.8 24.7 %all-gather.11.cloned.1.call-done = bf16[1664,768]{1,0:T(8,128)(2,1)} async-done(((bf16[416,768]{1,0:T(8,128)(2,1)}), bf16[1664,768]{1,0:T(8,128)(2,1)}) %all-gather.11.cloned.1.call-update) | async-done | bytes 2555920 | tf_op jit(solution)/shard_map/all_gather | solution.py:69
  141.5 15.5 %multiply_convert_fusion.3 = (bf16[1664,768]{1,0:T(8,128)(2,1)S(1)}, f32[1664,768]{1,0:T(8,128)}, f32[1664,768]{1,0:T(8,128)}) fusion(f32[768]{0:T(1024)S(1)} %get-tuple-element.375, bf16[1664,768]{1,0:T(8,128)(2,1)} %all-gather.11.cloned.1.call-done, bf16[2,768,768]{2,1,0:T(8,128)(2,1)} %param.36), kind=kOutput, calls=%fused_computation.149 | convolution fusion | flops 2047279104 | bytes 16518144 | tf_op jit(solution)/shard_map/dot_general | solution.py:211
  163.5 33.1 %reduce-scatter.11.cloned.1.call-done = bf16[416,768]{1,0:T(8,128)(2,1)} async-done(((bf16[1664,768]{1,0:T(8,128)(2,1)}), bf16[416,768]{1,0:T(8,128)(2,1)}) %reduce-scatter.11.cloned.1.call-update) | async-done | bytes 638992 | tf_op jit(solution)/shard_map/reduce_scatter | solution.py:82
  199.8 25.1 %all-gather.13.cloned.1.call-done = bf16[1664,768]{1,0:T(8,128)(2,1)} async-done(((bf16[416,768]{1,0:T(8,128)(2,1)}), bf16[1664,768]{1,0:T(8,128)(2,1)}) %all-gather.13.cloned.1.call-update) | async-done | bytes 2555920 | tf_op jit(solution)/shard_map/all_gather | solution.py:69
  246.5 16.4 %while.53 = (s32[]{:T(128)}, bf16[2,832,3,64]{1,3,2,0:T(8,128)(2,1)}, f32[2,3,832]{2,1,0:T(4,128)S(1)}, bf16[2,832,3,64]{1,3,2,0:T(8,128)(2,1)S(1)}, s32[2,832]{...) while((s32[]{:T(128)}, ...), condition=%wide.region_19.20_spmd, body=%wide.region_16.19_spmd.sunk | while | flops 557397568 | bytes 35036316 | solution.py:204
  272.4 34.3 %reduce-scatter.13.cloned.1.call-done = bf16[416,768]{1,0:T(8,128)(2,1)} async-done(((bf16[1664,768]{1,0:T(8,128)(2,1)}), bf16[416,768]{1,0:T(8,128)(2,1)}) %reduce-scatter.13.cloned.1.call-update) | async-done | bytes 638992 | tf_op jit(solution)/shard_map/reduce_scatter | solution.py:82
  311.0 24.6 %all-gather.15.cloned.1.call-done = bf16[1664,768]{1,0:T(8,128)(2,1)} async-done(((bf16[416,768]{1,0:T(8,128)(2,1)}), bf16[1664,768]{1,0:T(8,128)(2,1)}) %all-gather.15.cloned.1.call-update) | async-done | bytes 2555920 | tf_op jit(solution)/shard_map/all_gather | solution.py:69
  335.6 16.3 %multiply_convert_fusion.2 = (bf16[1664,768]{1,0:T(8,128)(2,1)}, f32[1664,768]{1,0:T(8,128)}, f32[1664,768]{1,0:T(8,128)}) fusion(f32[768]{0:T(1024)S(1)} %copy-done.156, bf16[1664,768]{1,0:T(8,128)(2,1)} %all-gather.15.cloned.1.call-done, bf16[2,768,768]{2,1,0:T(8,128)(2,1)} %param.36), kind=kOutput, calls=%fused_computation.136 | convolution fusion | flops 2047279104 | bytes 16518144 | tf_op jit(solution)/shard_map/dot_general | solution.py:211
  351.8 10.6 all-gather.17.cloned.1.call-done
  362.4 9.5 convert_reduce_fusion
  377.4 5.7 convolution_convert_fusion.2
  383.1 28.5 %reduce-scatter.17.cloned.1.call-done = bf16[416,768]{1,0:T(8,128)(2,1)} async-done(((bf16[1664,768]{1,0:T(8,128)(2,1)}), bf16[416,768]{1,0:T(8,128)(2,1)}) %reduce-scatter.17.cloned.1.call-update) | async-done | bytes 638992 | tf_op jit(solution)/shard_map/reduce_scatter | solution.py:98
  413.8 35.0 %reduce-scatter.15.cloned.1.call-done = bf16[416,768]{1,0:T(8,128)(2,1)} async-done(((bf16[1664,768]{1,0:T(8,128)(2,1)}), bf16[416,768]{1,0:T(8,128)(2,1)}) %reduce-scatter.15.cloned.1.call-update) | async-done | bytes 638992 | tf_op jit(solution)/shard_map/reduce_scatter | solution.py:82
  455.5 24.3 %all-gather.19.cloned.1.call-done = bf16[1664,768]{1,0:T(8,128)(2,1)} async-done(((bf16[416,768]{1,0:T(8,128)(2,1)}), bf16[1664,768]{1,0:T(8,128)(2,1)}) %all-gather.19.cloned.1.call-update) | async-done | bytes 2555920 | tf_op jit(solution)/shard_map/all_gather | solution.py:73
  489.8 29.1 %while.54 = (s32[]{:T(128)}, f32[2,832,3,64]{1,3,2,0:T(8,128)}, f32[2,832,3,64]{1,3,2,0:T(8,128)}, bf16[2,832,3,64]{1,3,2,0:T(8,128)(2,1)}, bf16[2,832,3,64]{1,3...) while((s32[]{:T(128)}, f32[2,832,3,64]{1,3,2,0:T(8,128)}, ...), condition=%wide.region_29.30_spmd, body=%wide.region_27.29_spmd.sunk | while | flops 1361229312 | bytes 86945512 | solution.py:282
  521.4 5.3 multiply_add_fusion
  526.8 3.9 multiply_add_fusion.1
  539.2 34.4 %reduce-scatter.19.cloned.1.call-done = bf16[416,768]{1,0:T(8,128)(2,1)} async-done(((bf16[1664,768]{1,0:T(8,128)(2,1)}), bf16[416,768]{1,0:T(8,128)(2,1)}) %reduce-scatter.19.cloned.1.call-update) | async-done | bytes 638992 | tf_op jit(solution)/shard_map/reduce_scatter | solution.py:98
  582.1 24.8 %all-gather.21.cloned.1.call-done = bf16[1664,768]{1,0:T(8,128)(2,1)} async-done(((bf16[416,768]{1,0:T(8,128)(2,1)}), bf16[1664,768]{1,0:T(8,128)(2,1)}) %all-gather.21.cloned.1.call-update) | async-done | bytes 2555920 | tf_op jit(solution)/shard_map/all_gather | solution.py:73
  607.0 9.5 convert_reduce_fusion.1
  621.7 34.4 %reduce-scatter.21.cloned.1.call-done = bf16[416,768]{1,0:T(8,128)(2,1)} async-done(((bf16[1664,768]{1,0:T(8,128)(2,1)}), bf16[416,768]{1,0:T(8,128)(2,1)}) %reduce-scatter.21.cloned.1.call-update) | async-done | bytes 638992 | tf_op jit(solution)/shard_map/reduce_scatter | solution.py:98
  663.2 25.3 %all-gather.23.cloned.1.call-done = bf16[1664,768]{1,0:T(8,128)(2,1)} async-done(((bf16[416,768]{1,0:T(8,128)(2,1)}), bf16[1664,768]{1,0:T(8,128)(2,1)}) %all-gather.23.cloned.1.call-update) | async-done | bytes 2555920 | tf_op jit(solution)/shard_map/all_gather | solution.py:73
  696.3 29.0 %while.55 = (s32[]{:T(128)}, f32[2,832,3,64]{1,3,2,0:T(8,128)}, f32[2,832,3,64]{1,3,2,0:T(8,128)}, bf16[2,832,3,64]{1,3,2,0:T(8,128)(2,1)S(1)}, bf16[2,832,3,64]...) while((s32[]{:T(128)}, f32[2,832,3,64]{1,3,2,0:T(8,128)}, ...), condition=%wide.region_38.39_spmd, body=%wide.region_36.38_spmd.sunk | while | flops 1361229312 | bytes 81833648 | solution.py:282
  727.4 4.6 multiply_add_fusion.2
  749.3 5.0 convolution_bitcast_fusion
  784.7 39.4 %all-reduce.17 = (f32[2,3,192]{2,1,0:T(4,128)S(1)}, f32[2,2,96]{2,1,0:T(2,128)}, f32[2,768]{1,0:T(2,128)}) all-reduce(f32[2,3,192]{2,1,0:T(4,128)S(1)} %pad_maximum_fusion.8, f32[2,2,96]{2,1,0:T(2,128)S(1)} %pad_maximum_fusion.16, f32[2,768]{1,0:T(2,128)S(1)} %pad_maximum_fusion.14), channel_id=1, replica_groups=mesh['dp'=8,'tensor'=4] {'dp'}, use_global_device_ids=true, to_apply=%region_51.52 | all-reduce | flops 3072 | bytes 24576 | tf_op jit(solution)/shard_map/psum | solution.py:334
  828.3 42.4 %all-reduce.16 = (f32[2,768]{1,0:T(2,128)}, f32[2,768]{1,0:T(2,128)}, f32[2,768]{1,0:T(2,128)}, f32[2,768]{1,0:T(2,128)}, f32[2,768]{1,0:T(2,128)}, /*index=5*/f32[2,768]{1,0:T(2,128)}) all-reduce(f32[2,768]{1,0:T(2,128)S(1)} %pad_maximum_fusion.9, ...), channel_id=1, replica_groups=mesh['dp'=8,'tensor'=4] {'dp','tensor'}, use_global_device_ids=true, to_apply=%region_44.45 | all-reduce | flops 9216 | bytes 73728 | tf_op jit(solution)/shard_map/psum | solution.py:335
  873.8 356.6 %all-reduce.21.cloned.1.call-done = (f32[2,3,768,192]{2,3,1,0:T(8,128)}, f32[2,192,768]{2,1,0:T(8,128)}, f32[2,768,768]{2,1,0:T(8,128)}, f32[2,768,768]{2,1,0:T(8,128)}) async-done(((f32[2,3,768,192]{2,3,1,0:T(8,128)}, f32[2,192,768]{2,1,0:T(8,128)}, f32[2,768,768]{2,1,0:T(8,128)}, f32[2,768,768]{2,1,0:T(8,128)}), (f32[2,3,768,192]{2,3,1,0:T(8,128)}, f32[2,192,768]{2,1,0:T(8,128)}, ...) | async-done | bytes 14155792 | tf_op jit(solution)/shard_map/psum | solution.py:334
  1230.4 4.3 copy.229
  (630 shorter events, 296.5 us)
Async XLA Ops:
  7.2 35.7 %all-gather.9.cloned.1.call-start = ((), (), s32[]{:S(2)}) async-start(), calls=%async_computation.8 | async-start | bytes 3194880 | tf_op jit(solution)/shard_map/all_gather | solution.py:69
  14.9 97.1 %reduce-scatter.9.cloned.1.call-start = ((), (), s32[]{:S(2)}) async-start(), calls=%async_computation.9 | async-start | bytes 3194880 | tf_op jit(solution)/shard_map/reduce_scatter | solution.py:82
  77.6 63.9 %all-gather.11.cloned.1.call-start = ((), (), s32[]{:S(2)}) async-start(), calls=%async_computation.10 | async-start | bytes 3194880 | tf_op jit(solution)/shard_map/all_gather | solution.py:69
  78.4 118.2 %copy-start.89 = (f32[768]{0:T(1024)}, f32[768]{0:T(1024)S(1)}, u32[]{:S(2)}) copy-start(f32[768]{0:T(1024)S(1)} %get-tuple-element.381) | copy-start | bytes 9220
  116.2 80.4 %reduce-scatter.11.cloned.1.call-start = ((), (), s32[]{:S(2)}) async-start(), calls=%async_computation.11 | async-start | bytes 3194880 | tf_op jit(solution)/shard_map/reduce_scatter | solution.py:82
  162.2 62.7 %all-gather.13.cloned.1.call-start = ((), (), s32[]{:S(2)}) async-start(), calls=%async_computation.12 | async-start | bytes 3194880 | tf_op jit(solution)/shard_map/all_gather | solution.py:69
  198.1 108.6 %copy-start.3 = (f32[416,768]{1,0:T(8,128)}, f32[416,768]{1,0:T(8,128)S(1)}, u32[]{:S(2)}) copy-start(f32[416,768]{1,0:T(8,128)S(1)} %get-tuple-element.485) | copy-start | bytes 3833860
  199.6 107.1 %reduce-scatter.13.cloned.1.call-start = ((), (), s32[]{:S(2)}) async-start(), calls=%async_computation.13 | async-start | bytes 3194880 | tf_op jit(solution)/shard_map/reduce_scatter | solution.py:82
  272.3 63.2 %all-gather.15.cloned.1.call-start = ((), (), s32[]{:S(2)}) async-start(), calls=%async_computation.14 | async-start | bytes 3194880 | tf_op jit(solution)/shard_map/all_gather | solution.py:69
  310.2 52.2 %all-gather.17.cloned.1.call-start = ((), (), s32[]{:S(2)}) async-start(), calls=%async_computation.16 | async-start | bytes 3194880 | tf_op jit(solution)/shard_map/all_gather | solution.py:73
  311.0 100.6 %reduce-scatter.17.cloned.1.call-start = ((), (), s32[]{:S(2)}) async-start(), calls=%async_computation.17 | async-start | bytes 3194880 | tf_op jit(solution)/shard_map/reduce_scatter | solution.py:98
  377.1 71.7 %reduce-scatter.15.cloned.1.call-start = ((), (), s32[]{:S(2)}) async-start(), calls=%async_computation.15 | async-start | bytes 3194880 | tf_op jit(solution)/shard_map/reduce_scatter | solution.py:82
  383.0 65.8 %copy-start.145 = (f32[768]{0:T(1024)S(1)}, f32[768]{0:T(1024)}, u32[]{:S(2)}) copy-start(f32[768]{0:T(1024)} %get-tuple-element.372) | copy-start | bytes 9220
  383.1 96.7 %all-gather.19.cloned.1.call-start = ((), (), s32[]{:S(2)}) async-start(), calls=%async_computation.18 | async-start | bytes 3194880 | tf_op jit(solution)/shard_map/all_gather | solution.py:73
  454.4 119.1 %reduce-scatter.19.cloned.1.call-start = ((), (), s32[]{:S(2)}) async-start(), calls=%async_computation.19 | async-start | bytes 3194880 | tf_op jit(solution)/shard_map/reduce_scatter | solution.py:98
  539.1 67.8 %all-gather.21.cloned.1.call-start = ((), (), s32[]{:S(2)}) async-start(), calls=%async_computation.20 | async-start | bytes 3194880 | tf_op jit(solution)/shard_map/all_gather | solution.py:73
  581.6 79.4 %copy-start.14 = (f32[416,768]{1,0:T(8,128)}, f32[416,768]{1,0:T(8,128)S(1)}, u32[]{:S(2)}) copy-start(f32[416,768]{1,0:T(8,128)S(1)} %get-tuple-element.473) | copy-start | bytes 3833860
  581.6 74.5 %reduce-scatter.21.cloned.1.call-start = ((), (), s32[]{:S(2)}) async-start(), calls=%async_computation.21 | async-start | bytes 3194880 | tf_op jit(solution)/shard_map/reduce_scatter | solution.py:98
  621.7 66.8 %all-gather.23.cloned.1.call-start = ((), (), s32[]{:S(2)}) async-start(), calls=%async_computation.22 | async-start | bytes 3194880 | tf_op jit(solution)/shard_map/all_gather | solution.py:73
  663.1 161.7 %reduce-scatter.23.cloned.1.call-start = ((), (), s32[]{:S(2)}) async-start(), calls=%async_computation.23 | async-start | bytes 3194880 | tf_op jit(solution)/shard_map/reduce_scatter | solution.py:98
  748.8 481.6 %all-reduce.21.cloned.1.call-start = ((), (), s32[]{:S(2)}) async-start(), calls=%async_computation.24 | async-start | bytes 28311552 | tf_op jit(solution)/shard_map/psum | solution.py:334
  781.9 44.5 %copy-start.127 = (f32[416]{0:T(512)S(1)}, f32[416]{0:T(512)}, u32[]{:S(2)}) copy-start(f32[416]{0:T(512)} %copy-done.126) | copy-start | bytes 4996
  781.9 44.5 %copy-start.119 = (f32[416]{0:T(512)S(1)}, f32[416]{0:T(512)}, u32[]{:S(2)}) copy-start(f32[416]{0:T(512)} %copy-done.118) | copy-start | bytes 4996
  782.4 88.3 %copy-start.11 = (bf16[416,768]{1,0:T(8,128)(2,1)S(1)}, bf16[416,768]{1,0:T(8,128)(2,1)}, u32[]{:S(2)}) copy-start(bf16[416,768]{1,0:T(8,128)(2,1)} %reduce-scatter.9.cloned.1.call-done) | copy-start | bytes 1916932
  782.4 88.3 %copy-start.15 = (f32[416,768]{1,0:T(8,128)S(1)}, f32[416,768]{1,0:T(8,128)}, u32[]{:S(2)}) copy-start(f32[416,768]{1,0:T(8,128)} %copy-done.14) | copy-start | bytes 3833860
  782.4 88.3 %copy-start.18 = (bf16[416,768]{1,0:T(8,128)(2,1)S(1)}, bf16[416,768]{1,0:T(8,128)(2,1)}, u32[]{:S(2)}) copy-start(bf16[416,768]{1,0:T(8,128)(2,1)} %reduce-scatter.21.cloned.1.call-done) | copy-start | bytes 1916932
  782.4 88.3 %copy-start.91 = (f32[768]{0:T(1024)S(1)}, f32[768]{0:T(1024)}, u32[]{:S(2)}) copy-start(f32[768]{0:T(1024)} %copy-done.89) | copy-start | bytes 9220
  782.4 88.3 %copy-start.94 = (f32[768]{0:T(1024)S(1)}, f32[768]{0:T(1024)}, u32[]{:S(2)}) copy-start(f32[768]{0:T(1024)} %copy-done.92) | copy-start | bytes 9220
  782.4 88.3 %copy-start.101 = (f32[416]{0:T(512)S(1)}, f32[416]{0:T(512)}, u32[]{:S(2)}) copy-start(f32[416]{0:T(512)} %copy-done.99) | copy-start | bytes 4996
  782.5 88.3 %copy-start.109 = (f32[416]{0:T(512)S(1)}, f32[416]{0:T(512)}, u32[]{:S(2)}) copy-start(f32[416]{0:T(512)} %copy-done.107) | copy-start | bytes 4996
  782.5 88.3 %copy-start.121 = (f32[416]{0:T(512)S(1)}, f32[416]{0:T(512)}, u32[]{:S(2)}) copy-start(f32[416]{0:T(512)} %copy-done.120) | copy-start | bytes 4996
  782.5 88.3 %copy-start.125 = (f32[416]{0:T(512)S(1)}, f32[416]{0:T(512)}, u32[]{:S(2)}) copy-start(f32[416]{0:T(512)} %copy-done.124) | copy-start | bytes 4996
  (162 other events, 1920.6 us)
Sparse Core Ops, SparseCore 0:
  15.0 27.8 all-gather.8
  77.7 34.2 reduce-scatter.8
  116.3 25.1 all-gather.10
  162.3 34.2 reduce-scatter.10
  199.7 25.1 all-gather.12
  272.4 34.2 reduce-scatter.12
  310.3 25.1 all-gather.14
  337.2 25.1 all-gather.16
  377.3 34.2 reduce-scatter.16
  414.6 34.2 reduce-scatter.14
  454.5 25.1 all-gather.18
  539.2 34.2 reduce-scatter.18
  581.7 25.1 all-gather.20
  621.8 34.2 reduce-scatter.20
  663.2 25.1 all-gather.22
  748.9 34.2 reduce-scatter.22
  788.9 441.4 all-reduce.20
where the time goes:
time: 1250 us
  waiting for transfers between devices  774 us (62%)
  matrix products  173 us (14%)
  other arithmetic  104 us (8%)
  local copies, waits for them, and re-layouts  96.6 us (8%)
  blocking collectives  81.8 us (7%)
  between operations  16.3 us (1%)
    psum x1, waiting for transfers between devices, body(): sharded_stacked = lax.psum(sharded_stacked, 'dp')  357 us
    reduce_scatter x4, waiting for transfers between devices, collect(): lax.psum_scatter(partial_term(jnp.int32(0), share_rows * lax.axis_size('t...  135 us
    all_gather x4, waiting for transfers between devices, spread(): return lax.all_gather(row_share, 'tensor', axis=0, tiled=True)  98.9 us
    reduce_scatter x4, waiting for transfers between devices, collect_back(): lax.psum_scatter(partial_term(jnp.int32(0), share_rows * lax.axis_size('t...  97.2 us
    all_gather x4, waiting for transfers between devices, spread_back(): return lax.all_gather(row_share, 'tensor', axis=0, tiled=True)  85 us
    psum x1, blocking collectives, body(): shared_stacked = lax.psum(shared_stacked, ('dp', 'tensor'))  42.4 us
    psum x1, blocking collectives, body(): sharded_stacked = lax.psum(sharded_stacked, 'dp')  39.4 us
    unnamed x334, local copies, waits for them, and re-layouts  33.4 us
  transfers between devices with their start and end apart: 17, of which 16 were waited for; matrix products, arithmetic and copies ran while one was open for 5% of the time, Pallas kernels for 0%

commit v1 on v0

v1 whole, which is shorter than its diff:
```python
from functools import partial

import jax
import jax.numpy as jnp
from jax import lax
from jax.sharding import PartitionSpec as P

HEAD_DIM = 64
LEN = 832
SIDE_S = 14
SIDE_M = 20
SIDE_L = 24
MAX_IMAGES = 4
LAYERS = 2

EPS = 1e-06
NEGATIVE = -1000000000.0
BF = jnp.bfloat16
F32 = jnp.float32

CORE = [(0, 1), (1, 0), (2, 3), (3, 2)]
ACROSS = [(0, 2), (2, 0), (1, 3), (3, 1)]


def over_core(values):
    return lax.ppermute(values, "tensor", CORE)


def over_y(values):
    return lax.ppermute(values, "tensor", ACROSS)


def over_bit(values, bit):
    size = lax.axis_size("dp")
    return lax.ppermute(values, "dp", [(at, at ^ (1 << bit)) for at in range(size)])


def quarters(own):
    first = over_core(own)
    second = over_y(own)
    third = over_core(second)
    return (own, first, second, third)


def places_at(lengths, position):
    ends = jnp.cumsum(lengths)
    starts = ends - lengths
    segment = jnp.sum((position[:, None] >= ends[None, :]).astype(jnp.int32), axis=1)
    belongs = segment[:, None] == jnp.arange(MAX_IMAGES, dtype=jnp.int32)[None, :]
    begin_at = jnp.sum(jnp.where(belongs, starts[None, :], 0), axis=1)
    size = jnp.sum(jnp.where(belongs, lengths[None, :], 0), axis=1)
    side = jnp.where(
        size == SIDE_S * SIDE_S, SIDE_S, jnp.where(size == SIDE_M * SIDE_M, SIDE_M, SIDE_L)
    ).astype(jnp.int32)
    offset = position - begin_at
    inside = segment < MAX_IMAGES
    row_at = jnp.where(inside, offset // side, 0)
    column_at = jnp.where(inside, offset % side, 0)
    return segment, row_at, column_at


def norm_parts(values):
    average = jnp.mean(values, axis=-1, keepdims=True)
    centred = values - average
    variance = jnp.mean(centred * centred, axis=-1, keepdims=True)
    inverse = lax.rsqrt(variance + EPS)
    return centred * inverse, inverse


def norm_grads(values, gain, incoming):
    xhat, inverse = norm_parts(values)
    grad_gain = jnp.sum(incoming * xhat, axis=0)
    grad_shift = jnp.sum(incoming, axis=0)
    scaled = incoming * gain
    through = inverse * (
        scaled
        - jnp.mean(scaled, axis=-1, keepdims=True)
        - xhat * jnp.mean(scaled * xhat, axis=-1, keepdims=True)
    )
    return through, grad_gain, grad_shift


def mm(left, right):
    return lax.dot_general(left, right, (((1,), (0,)), ((), ())), preferred_element_type=F32)


def mm_nt(left, right):
    return lax.dot_general(left, right, (((1,), (1,)), ((), ())), preferred_element_type=F32)


def mm_tn(left, right):
    return lax.dot_general(left, right, (((0,), (0,)), ((), ())), preferred_element_type=F32)


def turn(values, cosine, sine):
    half = HEAD_DIM // 2
    first, second = values[..., :half], values[..., half:]
    return jnp.concatenate(
        [first * cosine - second * sine, first * sine + second * cosine], axis=-1
    )


def masked_scores(query, key, allowed):
    scores = jnp.einsum("qhe,khe->hqk", query, key, preferred_element_type=F32) * (HEAD_DIM**-0.5)
    return jnp.where(allowed[None], scores, NEGATIVE)


def attend(query, key, value, allowed):
    scores = masked_scores(query, key, allowed)
    highest = jnp.max(scores, axis=-1, keepdims=True)
    exp_scores = jnp.exp(scores - highest)
    totals = jnp.sum(exp_scores, axis=-1, keepdims=True)
    probs = (exp_scores / totals).astype(BF)
    mixed = jnp.einsum("hqk,khe->qhe", probs, value, preferred_element_type=F32).astype(BF)
    return mixed, highest + jnp.log(totals)


def attend_back(query, key, value, allowed, log_totals, grad_mixed):
    scaling = HEAD_DIM**-0.5
    scores = masked_scores(query, key, allowed)
    probs = jnp.exp(scores - log_totals)
    low = probs.astype(BF)
    grad_value = jnp.einsum("hqk,qhe->khe", low, grad_mixed, preferred_element_type=F32)
    grad_probs = jnp.einsum("qhe,khe->hqk", grad_mixed, value, preferred_element_type=F32)
    grad_scores = (
        probs * (grad_probs - jnp.sum(probs * grad_probs, axis=-1, keepdims=True))
    ).astype(BF)
    grad_query = jnp.einsum("hqk,khe->qhe", grad_scores, key, preferred_element_type=F32) * scaling
    grad_key = jnp.einsum("hqk,qhe->khe", grad_scores, query, preferred_element_type=F32) * scaling
    return grad_query, grad_key, grad_value


def reduce_weight(parts):
    second = (parts[2] + over_core(parts[3].astype(BF)).astype(F32)).astype(BF)
    total = (
        parts[0] + over_core(parts[1].astype(BF)).astype(F32) + over_y(second).astype(F32)
    )
    me = lax.axis_index("dp")
    bits = lax.axis_size("dp").bit_length() - 1
    for bit in range(bits):
        half = total.shape[0] // 2
        mine = (me >> bit) & 1
        keep = lax.dynamic_slice_in_dim(total, mine * half, half, 0)
        send = lax.dynamic_slice_in_dim(total, (1 - mine) * half, half, 0)
        total = keep + over_bit(send.astype(BF), bit).astype(F32)
    total = total.astype(BF)
    for bit in reversed(range(bits)):
        other = over_bit(total, bit)
        mine = ((me >> bit) & 1) == 0
        total = jnp.concatenate(
            [jnp.where(mine, total, other), jnp.where(mine, other, total)], axis=0
        )
    return total.astype(F32)


def reduce_small(shared, split):
    rows = shared.shape[0]
    body = jnp.concatenate([shared] + list(split), axis=0)
    width = split[0].shape[0]
    other = over_core(body)
    mine = [split[at] + other[rows + (at ^ 1) * width : rows + ((at ^ 1) + 1) * width] for at in (0, 2)]
    both = shared + other[:rows]
    body = jnp.concatenate([both] + mine, axis=0)
    other = over_y(body)
    total = jnp.concatenate([both + other[:rows], mine[0] + other[rows + width :]], axis=0)
    for bit in range(lax.axis_size("dp").bit_length() - 1):
        total = total + over_bit(total, bit)
    return total[:rows], total[rows:]


def body(
    tokens,
    out_grad,
    image_lengths,
    norm1_gain,
    norm1_bias,
    qkv_weight,
    qkv_bias,
    rope_freqs,
    out_weight,
    out_bias,
    norm2_gain,
    norm2_bias,
    up_weight,
    up_bias,
    down_weight,
    down_bias,
):
    count, width = tokens.shape
    inner = qkv_weight.shape[3]
    heads = inner // HEAD_DIM
    hidden = up_weight.shape[2]
    me = lax.axis_index("tensor")
    lengths = lax.dynamic_index_in_dim(image_lengths, me // 2, 0, keepdims=False)
    half_at = me % 2
    position = jnp.arange(count, dtype=jnp.int32)
    segment, row_at, column_at = places_at(lengths, position + half_at * count)
    segment_other, _, _ = places_at(lengths, position + (1 - half_at) * count)
    allowed = segment[:, None] == jnp.concatenate([segment, segment_other])[None, :]
    row_at = row_at.astype(F32)
    column_at = column_at.astype(F32)

    small = jnp.concatenate(
        [qkv_bias.reshape(LAYERS, -1), rope_freqs.reshape(LAYERS, -1), up_bias], axis=1
    )
    small = quarters(small)
    weights = []
    for l in range(LAYERS):
        weights.append(
            (
                quarters(qkv_weight[l].reshape(-1, inner)),
                quarters(out_weight[l]),
                quarters(up_weight[l]),
                quarters(down_weight[l]),
            )
        )

    current = tokens.astype(F32)
    kept = []
    for l in range(LAYERS):
        qkv, out, up, down = weights[l]
        inputs = current
        xhat, _ = norm_parts(inputs)
        normed = (xhat * norm1_gain[l] + norm1_bias[l]).astype(BF)
        turned_q, turned_k, values, trig = [], [], [], []
        keys_all, values_all = [None] * 4, [None] * 4
        for j in range(4):
            bias = small[j][l, : 3 * inner].reshape(3, inner)
            freqs = small[j][l, 3 * inner : 3 * inner + 2 * inner // 2].reshape(2, heads, -1)
            angles = row_at[:, None, None] * freqs[0] + column_at[:, None, None] * freqs[1]
            cosine, sine = jnp.cos(angles), jnp.sin(angles)
            trig.append((cosine, sine))
            stack = qkv[j].reshape(3, width, inner)
            query, key, value = [(mm(normed, stack[i]) + bias[i]) for i in range(3)]
            turned_q.append(turn(query.reshape(count, heads, -1), cosine, sine).astype(BF))
            turned_k.append(turn(key.reshape(count, heads, -1), cosine, sine).astype(BF))
            values.append(value.astype(BF).reshape(count, heads, -1))
            if j % 2:
                sent = jnp.stack([turned_k[j - 1], values[j - 1], turned_k[j], values[j]])
                came = over_core(sent)
                for at, where in ((j - 1, 2), (j, 0)):
                    keys_all[at] = jnp.concatenate([turned_k[at], came[where]], axis=0)
                    values_all[at] = jnp.concatenate([values[at], came[where + 1]], axis=0)
        mixed, log_totals = [], []
        total = inputs + out_bias[l]
        for j in range(4):
            mixed_j, log_j = attend(turned_q[j], keys_all[j], values_all[j], allowed)
            mixed.append(mixed_j.reshape(count, inner))
            log_totals.append(log_j)
            total = total + mm(mixed[j], out[j])
        middle = total
        xhat, _ = norm_parts(middle)
        normed_mlp = (xhat * norm2_gain[l] + norm2_bias[l]).astype(BF)
        active, slope = [], []
        total = middle + down_bias[l]
        for j in range(4):
            pre = mm(normed_mlp, up[j]) + small[j][l, 4 * inner :]
            normal = 0.5 * (1.0 + lax.erf(pre * (0.5**0.5)))
            active.append((pre * normal).astype(BF))
            slope.append((normal + pre * jnp.exp(-0.5 * pre * pre) * 0.3989422804014327).astype(BF))
            total = total + mm(active[j], down[j])
        current = total
        kept.append(
            (inputs, normed, turned_q, keys_all, values_all, trig, mixed, log_totals, middle, normed_mlp, active, slope)
        )
    activations = current.astype(BF)

    gradient = out_grad.astype(F32)
    big = [None] * LAYERS
    shared_rows, split_rows = [], [[], [], [], []]
    for l in reversed(range(LAYERS)):
        qkv, out, up, down = weights[l]
        (inputs, normed, turned_q, keys_all, values_all, trig, mixed, log_totals, middle, normed_mlp, active, slope) = kept[l]
        low = gradient.astype(BF)
        grad_down_bias = jnp.sum(low.astype(F32), axis=0)
        grad_down, grad_up, grad_up_bias = [None] * 4, [None] * 4, [None] * 4
        total = None
        for j in (3, 2, 1, 0):
            grad_pre = (mm_nt(low, down[j]) * slope[j].astype(F32)).astype(BF)
            grad_down[j] = mm_tn(active[j], low)
            grad_up[j] = mm_tn(normed_mlp, grad_pre)
            grad_up_bias[j] = jnp.sum(grad_pre.astype(F32), axis=0)
            term = mm_nt(grad_pre, up[j])
            total = term if total is None else total + term
        grad_down = reduce_weight(grad_down)
        grad_up = reduce_weight(grad_up)
        through, grad_gain2, grad_shift2 = norm_grads(middle, norm2_gain[l], total)
        grad_middle = gradient + through
        low = grad_middle.astype(BF)
        grad_out_bias = jnp.sum(low.astype(F32), axis=0)
        grad_out, grad_qkv = [None] * 4, [None] * 4
        grad_qkv_bias, grad_freqs = [None] * 4, [None] * 4
        parts = [None] * 4
        total = None
        for pair in ((3, 2), (1, 0)):
            sent = []
            for j in pair:
                grad_out[j] = mm_tn(mixed[j], low)
                grad_mixed = mm_nt(low, out[j]).astype(BF).reshape(count, heads, -1)
                grad_q, grad_k, grad_v = attend_back(
                    turned_q[j], keys_all[j], values_all[j], allowed, log_totals[j], grad_mixed
                )
                parts[j] = (grad_q, grad_k[:count], grad_v[:count])
                sent += [grad_k[count:].astype(BF), grad_v[count:].astype(BF)]
            came = over_core(jnp.stack(sent))
            for at, j in enumerate(pair):
                grad_q, grad_k, grad_v = parts[j]
                grad_k = grad_k + came[2 * (1 - at)].astype(F32)
                grad_v = grad_v + came[2 * (1 - at) + 1].astype(F32)
                cosine, sine = trig[j]
                half = HEAD_DIM // 2
                angle = 0.0
                turned_back = []
                for grad, turned in ((grad_q, turned_q[j]), (grad_k, keys_all[j][:count])):
                    turned_back.append(turn(grad, cosine, -sine))
                    angle = angle + (
                        grad[..., half:] * turned[..., :half].astype(F32)
                        - grad[..., :half] * turned[..., half:].astype(F32)
                    )
                grad_freqs[j] = jnp.concatenate(
                    [
                        jnp.sum(row_at[:, None, None] * angle, axis=0).reshape(-1),
                        jnp.sum(column_at[:, None, None] * angle, axis=0).reshape(-1),
                    ]
                )
                grads = [
                    item.astype(BF).reshape(count, inner)
                    for item in (turned_back[0], turned_back[1], grad_v)
                ]
                stack = qkv[j].reshape(3, width, inner)
                grad_qkv[j] = jnp.concatenate([mm_tn(normed, item) for item in grads], axis=0)
                grad_qkv_bias[j] = jnp.concatenate([jnp.sum(item.astype(F32), axis=0) for item in grads])
                for i in range(3):
                    term = mm_nt(grads[i], stack[i])
                    total = term if total is None else total + term
        grad_out = reduce_weight(grad_out)
        grad_qkv = reduce_weight(grad_qkv)
        through, grad_gain1, grad_shift1 = norm_grads(inputs, norm1_gain[l], total)
        gradient = grad_middle + through
        big[l] = (grad_qkv.reshape(3, width, inner), grad_out, grad_up, grad_down)
        shared_rows = [grad_gain1, grad_shift1, grad_out_bias, grad_gain2, grad_shift2, grad_down_bias] + shared_rows
        for j in range(4):
            split_rows[j] = [jnp.concatenate([grad_qkv_bias[j], grad_freqs[j], grad_up_bias[j]]).reshape(-1, width)] + split_rows[j]

    shared, split = reduce_small(
        jnp.stack(shared_rows), [jnp.concatenate(rows, axis=0) for rows in split_rows]
    )
    shared = shared.reshape(LAYERS, 6, width)
    split = split.reshape(LAYERS, -1)
    stacked = [jnp.stack([big[l][item] for l in range(LAYERS)]) for item in range(4)]
    return (
        activations,
        gradient,
        shared[:, 0],
        shared[:, 1],
        stacked[0],
        split[:, : 3 * inner].reshape(LAYERS, 3, inner),
        split[:, 3 * inner : 4 * inner].reshape(LAYERS, 2, inner // 2),
        stacked[1],
        shared[:, 2],
        shared[:, 3],
        shared[:, 4],
        stacked[2],
        split[:, 4 * inner :],
        stacked[3],
        shared[:, 5],
    )


def solution(mesh):
    in_specs = (
        P(("dp", "tensor"), None),
        P(("dp", "tensor"), None),
        P("dp", None),
        P(),
        P(),
        P(None, None, None, "tensor"),
        P(None, None, "tensor"),
        P(None, None, "tensor"),
        P(None, "tensor", None),
        P(),
        P(),
        P(),
        P(None, None, "tensor"),
        P(None, "tensor"),
        P(None, "tensor", None),
        P(),
    )
    out_specs = (
        P(("dp", "tensor"), None),
        P(("dp", "tensor"), None),
        P(),
        P(),
        P(None, None, None, "tensor"),
        P(None, None, "tensor"),
        P(None, None, "tensor"),
        P(None, "tensor", None),
        P(),
        P(),
        P(),
        P(None, None, "tensor"),
        P(None, "tensor"),
        P(None, "tensor", None),
        P(),
    )
    return jax.shard_map(body, mesh=mesh, in_specs=in_specs, out_specs=out_specs, check_vma=False)
```

time: 1250 us -> 816 us (0.65)
  waiting for transfers between devices: 774 us -> 279 us
  starting transfers between devices: 1.92 us -> 91.8 us
  blocking collectives: 81.8 us -> 0 us
  matrix products: 173 us -> 197 us
  local copies, waits for them, and re-layouts: 96.6 us -> 118 us
    psum x1 -> x0, waiting for transfers between devices: 357 us -> none  [body(): sharded_stacked = lax.psum(sharded_stacked, 'dp')]
    ppermute x0 -> x112, waiting for transfers between devices: none -> 279 us  [the longest x18 153 us: over_y(): return lax.ppermute(values, 'tensor', ACROSS)]
    reduce_scatter x8 -> x0, waiting for transfers between devices: 233 us -> none  [the longest x4 135 us: collect(): lax.psum_scatter(partial_term(jnp.int32(0), share_rows * lax.axis_size('t...]
    all_gather x8 -> x0, waiting for transfers between devices: 184 us -> none  [the longest x4 98.9 us: spread(): return lax.all_gather(row_share, 'tensor', axis=0, tiled=True)]
    ppermute x0 -> x112, starting transfers between devices: none -> 91.8 us  [the longest x51 61.3 us: over_bit(): lax.ppermute(values, 'dp', [(at, at ^ 1 << bit) for at in range(size)])]
    psum x2 -> x0, blocking collectives: 81.8 us -> none  [the longest x1 42.4 us: body(): shared_stacked = lax.psum(shared_stacked, ('dp', 'tensor'))]
    dot_general x50 -> x192, matrix products: 165 us -> 197 us  [the longest x48 60.4 us: mm_tn(): lax.dot_general(left, right, (((0,), (0,)), ((), ())), preferred_element_...]
    reduce_sum x0 -> x24, local copies, waits for them, and re-layouts: none -> 24.8 us  [body(): jnp.sum(item.astype(F32), axis=0)]
  transfers between devices with their start and end apart: 17 -> 112, of which waited for: 16 -> 43; matrix products, arithmetic and copies ran while one was open for 5% -> 45% of each run, Pallas kernels for 0% -> 0%
where the time goes in v1:
time: 816 us; the launch traced here: 804 us
  waiting for transfers between devices  279 us (34%)
  matrix products  197 us (24%)
  local copies, waits for them, and re-layouts  118 us (14%)
  other arithmetic  111 us (14%)
  starting transfers between devices  91.8 us (11%)
    ppermute x18, waiting for transfers between devices, over_y(): return lax.ppermute(values, 'tensor', ACROSS)  153 us
    ppermute x51, waiting for transfers between devices, over_bit(): lax.ppermute(values, 'dp', [(at, at ^ 1 << bit) for at in range(size)])  123 us
    ppermute x51, starting transfers between devices, over_bit(): lax.ppermute(values, 'dp', [(at, at ^ 1 << bit) for at in range(size)])  61.3 us
    dot_general x48, matrix products, mm_tn(): lax.dot_general(left, right, (((0,), (0,)), ((), ())), preferred_element_...  60.4 us
    dot_general x48, matrix products, mm_nt(): lax.dot_general(left, right, (((1,), (1,)), ((), ())), preferred_element_...  42.4 us
    dot_general x48, matrix products, mm(): lax.dot_general(left, right, (((1,), (0,)), ((), ())), preferred_element_...  39.4 us
    unnamed x819, local copies, waits for them, and re-layouts  26.7 us
    reduce_sum x24, local copies, waits for them, and re-layouts, body(): jnp.sum(item.astype(F32), axis=0)  24.8 us
  transfers between devices with their start and end apart: 112, of which 43 were waited for; matrix products, arithmetic and copies ran while one was open for 45% of the time, Pallas kernels for 0%

profile of v1, /device:TPU:0, one launch (start us, length us, event | category | flops | bytes accessed | tf_op | source)
XLA Modules:
  0.0 804.0 jit_solution(1127587419755589929)
XLA Ops:
  5.0 3.0 collective-permute-start.4
  20.2 3.3 slice_bitcast_fusion.1
  98.9 15.2 %collective-permute-done.13 = bf16[768,768]{1,0:T(8,128)(2,1)S(1)} collective-permute-done((bf16[768,768]{1,0:T(8,128)(2,1)S(1)}, bf16[768,768]{1,0:T(8,128)(2,1)S(1)}, u32[]{:S(2)}, u32[]{:S(2)}) %collective-permute-start.13) | collective-permute-done | bytes 1179680 | tf_op jit(solution)/shard_map/ppermute | solution.py:30
  166.1 23.2 %collective-permute-done.27 = bf16[768,768]{1,0:T(8,128)(2,1)S(1)} collective-permute-done((bf16[768,768]{1,0:T(8,128)(2,1)S(1)}, bf16[768,768]{1,0:T(8,128)(2,1)S(1)}, u32[]{:S(2)}, u32[]{:S(2)}) %collective-permute-start.27) | collective-permute-done | bytes 1179680 | tf_op jit(solution)/shard_map/ppermute | solution.py:30
  257.5 6.1 collective-permute-done.69
  396.1 4.1 collective-permute-done.75
  401.6 3.1 add_convert_fusion.2
  406.5 3.2 add_convert_fusion
  409.8 4.2 collective-permute-done.60
  488.2 3.1 collective-permute-start.63
  520.7 21.5 %collective-permute-done.87 = bf16[768,768]{1,0:T(8,128)(2,1)S(1)} collective-permute-done((bf16[768,768]{1,0:T(8,128)(2,1)S(1)}, bf16[768,768]{1,0:T(8,128)(2,1)S(1)}, u32[]{:S(2)}, u32[]{:S(2)}) %collective-permute-start.87) | collective-permute-done | bytes 1179680 | tf_op jit(solution)/shard_map/ppermute | solution.py:30
  544.8 16.4 %collective-permute-done.51 = bf16[2304,192]{0,1:T(8,128)(2,1)S(1)} collective-permute-done((bf16[2304,192]{0,1:T(8,128)(2,1)S(1)}, bf16[2304,192]{0,1:T(8,128)(2,1)S(1)}, u32[]{:S(2)}, u32[]{:S(2)}) %collective-permute-start.51) | collective-permute-done | bytes 884768 | tf_op jit(solution)/shard_map/ppermute | solution.py:30
  562.8 23.6 %collective-permute-done.105 = bf16[768,768]{1,0:T(8,128)(2,1)S(1)} collective-permute-done((bf16[768,768]{1,0:T(8,128)(2,1)S(1)}, bf16[768,768]{1,0:T(8,128)(2,1)S(1)}, u32[]{:S(2)}, u32[]{:S(2)}) %collective-permute-start.105) | collective-permute-done | bytes 1179680 | tf_op jit(solution)/shard_map/ppermute | solution.py:30
  588.7 9.1 %collective-permute-done.52 = bf16[1152,192]{0,1:T(8,128)(2,1)S(1)} collective-permute-done((bf16[1152,192]{0,1:T(8,128)(2,1)S(1)}, bf16[1152,192]{0,1:T(8,128)(2,1)S(1)}, u32[]{:S(2)}, u32[]{:S(2)}) %collective-permute-start.52) | collective-permute-done | bytes 442400 | tf_op jit(solution)/shard_map/ppermute | solution.py:35
  599.6 11.9 %collective-permute-done.106 = bf16[384,768]{1,0:T(8,128)(2,1)S(1)} collective-permute-done((bf16[384,768]{1,0:T(8,128)(2,1)S(1)}, bf16[384,768]{1,0:T(8,128)(2,1)S(1)}, u32[]{:S(2)}, u32[]{:S(2)}) %collective-permute-start.106) | collective-permute-done | bytes 589856 | tf_op jit(solution)/shard_map/ppermute | solution.py:35
  614.9 22.1 %collective-permute-done.96 = bf16[768,768]{1,0:T(8,128)(2,1)S(1)} collective-permute-done((bf16[768,768]{1,0:T(8,128)(2,1)S(1)}, bf16[768,768]{1,0:T(8,128)(2,1)S(1)}, u32[]{:S(2)}, u32[]{:S(2)}) %collective-permute-start.96) | collective-permute-done | bytes 1179680 | tf_op jit(solution)/shard_map/ppermute | solution.py:30
  639.5 16.0 %collective-permute-done.42 = bf16[2304,192]{0,1:T(8,128)(2,1)S(1)} collective-permute-done((bf16[2304,192]{0,1:T(8,128)(2,1)S(1)}, bf16[2304,192]{0,1:T(8,128)(2,1)S(1)}, u32[]{:S(2)}, u32[]{:S(2)}) %collective-permute-start.42) | collective-permute-done | bytes 884768 | tf_op jit(solution)/shard_map/ppermute | solution.py:30
  658.9 7.2 collective-permute-done.54
  667.8 3.0 collective-permute-start.90
  671.1 8.5 %collective-permute-done.55 = bf16[288,192]{0,1:T(8,128)(2,1)S(1)} collective-permute-done((bf16[288,192]{0,1:T(8,128)(2,1)S(1)}, bf16[288,192]{0,1:T(8,128)(2,1)S(1)}, u32[]{:S(2)}, u32[]{:S(2)}) %collective-permute-start.55) | collective-permute-done | bytes 110624 | tf_op jit(solution)/shard_map/ppermute | solution.py:35
  679.8 2.9 collective-permute-done.90
  691.1 4.0 collective-permute-done.56
  695.4 3.1 collective-permute-done.91
  698.5 3.5 collective-permute-start.57
  707.4 16.7 %collective-permute-done.45 = bf16[288,192]{0,1:T(8,128)(2,1)S(1)} collective-permute-done((bf16[288,192]{0,1:T(8,128)(2,1)S(1)}, bf16[288,192]{0,1:T(8,128)(2,1)S(1)}, u32[]{:S(2)}, u32[]{:S(2)}) %collective-permute-start.45) | collective-permute-done | bytes 110624 | tf_op jit(solution)/shard_map/ppermute | solution.py:35
  732.8 4.5 collective-permute-done.98
  738.1 2.9 collective-permute-start.99
  742.7 6.6 collective-permute-done.81
  750.4 6.7 collective-permute-done.99
  761.8 3.1 collective-permute-done.100
  784.5 4.9 collective-permute-done.84
  793.3 6.7 collective-permute-done.102
  (1575 shorter events, 523.3 us)
Async XLA Ops:
  5.0 60.9 %collective-permute-start.4 = (bf16[2304,192]{0,1:T(8,128)(2,1)}, bf16[2304,192]{0,1:T(8,128)(2,1)}, u32[]{:S(2)}, u32[]{:S(2)}) collective-permute-start(bf16[2304,192]{0,1:T(8,128)(2,1)} %bitcast.255), channel_id=1, source_target_pairs={{0,2},{2,0},{1,3},{3,1},{4,6},{6,4},{5,7},{7,5},{8,10},{10,8},{9,1... | collective-permute-start | bytes 2654216 | tf_op jit(solution)/shard_map/ppermute | solution.py:30
  7.9 52.6 %collective-permute-start = (bf16[2304,192]{0,1:T(8,128)(2,1)}, bf16[2304,192]{0,1:T(8,128)(2,1)}, u32[]{:S(2)}, u32[]{:S(2)}) collective-permute-start(bf16[2304,192]{0,1:T(8,128)(2,1)} %bitcast.255), channel_id=1, source_target_pairs={{0,1},{1,0},{2,3},{3,2},{4,5},{5,4},{6,7},{7,6},{8,9},{9,8},{10,11... | collective-permute-start | bytes 2654216 | tf_op jit(solution)/shard_map/ppermute | solution.py:26
  10.2 84.7 %collective-permute-start.9 = (bf16[192,768]{1,0:T(8,128)(2,1)}, bf16[192,768]{1,0:T(8,128)(2,1)}, u32[]{:S(2)}, u32[]{:S(2)}) collective-permute-start(bf16[192,768]{1,0:T(8,128)(2,1)} %get-tuple-element.254), channel_id=1, source_target_pairs={{0,2},{2,0},{1,3},{3,1},{4,6},{6,4},{5,7},{7,5},{8,10},{10,8},{9,1... | collective-permute-start | bytes 884744 | tf_op jit(solution)/shard_map/ppermute | solution.py:30
  32.0 64.5 %collective-permute-start.3 = (bf16[192,768]{1,0:T(8,128)(2,1)}, bf16[192,768]{1,0:T(8,128)(2,1)S(1)}, u32[]{:S(2)}, u32[]{:S(2)}) collective-permute-start(bf16[192,768]{1,0:T(8,128)(2,1)} %get-tuple-element.254), channel_id=1, source_target_pairs={{0,1},{1,0},{2,3},{3,2},{4,5},{5,4},{6,7},{7,6},{8,9},{9,8},{10,11... | collective-permute-start | bytes 884744 | tf_op jit(solution)/shard_map/ppermute | solution.py:26
  51.4 68.6 %collective-permute-start.14 = (bf16[768,768]{1,0:T(8,128)(2,1)}, bf16[768,768]{1,0:T(8,128)(2,1)}, u32[]{:S(2)}, u32[]{:S(2)}) collective-permute-start(bf16[768,768]{1,0:T(8,128)(2,1)} %get-tuple-element.193), channel_id=1, source_target_pairs={{0,2},{2,0},{1,3},{3,1},{4,6},{6,4},{5,7},{7,5},{8,10},{10,8},{9,1... | collective-permute-start | bytes 3538952 | tf_op jit(solution)/shard_map/ppermute | solution.py:30
  60.5 68.6 %collective-permute-start.12 = (bf16[768,768]{1,0:T(8,128)(2,1)}, bf16[768,768]{1,0:T(8,128)(2,1)S(1)}, u32[]{:S(2)}, u32[]{:S(2)}) collective-permute-start(bf16[768,768]{1,0:T(8,128)(2,1)} %get-tuple-element.193), channel_id=1, source_target_pairs={{0,1},{1,0},{2,3},{3,2},{4,5},{5,4},{6,7},{7,6},{8,9},{9,8},{10,11... | collective-permute-start | bytes 3538952 | tf_op jit(solution)/shard_map/ppermute | solution.py:26
  125.6 39.5 %collective-permute-start.23 = (bf16[192,768]{1,0:T(8,128)(2,1)S(1)}, bf16[192,768]{1,0:T(8,128)(2,1)S(1)}, u32[]{:S(2)}, u32[]{:S(2)}) collective-permute-start(bf16[192,768]{1,0:T(8,128)(2,1)S(1)} %copy-done.302), channel_id=1, source_target_pairs={{0,2},{2,0},{1,3},{3,1},{4,6},{6,4},{5,7},{7,5},{8,10},{10,8},{9,1... | collective-permute-start | bytes 884744 | tf_op jit(solution)/shard_map/ppermute | solution.py:30
  129.1 36.5 %collective-permute-start.19 = (bf16[192,768]{1,0:T(8,128)(2,1)S(1)}, bf16[192,768]{1,0:T(8,128)(2,1)S(1)}, u32[]{:S(2)}, u32[]{:S(2)}) collective-permute-start(bf16[192,768]{1,0:T(8,128)(2,1)S(1)} %copy-done.302), channel_id=1, source_target_pairs={{0,1},{1,0},{2,3},{3,2},{4,5},{5,4},{6,7},{7,6},{8,9},{9,8},{10,11... | collective-permute-start | bytes 884744 | tf_op jit(solution)/shard_map/ppermute | solution.py:26
  133.0 56.3 %collective-permute-start.28 = (bf16[768,768]{1,0:T(8,128)(2,1)S(1)}, bf16[768,768]{1,0:T(8,128)(2,1)S(1)}, u32[]{:S(2)}, u32[]{:S(2)}) collective-permute-start(bf16[768,768]{1,0:T(8,128)(2,1)S(1)} %copy-done.167), channel_id=1, source_target_pairs={{0,2},{2,0},{1,3},{3,1},{4,6},{6,4},{5,7},{7,5},{8,10},{10,8},{9,1... | collective-permute-start | bytes 3538952 | tf_op jit(solution)/shard_map/ppermute | solution.py:30
  137.2 59.5 %collective-permute-start.26 = (bf16[768,768]{1,0:T(8,128)(2,1)S(1)}, bf16[768,768]{1,0:T(8,128)(2,1)S(1)}, u32[]{:S(2)}, u32[]{:S(2)}) collective-permute-start(bf16[768,768]{1,0:T(8,128)(2,1)S(1)} %copy-done.167), channel_id=1, source_target_pairs={{0,1},{1,0},{2,3},{3,2},{4,5},{5,4},{6,7},{7,6},{8,9},{9,8},{10,11... | collective-permute-start | bytes 3538952 | tf_op jit(solution)/shard_map/ppermute | solution.py:26
  151.1 38.2 %collective-permute-start.27 = (bf16[768,768]{1,0:T(8,128)(2,1)S(1)}, bf16[768,768]{1,0:T(8,128)(2,1)S(1)}, u32[]{:S(2)}, u32[]{:S(2)}) collective-permute-start(bf16[768,768]{1,0:T(8,128)(2,1)S(1)} %copy-done.168), channel_id=1, source_target_pairs={{0,2},{2,0},{1,3},{3,1},{4,6},{6,4},{5,7},{7,5},{8,10},{10,8},{9,1... | collective-permute-start | bytes 3538952 | tf_op jit(solution)/shard_map/ppermute | solution.py:30
  256.5 144.5 %collective-permute-start.86 = (bf16[768,768]{1,0:T(8,128)(2,1)}, bf16[768,768]{1,0:T(8,128)(2,1)}, u32[]{:S(2)}, u32[]{:S(2)}) collective-permute-start(bf16[768,768]{1,0:T(8,128)(2,1)} %convolution_convert_fusion.4), channel_id=1, source_target_pairs={{0,1},{1,0},{2,3},{3,2},{4,5},{5,4},{6,7},{7,6},{8,9},{9,8},{10,11... | collective-permute-start | bytes 3538952 | tf_op jit(solution)/shard_map/ppermute | solution.py:26
  257.4 263.2 %collective-permute-start.85 = (bf16[768,768]{1,0:T(8,128)(2,1)}, bf16[768,768]{1,0:T(8,128)(2,1)}, u32[]{:S(2)}, u32[]{:S(2)}) collective-permute-start(bf16[768,768]{1,0:T(8,128)(2,1)} %convolution_convert_fusion.5), channel_id=1, source_target_pairs={{0,1},{1,0},{2,3},{3,2},{4,5},{5,4},{6,7},{7,6},{8,9},{9,8},{10,11... | collective-permute-start | bytes 3538952 | tf_op jit(solution)/shard_map/ppermute | solution.py:26
  263.5 141.1 %collective-permute-start.104 = (bf16[768,768]{1,0:T(8,128)(2,1)}, bf16[768,768]{1,0:T(8,128)(2,1)}, u32[]{:S(2)}, u32[]{:S(2)}) collective-permute-start(bf16[768,768]{1,0:T(8,128)(2,1)} %convolution_convert_fusion), channel_id=1, source_target_pairs={{0,1},{1,0},{2,3},{3,2},{4,5},{5,4},{6,7},{7,6},{8,9},{9,8},{10,11... | collective-permute-start | bytes 3538952 | tf_op jit(solution)/shard_map/ppermute | solution.py:26
  263.7 298.4 %collective-permute-start.103 = (bf16[768,768]{1,0:T(8,128)(2,1)}, bf16[768,768]{1,0:T(8,128)(2,1)}, u32[]{:S(2)}, u32[]{:S(2)}) collective-permute-start(bf16[768,768]{1,0:T(8,128)(2,1)} %convolution_convert_fusion.1), channel_id=1, source_target_pairs={{0,1},{1,0},{2,3},{3,2},{4,5},{5,4},{6,7},{7,6},{8,9},{9,8},{10,11... | collective-permute-start | bytes 3538952 | tf_op jit(solution)/shard_map/ppermute | solution.py:26
  269.4 86.7 %collective-permute-start.70 = (bf16[96,768]{1,0:T(8,128)(2,1)S(1)}, bf16[96,768]{1,0:T(8,128)(2,1)S(1)}, u32[]{:S(2)}, u32[]{:S(2)}) collective-permute-start(bf16[96,768]{1,0:T(8,128)(2,1)S(1)} %dynamic-slice_convert_fusion.16), channel_id=1, source_target_pairs={{0,4},{4,0},{8,12},{12,8},{16,20},{20,16},{24,28},{28,24},{1,5},{5... | collective-permute-start | bytes 442376 | tf_op jit(solution)/shard_map/ppermute | solution.py:35
  414.0 87.2 %collective-permute-start.50 = (bf16[2304,192]{0,1:T(8,128)(2,1)}, bf16[2304,192]{0,1:T(8,128)(2,1)}, u32[]{:S(2)}, u32[]{:S(2)}) collective-permute-start(bf16[2304,192]{0,1:T(8,128)(2,1)} %pad_maximum_fusion.4), channel_id=1, source_target_pairs={{0,1},{1,0},{2,3},{3,2},{4,5},{5,4},{6,7},{7,6},{8,9},{9,8},{10,11... | collective-permute-start | bytes 2654216 | tf_op jit(solution)/shard_map/ppermute | solution.py:26
  415.0 67.8 %collective-permute-start.61 = (bf16[96,768]{1,0:T(8,128)(2,1)}, bf16[96,768]{1,0:T(8,128)(2,1)}, u32[]{:S(2)}, u32[]{:S(2)}) collective-permute-start(bf16[96,768]{1,0:T(8,128)(2,1)} %dynamic-slice_convert_fusion.17), channel_id=1, source_target_pairs={{0,4},{4,0},{8,12},{12,8},{16,20},{20,16},{24,28},{28,24},{1,5},{5... | collective-permute-start | bytes 442376 | tf_op jit(solution)/shard_map/ppermute | solution.py:35
  519.1 42.0 %collective-permute-start.51 = (bf16[2304,192]{0,1:T(8,128)(2,1)S(1)}, bf16[2304,192]{0,1:T(8,128)(2,1)S(1)}, u32[]{:S(2)}, u32[]{:S(2)}) collective-permute-start(bf16[2304,192]{0,1:T(8,128)(2,1)S(1)} %copy-done.223), channel_id=1, source_target_pairs={{0,2},{2,0},{1,3},{3,1},{4,6},{6,4},{5,7},{7,5},{8,10},{10,8},{9,1... | collective-permute-start | bytes 2654216 | tf_op jit(solution)/shard_map/ppermute | solution.py:30
  520.6 91.1 %collective-permute-start.76 = (bf16[768,768]{1,0:T(8,128)(2,1)S(1)}, bf16[768,768]{1,0:T(8,128)(2,1)S(1)}, u32[]{:S(2)}, u32[]{:S(2)}) collective-permute-start(bf16[768,768]{1,0:T(8,128)(2,1)S(1)} %copy-done.390), channel_id=1, source_target_pairs={{0,1},{1,0},{2,3},{3,2},{4,5},{5,4},{6,7},{7,6},{8,9},{9,8},{10,11... | collective-permute-start | bytes 3538952 | tf_op jit(solution)/shard_map/ppermute | solution.py:26
  542.2 44.2 %collective-permute-start.105 = (bf16[768,768]{1,0:T(8,128)(2,1)S(1)}, bf16[768,768]{1,0:T(8,128)(2,1)S(1)}, u32[]{:S(2)}, u32[]{:S(2)}) collective-permute-start(bf16[768,768]{1,0:T(8,128)(2,1)S(1)} %copy-done.391), channel_id=1, source_target_pairs={{0,2},{2,0},{1,3},{3,1},{4,6},{6,4},{5,7},{7,5},{8,10},{10,8},{9,1... | collective-permute-start | bytes 3538952 | tf_op jit(solution)/shard_map/ppermute | solution.py:30
  544.7 68.4 %collective-permute-start.94 = (bf16[768,768]{1,0:T(8,128)(2,1)S(1)}, bf16[768,768]{1,0:T(8,128)(2,1)S(1)}, u32[]{:S(2)}, u32[]{:S(2)}) collective-permute-start(bf16[768,768]{1,0:T(8,128)(2,1)S(1)} %copy-done.389), channel_id=1, source_target_pairs={{0,1},{1,0},{2,3},{3,2},{4,5},{5,4},{6,7},{7,6},{8,9},{9,8},{10,11... | collective-permute-start | bytes 3538952 | tf_op jit(solution)/shard_map/ppermute | solution.py:26
  561.2 51.2 %collective-permute-start.78 = (bf16[768,768]{1,0:T(8,128)(2,1)S(1)}, bf16[768,768]{1,0:T(8,128)(2,1)S(1)}, u32[]{:S(2)}, u32[]{:S(2)}) collective-permute-start(bf16[768,768]{1,0:T(8,128)(2,1)S(1)} %add_convert_fusion.3), channel_id=1, source_target_pairs={{0,2},{2,0},{1,3},{3,1},{4,6},{6,4},{5,7},{7,5},{8,10},{10,8},{9,1... | collective-permute-start | bytes 3538952 | tf_op jit(solution)/shard_map/ppermute | solution.py:30
  562.1 36.5 %collective-permute-start.88 = (bf16[384,768]{1,0:T(8,128)(2,1)S(1)}, bf16[384,768]{1,0:T(8,128)(2,1)S(1)}, u32[]{:S(2)}, u32[]{:S(2)}) collective-permute-start(bf16[384,768]{1,0:T(8,128)(2,1)S(1)} %dynamic-slice_convert_fusion.2), channel_id=1, source_target_pairs={{0,4},{4,0},{8,12},{12,8},{16,20},{20,16},{24,28},{28,24},{1,5},{5... | collective-permute-start | bytes 1769480 | tf_op jit(solution)/shard_map/ppermute | solution.py:35
  598.6 38.4 %collective-permute-start.96 = (bf16[768,768]{1,0:T(8,128)(2,1)S(1)}, bf16[768,768]{1,0:T(8,128)(2,1)S(1)}, u32[]{:S(2)}, u32[]{:S(2)}) collective-permute-start(bf16[768,768]{1,0:T(8,128)(2,1)S(1)} %add_convert_fusion.1), channel_id=1, source_target_pairs={{0,2},{2,0},{1,3},{3,1},{4,6},{6,4},{5,7},{7,5},{8,10},{10,8},{9,1... | collective-permute-start | bytes 3538952 | tf_op jit(solution)/shard_map/ppermute | solution.py:30
  611.7 43.9 %collective-permute-start.42 = (bf16[2304,192]{0,1:T(8,128)(2,1)S(1)}, bf16[2304,192]{0,1:T(8,128)(2,1)S(1)}, u32[]{:S(2)}, u32[]{:S(2)}) collective-permute-start(bf16[2304,192]{0,1:T(8,128)(2,1)S(1)} %fusion.49), channel_id=1, source_target_pairs={{0,2},{2,0},{1,3},{3,1},{4,6},{6,4},{5,7},{7,5},{8,10},{10,8},{9,1... | collective-permute-start | bytes 2654216 | tf_op jit(solution)/shard_map/ppermute | solution.py:30
  612.4 44.0 %collective-permute-start.53 = (bf16[576,192]{0,1:T(8,128)(2,1)S(1)}, bf16[576,192]{0,1:T(8,128)(2,1)S(1)}, u32[]{:S(2)}, u32[]{:S(2)}) collective-permute-start(bf16[576,192]{0,1:T(8,128)(2,1)S(1)} %dynamic-slice_convert_fusion.10), channel_id=1, source_target_pairs={{0,8},{4,12},{8,0},{12,4},{16,24},{20,28},{24,16},{28,20},{1,9},{5... | collective-permute-start | bytes 663560 | tf_op jit(solution)/shard_map/ppermute | solution.py:35
  613.1 54.5 %collective-permute-start.89 = (bf16[192,768]{1,0:T(8,128)(2,1)S(1)}, bf16[192,768]{1,0:T(8,128)(2,1)S(1)}, u32[]{:S(2)}, u32[]{:S(2)}) collective-permute-start(bf16[192,768]{1,0:T(8,128)(2,1)S(1)} %dynamic-slice_convert_fusion.8), channel_id=1, source_target_pairs={{0,8},{4,12},{8,0},{12,4},{16,24},{20,28},{24,16},{28,20},{1,9},{5... | collective-permute-start | bytes 884744 | tf_op jit(solution)/shard_map/ppermute | solution.py:35
  638.4 63.8 %collective-permute-start.79 = (bf16[384,768]{1,0:T(8,128)(2,1)S(1)}, bf16[384,768]{1,0:T(8,128)(2,1)S(1)}, u32[]{:S(2)}, u32[]{:S(2)}) collective-permute-start(bf16[384,768]{1,0:T(8,128)(2,1)S(1)} %dynamic-slice_convert_fusion.3), channel_id=1, source_target_pairs={{0,4},{4,0},{8,12},{12,8},{16,20},{20,16},{24,28},{28,24},{1,5},{5... | collective-permute-start | bytes 1769480 | tf_op jit(solution)/shard_map/ppermute | solution.py:35
  655.6 48.9 %collective-permute-start.97 = (bf16[384,768]{1,0:T(8,128)(2,1)S(1)}, bf16[384,768]{1,0:T(8,128)(2,1)S(1)}, u32[]{:S(2)}, u32[]{:S(2)}) collective-permute-start(bf16[384,768]{1,0:T(8,128)(2,1)S(1)} %dynamic-slice_convert_fusion.1), channel_id=1, source_target_pairs={{0,4},{4,0},{8,12},{12,8},{16,20},{20,16},{24,28},{28,24},{1,5},{5... | collective-permute-start | bytes 1769480 | tf_op jit(solution)/shard_map/ppermute | solution.py:35
  698.5 43.4 %collective-permute-start.57 = (bf16[1152,192]{0,1:T(8,128)(2,1)S(1)}, bf16[1152,192]{0,1:T(8,128)(2,1)S(1)}, u32[]{:S(2)}, u32[]{:S(2)}) collective-permute-start(bf16[1152,192]{0,1:T(8,128)(2,1)S(1)} %pad_maximum_fusion.19), channel_id=1, source_target_pairs={{0,4},{4,0},{8,12},{12,8},{16,20},{20,16},{24,28},{28,24},{1,5},{5... | collective-permute-start | bytes 1327112 | tf_op jit(solution)/shard_map/ppermute | solution.py:35
  728.7 36.3 %collective-permute-start.93 = (bf16[384,768]{1,0:T(8,128)(2,1)}, bf16[384,768]{1,0:T(8,128)(2,1)}, u32[]{:S(2)}, u32[]{:S(2)}) collective-permute-start(bf16[384,768]{1,0:T(8,128)(2,1)} %pad_maximum_fusion.15), channel_id=1, source_target_pairs={{0,4},{4,0},{8,12},{12,8},{16,20},{20,16},{24,28},{28,24},{1,5},{5... | collective-permute-start | bytes 1769480 | tf_op jit(solution)/shard_map/ppermute | solution.py:35
  (484 other events, 4457.7 us)

commit v2 on v1

v2 whole, which is shorter than its diff:
```python
from functools import partial

import jax
import jax.numpy as jnp
from jax import lax
from jax.experimental import pallas as pl
from jax.experimental.pallas import tpu as pltpu
from jax.sharding import PartitionSpec as P

HEAD_DIM = 64
LEN = 832
SIDE_S = 14
SIDE_M = 20
SIDE_L = 24
MAX_IMAGES = 4
LAYERS = 2

EPS = 1e-06
NEGATIVE = -1000000000.0
BF = jnp.bfloat16
F32 = jnp.float32

CORE = [(0, 1), (1, 0), (2, 3), (3, 2)]
ACROSS = [(0, 2), (2, 0), (1, 3), (3, 1)]


def over_core(values):
    return lax.ppermute(values, "tensor", CORE)


def over_y(values):
    return lax.ppermute(values, "tensor", ACROSS)


def over_bit(values, bit):
    size = lax.axis_size("dp")
    return lax.ppermute(values, "dp", [(at, at ^ (1 << bit)) for at in range(size)])


def places_at(lengths, position):
    ends = jnp.cumsum(lengths)
    starts = ends - lengths
    segment = jnp.sum((position[:, None] >= ends[None, :]).astype(jnp.int32), axis=1)
    belongs = segment[:, None] == jnp.arange(MAX_IMAGES, dtype=jnp.int32)[None, :]
    begin_at = jnp.sum(jnp.where(belongs, starts[None, :], 0), axis=1)
    size = jnp.sum(jnp.where(belongs, lengths[None, :], 0), axis=1)
    side = jnp.where(
        size == SIDE_S * SIDE_S, SIDE_S, jnp.where(size == SIDE_M * SIDE_M, SIDE_M, SIDE_L)
    ).astype(jnp.int32)
    offset = position - begin_at
    inside = segment < MAX_IMAGES
    row_at = jnp.where(inside, offset // side, 0)
    column_at = jnp.where(inside, offset % side, 0)
    return segment, row_at, column_at


PLANS = (
    (((3, 2), (5, 1), (6, 1), (7, 1), (8, 1), (9, 1), (10, 1)), ((4, 1), (5, 1), (6, 1), (7, 1), (8, 1), (9, 1), (10, 1))),
    (
        ((3, 2), (5, 1), (6, 1), (7, 1), (8, 1), (9, 1), (10, 1)),
        ((5, 1), (6, 1), (7, 1), (8, 1), (9, 1), (10, 1), (11, 1)),
    ),
)
SMALL_PLAN = ((1, 1), (2, 1), (3, 1), (4, 1), (5, 1), (6, 1))
VMEM_BYTES = 58 * 2**20
PARAMS = pltpu.CompilerParams(vmem_limit_bytes=VMEM_BYTES)
WHOLE = pl.BlockSpec(memory_space=pltpu.VMEM)
PLACE = pl.BlockSpec(memory_space=pl.ANY)
SCALAR = pl.BlockSpec(memory_space=pltpu.SMEM)
HALF = HEAD_DIM // 2
SIDE_ROWS = 32
SMALL_ROWS = 16


def dot(left, right, on_left, on_right):
    return lax.dot_general(
        left, right, (((on_left,), (on_right,)), ((), ())), preferred_element_type=F32
    )


def norm_parts(values):
    average = jnp.mean(values, axis=-1, keepdims=True)
    centred = values - average
    variance = jnp.mean(centred * centred, axis=-1, keepdims=True)
    inverse = lax.rsqrt(variance + EPS)
    return centred * inverse, inverse


def norm_back(values, gain, incoming):
    xhat, inverse = norm_parts(values)
    grad_gain = jnp.sum(incoming * xhat, axis=0, keepdims=True)
    grad_shift = jnp.sum(incoming, axis=0, keepdims=True)
    scaled = incoming * gain
    through = inverse * (
        scaled
        - jnp.mean(scaled, axis=-1, keepdims=True)
        - xhat * jnp.mean(scaled * xhat, axis=-1, keepdims=True)
    )
    return through, grad_gain, grad_shift


def first_half(shape):
    return lax.broadcasted_iota(jnp.int32, shape, 1) % HEAD_DIM < HALF


def swap(values):
    width = values.shape[1]
    return jnp.where(
        first_half(values.shape),
        pltpu.roll(values, width - HALF, 1),
        pltpu.roll(values, HALF, 1),
    )


def one_head(values, head):
    lane = lax.broadcasted_iota(jnp.int32, values.shape, 1)
    return jnp.where((lane < HEAD_DIM) == (head == 0), values, jnp.zeros_like(values))


def join_heads(first, second):
    lane = lax.broadcasted_iota(jnp.int32, first.shape, 1)
    return jnp.where(lane < HEAD_DIM, first, second)


class Held:
    def __init__(self, source, buffer, sem):
        self.copy, self.buffer, self.done = pltpu.make_async_copy(source, buffer, sem), buffer, False
        self.shape, self.dtype = buffer.shape, buffer.dtype
        self.copy.start()

    def wait(self):
        if not self.done:
            self.copy.wait()
            self.done = True

    def __getitem__(self, at):
        self.wait()
        return self.buffer[at]


class Given:
    def __init__(self, target, buffer, sems):
        self.target, self.buffer, self.sems, self.copies = target, buffer, sems, []

    def __setitem__(self, at, values):
        self.buffer[at] = values

    def __getitem__(self, at):
        return self.buffer[at]

    def leave(self, at=None):
        source, target = self.buffer, self.target
        if at is not None:
            source, target = source.at[at], target.at[at]
        self.copies.append(pltpu.make_async_copy(source, target, self.sems.at[len(self.copies)]))
        self.copies[-1].start()


PIECES_OUT = 6


def staged(body, name, flops, scalars, inputs, raws, outs, raw_outs=(), scratch=(), gates=()):
    counts = [len(inputs), len(raws), len(gates), len(outs), len(raw_outs)]

    def kernel(numbers, *refs):
        groups = []
        for count in counts:
            groups.append(refs[:count])
            refs = refs[count:]
        sources, plain, _, targets, plain_targets = groups
        in_buffers, out_buffers, rest = refs[: counts[0]], refs[counts[0] : counts[0] + counts[3]], refs[counts[0] + counts[3] :]
        in_sems, out_sems, rest = rest[0], rest[1], rest[2:]
        held = [Held(*item, in_sems.at[at]) for at, item in enumerate(zip(sources, in_buffers))]
        given = [Given(*item, out_sems.at[at]) for at, item in enumerate(zip(targets, out_buffers))]
        body(numbers, held, plain, given, plain_targets, *rest)
        for item in held:
            item.wait()
        for item in given:
            if not item.copies:
                item.leave()
        for item in given:
            for copy in item.copies:
                copy.wait()

    return pl.pallas_call(
        kernel,
        out_shape=list(outs) + list(raw_outs),
        in_specs=[SCALAR] + [PLACE] * sum(counts[:3]),
        out_specs=[PLACE] * sum(counts[3:]),
        scratch_shapes=[pltpu.VMEM(item.shape, item.dtype) for item in list(inputs) + list(outs)]
        + [pltpu.SemaphoreType.DMA((max(counts[0], 1),)), pltpu.SemaphoreType.DMA((max(counts[3], 1), PIECES_OUT))]
        + list(scratch),
        compiler_params=PARAMS,
        name=name,
        cost_estimate=pl.CostEstimate(flops=flops // 8, bytes_accessed=2**20, transcendentals=0),
    )(scalars, *inputs, *raws, *gates)


def fetch(pairs, sems):
    copies = [pltpu.make_async_copy(source, target, sems.at[at]) for at, (source, target) in enumerate(pairs)]
    for copy in copies:
        copy.start()
    return copies


def att_pairs(near, refs, into, xbit, parts):
    inner = into.shape[1] // 2
    low, high = pl.ds(0, inner), pl.ds(inner, inner)
    if near:
        return [(refs[0].at[pl.ds(0, parts)], into.at[pl.ds(0, parts), low]), (refs[1].at[pl.ds(0, parts)], into.at[pl.ds(0, parts), high])]
    mine, other = pl.ds(2 * xbit, 2), pl.ds(2 - 2 * xbit, 2)
    return [
        (refs[0], into.at[mine, low]),
        (refs[1], into.at[other, low]),
        (refs[2], into.at[mine, high]),
        (refs[3], into.at[other, high]),
    ]


def mlp_pairs(near, refs, into, xbit):
    if near:
        return [(ref, into.at[quarter]) for quarter, ref in enumerate(refs)]
    slots = ((0, xbit), (0, 1 - xbit), (1, xbit), (1, 1 - xbit))
    return [(ref, into.at[quarter, slot]) for ref, (quarter, slot) in zip(refs, slots)]


def pack(layer, x_bit, first, second, cut, gates=()):
    _, rows, width, inner = first.shape
    more = second.shape[1]

    def body(numbers, _, raws, __, targets, held, sems):
        whole, half = targets
        for copy in fetch(
            [(raws[0].at[layer], held.at[pl.ds(0, rows)]), (raws[1].at[layer], held.at[pl.ds(rows, more)])], sems
        ):
            copy.wait()
        copies = [
            pltpu.make_async_copy(held.at[pl.ds(cut * numbers[0], cut)], half, sems.at[2]),
            pltpu.make_async_copy(held, whole, sems.at[3]),
        ]
        for copy in copies:
            copy.start()
        for copy in copies:
            copy.wait()

    return staged(
        body, "pack", 0, x_bit, (), (first, second), (),
        (
            jax.ShapeDtypeStruct((rows + more, width, inner), BF),
            jax.ShapeDtypeStruct((cut, width, inner), BF),
        ),
        (pltpu.VMEM((rows + more, width, inner), BF), pltpu.SemaphoreType.DMA((4,))), gates,
    )


def angle_tables(freqs, places):
    steps = lax.broadcasted_iota(jnp.int32, (SIDE_ROWS, 1), 0).astype(F32)
    found = []
    for axis in range(2):
        terms = steps * freqs[axis]
        table = jnp.concatenate([jnp.cos(terms), jnp.sin(terms)], axis=1)
        at = places[:, axis : axis + 1]
        column = lax.broadcasted_iota(jnp.int32, (places.shape[0], SIDE_ROWS), 1).astype(F32)
        chosen = lax.dot_general(
            (column == at).astype(F32), table, (((1,), (0,)), ((), ())),
            precision=lax.Precision.HIGHEST, preferred_element_type=F32,
        )
        width = terms.shape[1]
        found.append((chosen[:, :width], chosen[:, width:]))
    (row_cos, row_sin), (col_cos, col_sin) = found
    cosine = row_cos * col_cos - row_sin * col_sin
    sine = row_sin * col_cos + row_cos * col_sin
    return cosine, jnp.where(first_half(sine.shape), -sine, sine)


def qkv_part(near, layer, x_bit, source, gain, shift, small, places, weights, gates=()):
    count, width = source.shape
    inner = weights[0].shape[1]

    def body(numbers, inputs, raws, results, _, held, sems):
        gain, shift, places, first, second, source = inputs
        query, kept, sent, cosine, sine = results[:5]
        copies = fetch(att_pairs(near, raws, held, numbers[0], 3), sems)
        both = [item[layer : layer + 1] for item in (first, second)]
        bias = [
            jnp.concatenate([item[:, part * inner : (part + 1) * inner] for item in both], axis=1)
            for part in range(3)
        ]
        freqs = []
        for axis in range(2):
            begin = 3 * inner + axis * (inner // 2)
            pieces = [item[:, at : at + HALF] for item in both for at in range(begin, begin + inner // 2, HALF)]
            freqs.append(jnp.concatenate([piece for piece in pieces for _ in range(2)], axis=1))
        cosine[...], sine[...] = angle_tables(freqs, places[...])
        cosine.leave()
        sine.leave()
        if near:
            xhat, _ = norm_parts(source[...].astype(F32))
            normed = (xhat * gain[...] + shift[...]).astype(BF)
            results[5][...] = normed
            results[5].leave()
        else:
            normed = source[...]
        for copy in copies:
            copy.wait()
        for part in (1, 2, 0):
            values = dot(normed, held[part], 1, 1) + bias[part]
            if part < 2:
                values = values * cosine[...] + swap(values) * sine[...]
            if part == 0:
                query[...] = (values * HEAD_DIM**-0.5).astype(BF)
            else:
                kept[part - 1] = values.astype(BF)
                sent[part - 1] = pltpu.roll(values, inner, 1).astype(BF)
                sent.leave(part - 1)

    pair = jax.ShapeDtypeStruct((2, count, 2 * inner), BF)
    table = jax.ShapeDtypeStruct((count, 2 * inner), F32)
    outs = [jax.ShapeDtypeStruct((count, 2 * inner), BF), pair, pair, table, table]
    if near:
        outs.append(jax.ShapeDtypeStruct((count, width), BF))
    return staged(
        body, "qkv_near" if near else "qkv_far", 2 * count * width * 6 * inner, x_bit,
        (gain, shift, places, *small, source), weights, outs,
        scratch=(pltpu.VMEM((4, 2 * inner, width), BF), pltpu.SemaphoreType.DMA((len(weights),))), gates=gates,
    )


def attend(query, kept, came, here, there, number, gates=()):
    count, width = query.shape
    heads = width // HEAD_DIM

    def body(_, inputs, __, results, ___):
        query, kept, here, came, there = inputs
        mixed, spread, exps = results
        allowed = here[...] == there[...]
        for pair in range(heads // 2):
            lanes = slice(2 * HEAD_DIM * pair, 2 * HEAD_DIM * (pair + 1))
            keys = jnp.concatenate([kept[0, :, lanes], came[0, :, lanes]], axis=0)
            values = jnp.concatenate([kept[1, :, lanes], came[1, :, lanes]], axis=0)
            outs, inverses = [], []
            for head in range(2):
                scores = dot(one_head(query[:, lanes], head), keys, 1, 1)
                scores = jnp.where(allowed, scores, NEGATIVE)
                highest = jnp.max(scores, axis=1, keepdims=True)
                raised = jnp.exp(scores - highest)
                inverse = 1.0 / jnp.sum(raised, axis=1, keepdims=True)
                low = raised.astype(BF)
                exps[2 * pair + head] = low
                exps.leave(2 * pair + head)
                outs.append(dot(low, values, 1, 0) * inverse)
                inverses.append(jnp.broadcast_to(inverse, outs[0].shape))
            mixed[:, lanes] = join_heads(*outs).astype(BF)
            spread[:, lanes] = join_heads(*inverses)

    return staged(
        body, "attend", 8 * count * width * 768, number, (query, kept, here, came, there), (),
        (
            jax.ShapeDtypeStruct((count, width), BF),
            jax.ShapeDtypeStruct((count, width), F32),
            jax.ShapeDtypeStruct((heads, count, 2 * count), BF),
        ),
        gates=gates,
    )


def gelu_parts(pre):
    size = jnp.abs(pre)
    ratio = 1.0 / (1.0 + 0.3275911 * (0.5**0.5) * size)
    bell = jnp.exp(-0.5 * pre * pre)
    poly = ((((0.5 * 1.061405429 * ratio - 0.5 * 1.453152027) * ratio + 0.5 * 1.421413741) * ratio - 0.5 * 0.284496736) * ratio + 0.5 * 0.254829592) * ratio
    below = poly * bell
    normal = jnp.where(pre < 0, below, 1.0 - below)
    return pre * normal, normal + pre * (bell * 0.3989422804014327)


def feed(quarter, normed, held, up_bias, active, slope):
    value, rate = gelu_parts(dot(normed, held[quarter, 0], 1, 0) + up_bias[quarter])
    low = value.astype(BF)
    active[quarter] = low
    active.leave(quarter)
    slope[quarter] = rate.astype(BF)
    slope.leave(quarter)
    return dot(low, held[quarter, 1], 1, 0)


def mlp_near(layer, x_bit, inputs, mixed_near, mixed_far, out_bias, gain, shift, small, down_bias, outs, weights, gates=()):
    count, width = inputs.shape
    hidden = weights[0].shape[2]
    inner = outs[0].shape[1]

    def body(numbers, held_inputs, raws, results, _, held_out, held, sems):
        mixed_near, mixed_far, inputs, out_bias, gain, shift, first, second, down_bias = held_inputs
        up_bias = [item[layer : layer + 1, width:] for item in (first, second)]
        middle, normed_out, active, slope, total = results
        xbit = numbers[0]
        copies = fetch(
            [
                (raws[0].at[3], held_out.at[0]),
                (raws[1].at[3], held_out.at[1]),
                (raws[2].at[1], held_out.at[2 + 2 * (1 - xbit)]),
                (raws[3].at[1], held_out.at[2 + 2 * xbit]),
                (raws[4].at[1], held_out.at[3 + 2 * (1 - xbit)]),
                (raws[5].at[1], held_out.at[3 + 2 * xbit]),
            ]
            + mlp_pairs(True, raws[6:], held, xbit),
            sems,
        )
        for copy in copies[:6]:
            copy.wait()
        centre = dot(mixed_near[...], jnp.concatenate([held_out[0], held_out[1]], axis=0), 1, 0)
        centre = centre + dot(mixed_far[...], jnp.concatenate([held_out[2], held_out[3]], axis=0), 1, 0)
        centre = centre + inputs[...].astype(F32) + out_bias[...]
        middle[...] = centre
        middle.leave()
        xhat, _ = norm_parts(centre)
        normed = (xhat * gain[...] + shift[...]).astype(BF)
        normed_out[...] = normed
        normed_out.leave()
        gathered = centre + down_bias[...]
        for quarter in range(2):
            copies[6 + quarter].wait()
            gathered = gathered + feed(quarter, normed, held, up_bias, active, slope)
        total[...] = gathered

    kept = jax.ShapeDtypeStruct((2, count, hidden), BF)
    full = jax.ShapeDtypeStruct((count, width), F32)
    return staged(
        body, "mlp_near", 10 * count * width * width, x_bit,
        (mixed_near, mixed_far, inputs, out_bias, gain, shift, *small, down_bias), tuple(outs) + tuple(weights),
        (full, jax.ShapeDtypeStruct((count, width), BF), kept, kept, full),
        scratch=(
            pltpu.VMEM((6, inner, width), BF),
            pltpu.VMEM((2, 2, width, hidden), BF),
            pltpu.SemaphoreType.DMA((8,)),
        ),
        gates=gates,
    )


def mlp_far(layer, x_bit, normed, total, small, weights, dtype, gates=()):
    count, width = normed.shape
    hidden = weights[0].shape[1]

    def body(numbers, inputs, raws, results, _, held, sems):
        normed, first, second, total = inputs
        up_bias = [item[layer : layer + 1, width:] for item in (first, second)]
        active, slope, result = results
        copies = fetch(mlp_pairs(False, raws, held, numbers[0]), sems)
        gathered = None
        for quarter in range(2):
            for copy in copies[2 * quarter : 2 * quarter + 2]:
                copy.wait()
            term = feed(quarter, normed[...], held, up_bias, active, slope)
            gathered = total[...] + term if gathered is None else gathered + term
        result[...] = gathered.astype(dtype)

    kept = jax.ShapeDtypeStruct((2, count, hidden), BF)
    return staged(
        body, "mlp_far", 8 * count * width * width, x_bit, (normed, *small, total), weights,
        (kept, kept, jax.ShapeDtypeStruct((count, width), dtype)),
        scratch=(pltpu.VMEM((2, 2, width, hidden), BF), pltpu.SemaphoreType.DMA((4,))), gates=gates,
    )


def mlp_back(x_bit, gradient, normed, middle, gain, active, slope, near, far, gates=()):
    count, width = normed.shape
    hidden = active[0].shape[2]

    def body(numbers, inputs, raws, results, grads, held, ready, sems, out_sems):
        gradient, active_far, slope_far, normed, active_near, slope_near, gain, middle = inputs
        bias_grad, sums, grad_middle, low_middle = results
        xbit, up_slot = numbers[0], numbers[1]
        targets = (grads[0:1], grads[1:5], grads[5:6], grads[6:10])
        copies = fetch(
            mlp_pairs(False, raws[2:], held.at[pl.ds(2, 2)], xbit) + mlp_pairs(True, raws[:2], held.at[pl.ds(0, 2)], xbit), sems
        )
        needed = ((copies[4],), (copies[5],), copies[0:2], copies[2:4])
        leaving = []

        def leave(quarter, kind, slot, values):
            ready[quarter, kind] = values.astype(BF)
            rows = targets[quarter][0].shape[1]
            for at, target in enumerate(targets[quarter]):
                copy = pltpu.make_async_copy(
                    ready.at[quarter, kind, pl.ds(at * rows, rows)], target.at[slot], out_sems.at[len(leaving)]
                )
                copy.start()
                leaving.append(copy)

        incoming = gradient[...].astype(F32)
        low = incoming.astype(BF)
        gathered = None
        for quarter in (3, 2, 1, 0):
            active, slope = (active_near, slope_near) if quarter < 2 else (active_far, slope_far)
            leave(quarter, 0, 1 - up_slot, dot(active[quarter % 2], low, 0, 0))
            for copy in needed[quarter]:
                copy.wait()
            inside = dot(low, held[quarter, 1], 1, 1) * slope[quarter % 2].astype(F32)
            low_inside = inside.astype(BF)
            bias_grad[quarter : quarter + 1] = jnp.sum(low_inside.astype(F32), axis=0, keepdims=True)
            leave(quarter, 1, up_slot, dot(normed[...], low_inside, 0, 0))
            term = dot(low_inside, held[quarter, 0], 1, 1)
            gathered = term if gathered is None else gathered + term
        through, grad_gain, grad_shift = norm_back(middle[...], gain[...], gathered)
        result = incoming + through
        grad_middle[...] = result
        grad_middle.leave()
        low_result = result.astype(BF)
        low_middle[...] = low_result
        low_middle.leave()
        sums[0:1] = grad_gain
        sums[1:2] = grad_shift
        sums[2:3] = jnp.sum(low_result.astype(F32), axis=0, keepdims=True)
        sums[3:4] = jnp.sum(low.astype(F32), axis=0, keepdims=True)
        for copy in leaving:
            copy.wait()

    whole = jax.ShapeDtypeStruct((2, width, hidden), BF)
    part = jax.ShapeDtypeStruct((2, width // 4, hidden), BF)
    outs = [
        jax.ShapeDtypeStruct((4, hidden), F32),
        jax.ShapeDtypeStruct((4, width), F32),
        jax.ShapeDtypeStruct((count, width), F32),
        jax.ShapeDtypeStruct((count, width), BF),
    ]
    found = staged(
        body, "mlp_back", 32 * count * width * width, x_bit,
        (gradient, active[1], slope[1], normed, active[0], slope[0], gain, middle), tuple(near) + tuple(far), outs,
        ([whole] + [part] * 4) * 2,
        (
            pltpu.VMEM((4, 2, width, hidden), BF),
            pltpu.VMEM((4, 2, width, hidden), BF),
            pltpu.SemaphoreType.DMA((6,)),
            pltpu.SemaphoreType.DMA((20,)),
        ),
        gates,
    )
    return (found[4], found[5:9], found[9], found[10:14]), found[:4]


def attend_back(x_bit, incoming, sides, near, far, gates=()):
    count, width = sides[0][0].shape
    pairs = width // (2 * HEAD_DIM)
    inner, full = near[0].shape[1:]

    def body(numbers, inputs, raws, results, _, held, sems):
        incoming, xbit = inputs[0], numbers[0]
        copies = fetch(
            [
                (raws[0].at[3], held.at[0]),
                (raws[1].at[3], held.at[1]),
                (raws[2].at[1], held.at[2 + 2 * (1 - xbit)]),
                (raws[3].at[1], held.at[2 + 2 * xbit]),
                (raws[4].at[1], held.at[3 + 2 * (1 - xbit)]),
                (raws[5].at[1], held.at[3 + 2 * xbit]),
            ],
            sems,
        )
        for copy in copies:
            copy.wait()
        for side in (0, 1):
            mixed, spread, kept, came, query, exps = inputs[1 + 6 * side : 7 + 6 * side]
            grad_query, grad_kept, *grad_sent = results[4 * side : 4 * side + 4]
            both = jnp.concatenate([held[2 * side], held[2 * side + 1]], axis=0)
            scaled = dot(incoming[...], both, 1, 1) * spread[...]
            product_all = scaled * mixed[...].astype(F32)
            low_all = scaled.astype(BF)
            for pair in range(pairs):
                lanes = slice(2 * HEAD_DIM * pair, 2 * HEAD_DIM * (pair + 1))
                keys = jnp.concatenate([kept[0, :, lanes], came[0, :, lanes]], axis=0)
                values = jnp.concatenate([kept[1, :, lanes], came[1, :, lanes]], axis=0)
                low_mixed, product = low_all[:, lanes], product_all[:, lanes]
                for_query, for_key, for_value = [], [], []
                for head in range(2):
                    raised = exps[2 * pair + head]
                    level = jnp.sum(one_head(product, head), axis=1, keepdims=True)
                    grad_probs = dot(one_head(low_mixed, head), values, 1, 1)
                    grad_scores = (raised.astype(F32) * (grad_probs - level)).astype(BF)
                    for_value.append(dot(raised, low_mixed, 0, 0))
                    for_query.append(dot(grad_scores, keys, 1, 0))
                    for_key.append(dot(grad_scores, query[:, lanes], 0, 0))
                grad_query[:, lanes] = join_heads(*for_query).astype(BF)
                for part, both_heads in enumerate((for_key, for_value)):
                    joined = join_heads(*both_heads).astype(BF)
                    grad_kept[part, :, lanes] = joined[:count]
                    grad_sent[part][:, lanes] = joined[count:]
            for item in results[4 * side : 4 * side + 4]:
                item.leave()

    shapes = [
        jax.ShapeDtypeStruct((count, width), BF),
        jax.ShapeDtypeStruct((2, count, width), BF),
        jax.ShapeDtypeStruct((count, width), BF),
        jax.ShapeDtypeStruct((count, width), BF),
    ]
    ordered = [incoming]
    for query, kept, came, mixed, spread, exps in sides:
        ordered += [mixed, spread, kept, came, query, exps]
    found = staged(
        body, "attend_back", 32 * count * width * full, x_bit, ordered, tuple(near) + tuple(far), shapes * 2,
        scratch=(pltpu.VMEM((6, inner, full), BF), pltpu.SemaphoreType.DMA((6,))),
        gates=gates,
    )
    return found[:4], found[4:]


def qkv_back(x_bit, normed, incoming, places, sides, near, far, gain, inputs_kept, grad_middle, little, gates=()):
    count, width = normed.shape
    inner = near[0].shape[1]

    def body(numbers, inputs, raws, results, grads, held, ready, sems, out_sems):
        normed, incoming, places = inputs[:3]
        gain, inputs_kept, grad_middle, sums2, up_bias_grad = inputs[21:26]
        rows_out, result = results
        earlier = inputs[26:]
        base = SMALL_ROWS * len(earlier)
        for at, item in enumerate(earlier):
            rows_out[SMALL_ROWS * at : SMALL_ROWS * (at + 1)] = item[...]
        xbit = numbers[0]
        targets = (grads[0:1], grads[1:5], grads[5:6], grads[6:10])
        copies = fetch(
            att_pairs(False, raws[2:], held.at[1], xbit, 3) + att_pairs(True, raws[:2], held.at[0], xbit, 3), sems
        )
        needed = (copies[4:], copies[:4])
        slots = (2 * xbit, 2 * xbit + 1, 2 - 2 * xbit, 3 - 2 * xbit)
        leaving = []

        def store(side, part, values):
            ready[side, part] = values.astype(BF)
            for quarter in range(2):
                rows = targets[2 * side + quarter][0].shape[1]
                for at, target in enumerate(targets[2 * side + quarter]):
                    copy = pltpu.make_async_copy(
                        ready.at[side, part, pl.ds(quarter * inner + at * rows, rows)],
                        target.at[slots[part]],
                        out_sems.at[len(leaving)],
                    )
                    copy.start()
                    leaving.append(copy)

        gathered = None
        for side in (1, 0):
            mixed, grad_query, query, grad_kept, came_key, came_value, kept, cosine, sine = inputs[3 + 9 * side : 12 + 9 * side]
            lanes = slice(2 * inner * side, 2 * inner * (side + 1))
            store(side, 3, dot(mixed[...], incoming[...], 0, 0))
            sign = jnp.where(first_half(query.shape), -1.0, 1.0)
            raw_query = grad_query[...].astype(F32)
            raw_key = grad_kept[0].astype(F32) + pltpu.roll(came_key[...].astype(F32), inner, 1)
            raw_value = grad_kept[1].astype(F32) + pltpu.roll(came_value[...].astype(F32), inner, 1)
            angle = (raw_query * swap(query[...].astype(F32)) + raw_key * swap(kept[0].astype(F32))) * sign
            for axis in range(2):
                rows_out[base + 13 + axis : base + 14 + axis, lanes] = jnp.sum(
                    angle * places[:, axis : axis + 1], axis=0, keepdims=True
                )
            cos, sin = cosine[...], sine[...]
            turned = (
                (raw_query * cos - swap(raw_query) * sin) * HEAD_DIM**-0.5,
                raw_key * cos - swap(raw_key) * sin,
                raw_value,
            )
            lows = [item.astype(BF) for item in turned]
            for part in range(3):
                rows_out[base + 10 + part : base + 11 + part, lanes] = jnp.sum(
                    lows[part].astype(F32), axis=0, keepdims=True
                )
                store(side, part, dot(lows[part], normed[...], 0, 0))
            for copy in needed[side]:
                copy.wait()
            for part in range(3):
                term = dot(lows[part], held[side, part], 1, 0)
                gathered = term if gathered is None else gathered + term
        through, grad_gain, grad_shift = norm_back(inputs_kept[...].astype(F32), gain[...], gathered)
        result[...] = grad_middle[...] + through
        rows_out[base : base + 1] = grad_gain
        rows_out[base + 1 : base + 2] = grad_shift
        rows_out[base + 2 : base + 3] = sums2[2:3]
        rows_out[base + 3 : base + 5] = sums2[0:2]
        rows_out[base + 5 : base + 6] = sums2[3:4]
        rows_out[base + 6 : base + 10] = up_bias_grad[...]
        rows_out[base + 15 : base + 16] = jnp.zeros((1, rows_out.buffer.shape[1]), F32)
        for copy in leaving:
            copy.wait()

    rows = SMALL_ROWS * (len(little) - 1)
    outs = [jax.ShapeDtypeStruct((rows, width), F32), jax.ShapeDtypeStruct((count, width), F32)]
    whole = jax.ShapeDtypeStruct((4, inner, width), BF)
    part = jax.ShapeDtypeStruct((4, inner // 4, width), BF)
    ordered = [normed, incoming, places]
    for grad_query, grad_kept, came_key, came_value, query, kept, cosine, sine, mixed in sides:
        ordered += [mixed, grad_query, query, grad_kept, came_key, came_value, kept, cosine, sine]
    found = staged(
        body, "qkv_back", 32 * count * width * 2 * inner, x_bit,
        ordered + [gain, inputs_kept, grad_middle] + list(little), tuple(near) + tuple(far), outs,
        ([whole] + [part] * 4) * 2,
        (
            pltpu.VMEM((2, 4, 2 * inner, width), BF),
            pltpu.VMEM((2, 4, 2 * inner, width), BF),
            pltpu.SemaphoreType.DMA((6,)),
            pltpu.SemaphoreType.DMA((40,)),
        ),
        gates,
    )
    return (found[2], found[3:7], found[7], found[8:12]), found[:2]


def run_tasks(place, tasks, gates):
    inputs = [item for task in tasks for item in task[0]]
    outs = [jax.ShapeDtypeStruct(*item) for task in tasks for item in task[1]]

    def body(at, sources, _, results, __):
        for task in tasks:
            task[2](at[0], sources[: len(task[0])], results[: len(task[1])])
            sources, results = sources[len(task[0]) :], results[len(task[1]) :]

    found = staged(body, "sums", 0, place, inputs, (), outs, gates=gates)
    given = []
    for task in tasks:
        given.append(found[: len(task[1])])
        found = found[len(task[1]) :]
    return given


def wide(ref):
    return ref[...].astype(F32)


class Piece:
    def begin(self, found):
        self.own, first, self.second, third = found
        self.came_near = [over_core(item) for item in first]
        self.came_far = [over_core(item) for item in third]
        return self.came_near + self.came_far

    def sources(self):
        return (self.own, self.second, *self.came_near, *self.came_far)

    def sum_of(self, sources, quarter, slot, high):
        mine = sources[quarter]
        parts = sources[2 + 4 * quarter : 6 + 4 * quarter]
        if mine.shape[0] == 2:
            rows = mine.shape[1] // 2
            own = mine[slot, high * rows : (high + 1) * rows]
            came = jnp.concatenate([parts[2 * high][slot], parts[2 * high + 1][slot]], axis=0)
        else:
            own = mine[2 * slot + high]
            came = jnp.concatenate([part[2 * slot + high] for part in parts], axis=0)
        return own.astype(F32) + came.astype(F32)

    def size(self):
        slots, rows, width = self.own.shape
        return slots * rows // 4, width

    def cross(self):
        half, width = self.size()

        def sums(at, sources, results):
            del at
            for slot in range(2):
                results[0][slot] = self.sum_of(sources, 1, slot, 0).astype(BF)
                results[1][slot] = self.sum_of(sources, 0, slot, 0).astype(BF)
                results[2 + slot][0] = self.sum_of(sources, 0, slot, 1).astype(BF)
                results[2 + slot][1] = self.sum_of(sources, 1, slot, 1).astype(BF)

        def after(found):
            up, self.low, self.high, away = found
            self.across, self.sideways = over_y(up), over_bit(away, 0)
            return [self.across, self.sideways]

        return self.sources(), [((2, half, width), BF)] * 4, sums, after

    def turn(self):
        _, half, width = self.low.shape

        def sums(at, sources, results):
            del at
            for way in range(2):
                results[2 * way][...] = sources[2 * way][0].astype(F32) + sources[2 * way + 1][0].astype(F32)
                results[2 * way + 1][...] = (
                    sources[2 * way][1].astype(F32) + sources[2 * way + 1][1].astype(F32)
                ).astype(BF)

        def after(found):
            self.low_kept, low, self.high_kept, high = found
            self.low_came, self.high_came = over_bit(low, 0), over_y(high)
            return [self.low_came, self.high_came]

        shapes = [((half, width), F32), ((half, width), BF)] * 2
        return (self.low, self.across, self.high, self.sideways), shapes, sums, after

    def total_parts(self):
        if self.kept is None:
            inputs = (self.low_kept, self.low_came, self.high_kept, self.high_came)
            rows, width = self.low_kept.shape

            def total(sources):
                low, high = wide(sources[0]) + wide(sources[1]), wide(sources[2]) + wide(sources[3])
                return jnp.concatenate([low, high], axis=0)

            return inputs, 2 * rows, width, total

        def total(sources):
            result = wide(sources[0])
            for source in sources[1:]:
                result = result + wide(source)
            return result

        return (self.kept,) + tuple(self.came), self.kept.shape[0], self.kept.shape[1], total

    def halve(self, bit):
        inputs, rows, width, total_of = self.total_parts()
        half = rows // 2

        def sums(at, sources, results):
            total = total_of(sources)
            low, high = total[:half], total[half:]
            first = ((at >> bit) & 1) == 0
            results[0][...] = jnp.where(first, low, high)
            results[1][...] = jnp.where(first, high, low).astype(BF)

        def after(found):
            self.kept = found[0]
            self.came = (over_bit(found[1], bit),)
            return list(self.came)

        return inputs, [((half, width), F32), ((half, width), BF)], sums, after

    def whole(self):
        inputs, rows, width, total_of = self.total_parts()

        def sums(at, sources, results):
            del at
            results[0][...] = total_of(sources).astype(BF)

        return inputs, [((rows, width), BF)], sums, self.spread

    def spread(self, found):
        self.total = found[0]
        self.others = (over_bit(self.total, self.ways.pop()),)
        return list(self.others)

    def join(self, bit):
        rows, width = self.total.shape

        def sums(at, sources, results):
            first = ((at >> bit) & 1) == 0
            mine, other = sources[0][...], sources[1][...]
            results[0][:rows] = jnp.where(first, mine, other)
            results[0][rows:] = jnp.where(first, other, mine)

        return (self.total,) + self.others, [((2 * rows, width), BF)], sums, self.spread

    def tasks(self):
        bits = lax.axis_size("dp").bit_length() - 1
        self.kept = None
        calls = [self.cross, self.turn] + [partial(self.halve, bit) for bit in range(1, bits)]
        calls += [self.whole] + [partial(self.join, bit) for bit in reversed(range(1, bits))]
        self.ways = list(range(bits))
        return calls

    def result(self, bit):
        return (
            jnp.where(bit == 0, self.total, self.others[0]).astype(F32),
            jnp.where(bit == 0, self.others[0], self.total).astype(F32),
        )


class Whole(Piece):
    def over(self):
        half, width = self.size()

        def sums(at, sources, results):
            del at
            for slot in range(2):
                for high in range(2):
                    rows = slice(high * half, (high + 1) * half)
                    results[0][slot, rows] = self.sum_of(sources, 1, slot, high).astype(BF)
                    results[1][slot, rows] = self.sum_of(sources, 0, slot, high).astype(BF)

        def after(found):
            self.across, self.low = over_y(found[0]), found[1]
            return [self.across]

        return self.sources(), [((2, 2 * half, width), BF)] * 2, sums, after

    def along(self):
        def sums(at, sources, results):
            del at
            results[0][...] = (wide(sources[0]) + wide(sources[1])).astype(BF)

        def after(found):
            self.total = lax.psum(found[0], "dp")
            return []

        return (self.low, self.across), [(self.low.shape, BF)], sums, after

    def tasks(self):
        return [self.over, self.along]

    def result(self, bit):
        del bit
        return self.total[0].astype(F32), self.total[1].astype(F32)


class Small:
    def __init__(self, rows):
        self.mine, self.other = rows, over_core(rows)

    def add(self, quarter_bit, mine, other, result):
        rows, width = mine.shape
        lanes = width // 4
        if not quarter_bit:
            result[...] = mine[...] + other[...]
            return
        for base in range(0, rows, SMALL_ROWS):
            result[base : base + 6] = mine[base : base + 6] + other[base : base + 6]
            for quarter in range(4):
                own, partner = base + 6 + quarter, base + 6 + (quarter ^ quarter_bit)
                result[own : own + 1] = mine[own : own + 1] + other[partner : partner + 1]
            tail = other[base + 8 : base + SMALL_ROWS]
            if quarter_bit == 2:
                moved = pltpu.roll(tail, 2 * lanes, 1)
            else:
                lane = lax.broadcasted_iota(jnp.int32, tail.shape, 1)
                moved = jnp.where(
                    lane % (2 * lanes) < lanes, pltpu.roll(tail, 3 * lanes, 1), pltpu.roll(tail, lanes, 1)
                )
            result[base + 10 : base + SMALL_ROWS] = mine[base + 10 : base + SMALL_ROWS] + moved[2:]

    def step(self, quarter_bit, move):
        rows, width = self.mine.shape

        def sums(at, sources, results):
            del at
            self.add(quarter_bit, *sources, results[0])

        def after(found):
            self.mine = found[0]
            self.other = move(self.mine)
            return [self.other]

        return (self.mine, self.other), [((rows, width), F32)], sums, after

    def last(self):
        rows, width = self.mine.shape
        layers, lanes = rows // SMALL_ROWS, width // 4

        def sums(at, sources, results):
            del at
            self.add(2, *sources, results[9])
            total = results[9][...]
            for layer in range(layers):
                base = SMALL_ROWS * (layers - 1 - layer)
                for item in range(7):
                    results[item][layer : layer + 1] = total[base + item : base + item + 1]
                results[7][layer] = total[base + 10 : base + 13, :lanes]
                turned = total[base + 13 : base + 15, :lanes]
                results[8][layer] = jnp.concatenate(
                    [
                        turned[:, at : at + HALF] + turned[:, at + HALF : at + HEAD_DIM]
                        for at in range(0, lanes, HEAD_DIM)
                    ],
                    axis=1,
                )

        def after(found):
            self.found = found
            return []

        shapes = [((layers, width), F32)] * 7 + [((layers, 3, lanes), F32), ((layers, 2, lanes // 2), F32)]
        shapes.append(((rows, width), F32))
        return (self.mine, self.other), shapes, sums, after

    def tasks(self):
        bits = lax.axis_size("dp").bit_length() - 1
        moves = [partial(over_bit, bit=bit) for bit in (*range(1, bits), 0)] + [over_y]
        quarters = [1] + [0] * bits
        return [partial(self.step, *item) for item in zip(quarters, moves)] + [self.last]


def attention_outputs(x_bit, pieces):
    _, width = pieces[0].total.shape
    inner = pieces[0].total.shape[0] // 2
    layers = len(pieces)

    def body(numbers, inputs, _, results, __):
        for layer in reversed(range(layers)):
            mine, other = inputs[2 * layer : 2 * layer + 2]
            first = jnp.where(numbers[0] == 0, mine[...], other[...]).astype(F32)
            second = jnp.where(numbers[0] == 0, other[...], mine[...]).astype(F32)
            results[0][layer, 0] = first[:inner]
            results[0][layer, 1] = first[inner:]
            results[0][layer, 2] = second[:inner]
            results[0].leave(layer)
            results[1][layer] = second[inner:]
            results[1].leave(layer)

    items = [item for piece in pieces for item in (piece.total, piece.others[0])]
    return staged(
        body, "attention_outputs", 0, x_bit, items, (),
        (jax.ShapeDtypeStruct((layers, 3, inner, width), F32), jax.ShapeDtypeStruct((layers, inner, width), F32)),
    )


def over_bits(values, mask):
    size = lax.axis_size("dp")
    return lax.ppermute(values, "dp", [(at, at ^ mask) for at in range(size)])


def over_both(values):
    return lax.ppermute(values, "tensor", [(at, at ^ 3) for at in range(4)])


class FarFetch:
    def __init__(self, half):
        self.mine = over_y(half)

    def turn(self, hold):
        self.mine, _ = lax.optimization_barrier((self.mine, hold))
        self.other = over_bit(self.mine, 0)
        self.mine_core = over_core(self.mine)

    def end(self, hold):
        self.other, _ = lax.optimization_barrier((self.other, hold))
        self.found = (self.mine, self.other, self.mine_core, over_core(self.other))


def body(
    tokens,
    out_grad,
    image_lengths,
    norm1_gain,
    norm1_bias,
    qkv_weight,
    qkv_bias,
    rope_freqs,
    out_weight,
    out_bias,
    norm2_gain,
    norm2_bias,
    up_weight,
    up_bias,
    down_weight,
    down_bias,
):
    count, width = tokens.shape
    inner = qkv_weight.shape[3]
    heads = inner // HEAD_DIM
    me = lax.axis_index("tensor")
    xbit = lax.axis_index("dp") & 1
    x_bit = jnp.stack([xbit, xbit]).astype(jnp.int32)
    x_bit_plain = jnp.stack([xbit, jnp.zeros_like(xbit)]).astype(jnp.int32)

    small = jnp.concatenate(
        [qkv_bias.reshape(LAYERS, -1), rope_freqs.reshape(LAYERS, -1), up_bias], axis=1
    )
    near_small, far_small = (small, over_core(small)), (over_y(small), over_both(small))

    lengths = lax.dynamic_index_in_dim(image_lengths, me // 2, 0, keepdims=False)
    half_at = me % 2
    position = jnp.arange(count, dtype=jnp.int32)
    segment, row_at, column_at = places_at(lengths, position + half_at * count)
    segment_other, _, _ = places_at(lengths, position + (1 - half_at) * count)
    here_segment = segment[:, None].astype(F32)
    all_segments = jnp.concatenate([segment, segment_other])[None, :].astype(F32)
    places = jnp.stack([row_at, column_at], axis=1).astype(F32)

    qkv_turned = jnp.swapaxes(qkv_weight, 2, 3)
    near_att, far_att, near_mlp, far_mlp = [], [], [], []

    def fetch_att(layer, gates=()):
        packed, half = pack(layer, x_bit, qkv_turned, out_weight[:, None], 2, gates)
        near_att.append((packed, over_core(packed)))
        far_att.append(FarFetch(half))

    def fetch_mlp(layer, gates=()):
        both, half = pack(layer, x_bit, up_weight[:, None], down_weight[:, None], 1, gates)
        near_mlp.append((both, over_core(both)))
        far_mlp.append(FarFetch(half[0]))

    current = tokens
    kept_layers = []
    cosines, sines = [[] for _ in range(LAYERS)], [[] for _ in range(LAYERS)]
    before = ()
    fetch_att(0)
    for l in range(LAYERS):
        inputs = current
        gain, shift = norm1_gain[l : l + 1], norm1_bias[l : l + 1]
        queries, keeps, comes, mixes, spreads, exps = [], [], [], [], [], []

        def project(side, source, weights):
            nonlocal before
            found = qkv_part(
                side == 0, l, x_bit, source, gain, shift, (near_small, far_small)[side], places, weights, before
            )
            before = (found[0],)
            queries.append(found[0])
            keeps.append(found[1])
            comes.append(over_core(found[2]))
            cosines[l].append(found[3])
            sines[l].append(found[4])
            return found

        def mix(side):
            nonlocal before
            found = attend(queries[side], keeps[side], comes[side], here_segment, all_segments, x_bit, before)
            before = (found[0],)
            mixes.append(found[0])
            spreads.append(found[1])
            exps.append(found[2])

        normed = project(0, inputs, near_att[l])[5]
        if l:
            far_mlp[l].turn(queries[0])
        if l == 0:
            fetch_mlp(0, before + far_small)
            before = (near_mlp[0][0],)
            far_att[0].turn(near_mlp[0][0])
            mix(0)
            fetch_att(1, before)
            before = (near_att[1][0],)
            far_att[0].end(mixes[0])
            far_mlp[0].turn(mixes[0])
            project(1, normed, far_att[0].found)
            mix(1)
            fetch_mlp(1, before)
            before = (near_mlp[1][0],)
            far_att[1].turn(mixes[1])
            far_mlp[0].end(mixes[1])
        else:
            project(1, normed, far_att[l].found)
            mix(0)
            mix(1)
            far_mlp[l].end(mixes[1])
        middle, normed_mlp, active_near, slope_near, total = mlp_near(
            l, x_bit, inputs, mixes[0], mixes[1], out_bias[l : l + 1], norm2_gain[l : l + 1], norm2_bias[l : l + 1],
            near_small, down_bias[l : l + 1], near_att[l] + far_att[l].found, near_mlp[l], before,
        )
        active_far, slope_far, current = mlp_far(
            l, x_bit, normed_mlp, total, far_small, far_mlp[l].found, BF if l == LAYERS - 1 else F32
        )
        before = (current,)
        if l == 0:
            far_att[1].end(middle)
        kept_layers.append(
            (inputs, normed, queries, keeps, comes, mixes, spreads, exps, middle, normed_mlp, (active_near, active_far), (slope_near, slope_far))
        )
    activations = current

    gradient = out_grad
    small_rows = []
    summed = [None] * LAYERS
    waiting = []
    todo = []
    clock = 0
    latest = []
    here = lax.axis_index("dp").reshape(1).astype(jnp.int32)

    def ran(found):
        latest[:] = found[:1]
        return found

    def wait_until(arrays, when):
        waiting.append((when, arrays))

    def gates_now():
        nonlocal clock
        clock += 1
        due = [array for when, arrays in waiting if when <= clock for array in arrays]
        waiting[:] = [item for item in waiting if item[0] > clock]
        turn = [entry for entry in todo if entry[0] == clock]
        todo[:] = [entry for entry in todo if entry[0] != clock]
        if not turn:
            return due + latest
        tasks = [step() for _, _, step in turn]
        found = run_tasks(here, [task[:3] for task in tasks], due + latest)
        for (_, length, _), task, given in zip(turn, tasks, found):
            wait_until(task[3](given), clock + length)
        latest[:] = found[0][:1]
        return latest

    def plan(piece, base, table):
        start, length = 0, 1
        for at, step in enumerate(piece.tasks()):
            start, length = table[at] if at < len(table) else (start + length, 1)
            todo.append((base + start, length, step))

    for l in reversed(range(LAYERS)):
        (inputs, normed, queries, keeps, comes, mixes, spreads, exps, middle, normed_mlp, active, slope) = kept_layers[l]
        att = (near_att[l], far_att[l].found)
        pieces = [Piece(), Piece()]
        tables = PLANS[l > 0]
        for piece, table in zip(pieces, tables):
            plan(piece, clock, table)
        found, rest = mlp_back(
            x_bit, gradient, normed_mlp, middle, norm2_gain[l : l + 1], active, slope, near_mlp[l],
            far_mlp[l].found, gates_now(),
        )
        ran(rest)
        up_bias_grad, sums2, grad_middle, incoming = rest
        wait_until(pieces[0].begin(found), clock + tables[0][0][0] - 1)
        backs = attend_back(
            x_bit, incoming,
            [(queries[side], keeps[side], comes[side], mixes[side], spreads[side], exps[side]) for side in range(2)],
            *att, gates_now(),
        )
        ran(backs[0])
        sides = [
            (back[0], back[1], over_core(back[2]), over_core(back[3]), queries[side], keeps[side], cosines[l][side], sines[l][side], mixes[side])
            for side, back in enumerate(backs)
        ]
        found, rest = qkv_back(
            x_bit, normed, incoming, places, sides, *att, norm1_gain[l : l + 1], inputs, grad_middle,
            [sums2, up_bias_grad] + small_rows, gates_now(),
        )
        ran(rest)
        rows, gradient = rest
        small_rows = [rows]
        wait_until(pieces[1].begin(found), clock + tables[1][0][0] - 3)
        summed[l] = pieces

    little = Small(small_rows[0])
    wait_until([little.other], clock + SMALL_PLAN[0][0])
    plan(little, clock, SMALL_PLAN)
    while todo:
        gates_now()
    gain1, shift1, bias_out, gain2, shift2, bias_down, bias_up, bias_qkv, turns = little.found[:9]
    grad_qkv, grad_out = attention_outputs(x_bit, [summed[l][1] for l in range(LAYERS)])
    grad_up, grad_down = zip(*(summed[l][0].result(xbit) for l in range(LAYERS)))
    return (
        activations,
        gradient,
        gain1,
        shift1,
        jnp.swapaxes(grad_qkv, 2, 3),
        bias_qkv,
        turns,
        grad_out,
        bias_out,
        gain2,
        shift2,
        jnp.stack(grad_up),
        bias_up,
        jnp.stack(grad_down),
        bias_down,
    )


def solution(mesh):
    in_specs = (
        P(("dp", "tensor"), None),
        P(("dp", "tensor"), None),
        P("dp", None),
        P(),
        P(),
        P(None, None, None, "tensor"),
        P(None, None, "tensor"),
        P(None, None, "tensor"),
        P(None, "tensor", None),
        P(),
        P(),
        P(),
        P(None, None, "tensor"),
        P(None, "tensor"),
        P(None, "tensor", None),
        P(),
    )
    out_specs = (
        P(("dp", "tensor"), None),
        P(("dp", "tensor"), None),
        P(),
        P(),
        P(None, None, None, "tensor"),
        P(None, None, "tensor"),
        P(None, None, "tensor"),
        P(None, "tensor", None),
        P(),
        P(),
        P(),
        P(None, None, "tensor"),
        P(None, "tensor"),
        P(None, "tensor", None),
        P(),
    )
    return jax.shard_map(body, mesh=mesh, in_specs=in_specs, out_specs=out_specs, check_vma=False)
```

time: 816 us -> 621 us (0.76)
  Pallas kernels: 0 us -> 291 us
  matrix products: 197 us -> 0 us
  other arithmetic: 111 us -> 8.08 us
  local copies, waits for them, and re-layouts: 118 us -> 27.6 us
  waiting for transfers between devices: 279 us -> 210 us
  starting transfers between devices: 91.8 us -> 73.6 us
    pallas_call x0 -> x33, Pallas kernels: none -> 291 us  [staged(): pl.pallas_call(kernel, out_shape=list(outs) + list(raw_outs), in_specs=[S...]
    dot_general x192 -> x0, matrix products: 197 us -> none  [the longest x48 60.4 us: mm_tn(): lax.dot_general(left, right, (((0,), (0,)), ((), ())), preferred_element_...]
    ppermute x18 -> x14, waiting for transfers between devices: 153 us -> 22.6 us  [over_y(): return lax.ppermute(values, 'tensor', ACROSS)]
    ppermute x51 -> x35, waiting for transfers between devices: 123 us -> 175 us  [over_bit(): lax.ppermute(values, 'dp', [(at, at ^ 1 << bit) for at in range(size)])]
    reduce_sum x37 -> x0, other arithmetic: 33.7 us -> none  [the longest x20 14.4 us: body(): jnp.sum(item.astype(F32), axis=0)]
    reduce_sum x24 -> x0, local copies, waits for them, and re-layouts: 24.8 us -> none  [body(): jnp.sum(item.astype(F32), axis=0)]
    slice x25 -> x4, local copies, waits for them, and re-layouts: 22 us -> 2.39 us  [the longest x1 0.61 us: body(): down_bias[l:l + 1]]
    concatenate x31 -> x0, other arithmetic: 19 us -> none  [the longest x24 13.6 us: reduce_weight(): jnp.concatenate([jnp.where(mine, total, other), jnp.where(mine, other, to...]
  transfers between devices with their start and end apart: 112 -> 108, of which waited for: 43 -> 35; matrix products, arithmetic and copies ran while one was open for 45% -> 1% of each run, Pallas kernels for 0% -> 36%
where the time goes in v2:
time: 621 us; the launch traced here: 612 us
  Pallas kernels  291 us (47%)
  waiting for transfers between devices  210 us (34%)
  starting transfers between devices  73.6 us (12%)
  local copies, waits for them, and re-layouts  27.6 us (4%)
  other arithmetic  8.08 us (1%)
    pallas_call x33, Pallas kernels, staged(): pl.pallas_call(kernel, out_shape=list(outs) + list(raw_outs), in_specs=[S...  291 us
    ppermute x35, waiting for transfers between devices, over_bit(): lax.ppermute(values, 'dp', [(at, at ^ 1 << bit) for at in range(size)])  175 us
    ppermute x35, starting transfers between devices, over_bit(): lax.ppermute(values, 'dp', [(at, at ^ 1 << bit) for at in range(size)])  44.3 us
    unnamed x226, local copies, waits for them, and re-layouts  22.6 us
    ppermute x14, waiting for transfers between devices, over_y(): return lax.ppermute(values, 'tensor', ACROSS)  22.6 us
    ppermute x58, starting transfers between devices, over_core(): return lax.ppermute(values, 'tensor', CORE)  13.6 us
    ppermute x14, starting transfers between devices, over_y(): return lax.ppermute(values, 'tensor', ACROSS)  13.3 us
  transfers between devices with their start and end apart: 108, of which 35 were waited for; matrix products, arithmetic and copies ran while one was open for 1% of the time, Pallas kernels for 36%

profile of v2, /device:TPU:0, one launch (start us, length us, event | category | flops | bytes accessed | tf_op | source)
XLA Modules:
  0.0 612.0 jit_solution(8574316864834896563)
XLA Ops:
  15.9 7.4 %qkv_near.2 = (bf16[416,384]{1,0:T(8,128)(2,1)}, bf16[2,416,384]{2,1,0:T(8,128)(2,1)}, bf16[2,416,384]{2,1,0:T(8,128)(2,1)}, f32[416,384]{1,0:T(8,128)}, f32[416,384]{1,0:T(8,128)}, /*index=5*/bf16[416,768]{1,0:T(8,128)(2,1)}) custom-call(s32[2]{0:T(128)} %pad_add_fusion.1.numbers, f32[1,768]{1,0:T(1,128)} %get-tuple-element.520.refs_0_.refs_21_, ...), custom_call_target="tpu_custom_call" | custom-call | flops 92012544 | bytes 1048576 | tf_op jit(solution)/shard_map/qkv_near/pallas_call | solution.py:185
  34.5 8.3 %attend.4 = (bf16[416,384]{1,0:T(8,128)(2,1)}, f32[416,384]{1,0:T(8,128)}, bf16[6,416,832]{2,1,0:T(8,128)(2,1)}) custom-call(s32[2]{0:T(128)} %pad_add_fusion.1.numbers, bf16[416,384]{1,0:T(8,128)(2,1)} %get-tuple-element.225.refs_2_.refs_0_.refs_5_, bf16[2,416,384]{2,1,0:T(8,128)(2,1)} %get-tuple-element.226.refs_1_.refs_3_.refs_9_, ...), custom_call_target="tpu_custom_call" | custom-call | flops 122683392 | bytes 1048576 | tf_op jit(solution)/shard_map/attend/pallas_call | solution.py:185
  44.5 12.2 %collective-permute-done.11.refs_4_.refs_10_ = bf16[768,768]{1,0:T(8,128)(2,1)} collective-permute-done((bf16[768,768]{1,0:T(8,128)(2,1)}, bf16[768,768]{1,0:T(8,128)(2,1)}, u32[]{:S(2)}, u32[]{:S(2)}) %collective-permute-start.11) | collective-permute-done | bytes 1179680 | tf_op jit(solution)/shard_map/ppermute | solution.py:32
  62.5 7.7 %qkv_far.2 = (bf16[416,384]{1,0:T(8,128)(2,1)}, bf16[2,416,384]{2,1,0:T(8,128)(2,1)}, bf16[2,416,384]{2,1,0:T(8,128)(2,1)}, f32[416,384]{1,0:T(8,128)}, f32[416,384]{1,0:T(8,128)}) custom-call(s32[2]{0:T(128)} %pad_add_fusion.1.numbers, f32[1,768]{1,0:T(1,128)} %get-tuple-element.520.refs_0_.refs_21_, f32[1,768]{1,0:T(1,128)} %get-tuple-element.509.refs_1_, ...), custom_call_target="tpu_custom_call" | custom-call | flops 92012544 | bytes 1048576 | tf_op jit(solution)/shard_map/qkv_far/pallas_call | solution.py:185
  73.4 8.2 %attend.5 = (bf16[416,384]{1,0:T(8,128)(2,1)}, f32[416,384]{1,0:T(8,128)}, bf16[6,416,832]{2,1,0:T(8,128)(2,1)}) custom-call(s32[2]{0:T(128)} %pad_add_fusion.1.numbers, bf16[416,384]{1,0:T(8,128)(2,1)} %get-tuple-element.235.refs_0_.refs_5_.refs_11_.refs_14_, bf16[2,416,384]{2,1,0:T(8,128)(2,1)} %get-tuple-element.236.refs_1_.refs_9_.refs_18_, ...), custom_call_target="tpu_custom_call" | custom-call | flops 122683392 | bytes 1048576 | tf_op jit(solution)/shard_map/attend/pallas_call | solution.py:185
  92.8 11.3 %mlp_near.2 = (f32[416,768]{1,0:T(8,128)}, bf16[416,768]{1,0:T(8,128)(2,1)}, bf16[2,416,768]{2,1,0:T(8,128)(2,1)}, bf16[2,416,768]{2,1,0:T(8,128)(2,1)}, f32[416,768]{1,0:T(8,128)}) custom-call(s32[2]{0:T(128)} %pad_add_fusion.1.numbers, bf16[416,384]{1,0:T(8,128)(2,1)} %get-tuple-element.229.refs_2_.refs_0_.refs_1_.refs_3_, ...), custom_call_target="tpu_custom_call" | custom-call | flops 306708480 | bytes 1048576 | tf_op jit(solution)/shard_map/mlp_near/pallas_call | solution.py:185
  105.0 8.8 %mlp_far.2 = (bf16[2,416,768]{2,1,0:T(8,128)(2,1)}, bf16[2,416,768]{2,1,0:T(8,128)(2,1)}, f32[416,768]{1,0:T(8,128)}) custom-call(s32[2]{0:T(128)} %pad_add_fusion.1.numbers, bf16[416,768]{1,0:T(8,128)(2,1)} %get-tuple-element.240.refs_0_.refs_3_, f32[2,1536]{1,0:T(2,128)} %copy-done.99, f32[2,1536]{1,0:T(2,128)} %copy-done.98, ...), custom_call_target="tpu_custom_call" | custom-call | flops 245366784 | bytes 1048576 | tf_op jit(solution)/shard_map/mlp_far/pallas_call | solution.py:185
  114.8 7.4 %qkv_near.3 = (bf16[416,384]{1,0:T(8,128)(2,1)}, bf16[2,416,384]{2,1,0:T(8,128)(2,1)}, bf16[2,416,384]{2,1,0:T(8,128)(2,1)}, f32[416,384]{1,0:T(8,128)}, f32[416,384]{1,0:T(8,128)}, /*index=5*/bf16[416,768]{1,0:T(8,128)(2,1)}) custom-call(s32[2]{0:T(128)} %pad_add_fusion.1.numbers, f32[1,768]{1,0:T(1,128)} %get-tuple-element.519.refs_0_.refs_21_, ...), custom_call_target="tpu_custom_call" | custom-call | flops 92012544 | bytes 1048576 | tf_op jit(solution)/shard_map/qkv_near/pallas_call | solution.py:185
  124.0 7.3 %qkv_far.3 = (bf16[416,384]{1,0:T(8,128)(2,1)}, bf16[2,416,384]{2,1,0:T(8,128)(2,1)}, bf16[2,416,384]{2,1,0:T(8,128)(2,1)}, f32[416,384]{1,0:T(8,128)}, f32[416,384]{1,0:T(8,128)}) custom-call(s32[2]{0:T(128)} %pad_add_fusion.1.numbers, f32[1,768]{1,0:T(1,128)} %get-tuple-element.519.refs_0_.refs_21_, f32[1,768]{1,0:T(1,128)} %get-tuple-element.510.refs_1_, ...), custom_call_target="tpu_custom_call" | custom-call | flops 92012544 | bytes 1048576 | tf_op jit(solution)/shard_map/qkv_far/pallas_call | solution.py:185
  132.0 8.2 %attend.6 = (bf16[416,384]{1,0:T(8,128)(2,1)}, f32[416,384]{1,0:T(8,128)}, bf16[6,416,832]{2,1,0:T(8,128)(2,1)}) custom-call(s32[2]{0:T(128)} %pad_add_fusion.1.numbers, bf16[416,384]{1,0:T(8,128)(2,1)} %get-tuple-element.246.refs_10_.refs_0_.refs_5_, bf16[2,416,384]{2,1,0:T(8,128)(2,1)} %get-tuple-element.247.refs_1_.refs_3_.refs_9_, ...), custom_call_target="tpu_custom_call" | custom-call | flops 122683392 | bytes 1048576 | tf_op jit(solution)/shard_map/attend/pallas_call | solution.py:185
  141.1 8.6 %attend.7 = (bf16[416,384]{1,0:T(8,128)(2,1)}, f32[416,384]{1,0:T(8,128)}, bf16[6,416,832]{2,1,0:T(8,128)(2,1)}) custom-call(s32[2]{0:T(128)} %pad_add_fusion.1.numbers, bf16[416,384]{1,0:T(8,128)(2,1)} %get-tuple-element.254.refs_5_.refs_0_.refs_11_.refs_14_, bf16[2,416,384]{2,1,0:T(8,128)(2,1)} %get-tuple-element.256.refs_1_.refs_9_.refs_18_, ...), custom_call_target="tpu_custom_call" | custom-call | flops 122683392 | bytes 1048576 | tf_op jit(solution)/shard_map/attend/pallas_call | solution.py:185
  150.8 11.1 %mlp_near.3 = (f32[416,768]{1,0:T(8,128)}, bf16[416,768]{1,0:T(8,128)(2,1)}, bf16[2,416,768]{2,1,0:T(8,128)(2,1)}, bf16[2,416,768]{2,1,0:T(8,128)(2,1)}, f32[416,768]{1,0:T(8,128)}) custom-call(s32[2]{0:T(128)} %pad_add_fusion.1.numbers, bf16[416,384]{1,0:T(8,128)(2,1)} %get-tuple-element.255.refs_5_.refs_0_.refs_1_.refs_3_, ...), custom_call_target="tpu_custom_call" | custom-call | flops 306708480 | bytes 1048576 | tf_op jit(solution)/shard_map/mlp_near/pallas_call | solution.py:185
  163.3 8.5 %mlp_far.3 = (bf16[2,416,768]{2,1,0:T(8,128)(2,1)}, bf16[2,416,768]{2,1,0:T(8,128)(2,1)}, bf16[416,768]{1,0:T(8,128)(2,1)}) custom-call(s32[2]{0:T(128)} %pad_add_fusion.1.numbers, bf16[416,768]{1,0:T(8,128)(2,1)} %get-tuple-element.259.refs_0_.refs_3_, f32[2,1536]{1,0:T(2,128)} %copy-done.99, f32[2,1536]{1,0:T(2,128)} %copy-done.98, ...), custom_call_target="tpu_custom_call" | custom-call | flops 245366784 | bytes 1048576 | tf_op jit(solution)/shard_map/mlp_far/pallas_call | solution.py:185
  171.8 19.5 %mlp_back.2 = (f32[4,768]{1,0:T(4,128)}, f32[4,768]{1,0:T(4,128)}, f32[416,768]{1,0:T(8,128)}, bf16[416,768]{1,0:T(8,128)(2,1)}, bf16[2,768,768]{2,1,0:T(8,128)(...) custom-call(s32[2]{0:T(128)} %pad_add_fusion.1.numbers, ...), custom_call_target="tpu_custom_call" | custom-call | flops 981467136 | bytes 1048576 | tf_op jit(solution)/shard_map/mlp_back/pallas_call | solution.py:185
  195.8 19.2 %attend_back.2 = (bf16[416,384]{1,0:T(8,128)(2,1)}, bf16[2,416,384]{2,1,0:T(8,128)(2,1)}, bf16[416,384]{1,0:T(8,128)(2,1)}, bf16[416,384]{1,0:T(8,128)(2,1)}, bf...) custom-call(s32[2]{0:T(128)} %pad_add_fusion.1.numbers, ...), custom_call_target="tpu_custom_call" | custom-call | flops 490733568 | bytes 1048576 | tf_op jit(solution)/shard_map/attend_back/pallas_call | solution.py:185
  224.5 17.3 %qkv_back.2 = (f32[16,768]{1,0:T(8,128)}, f32[416,768]{1,0:T(8,128)}, bf16[4,192,768]{2,1,0:T(8,128)(2,1)}, bf16[4,48,768]{2,1,0:T(8,128)(2,1)}, bf16[4,48,768]{...) custom-call(s32[2]{0:T(128)} %pad_add_fusion.1.numbers, ...), custom_call_target="tpu_custom_call" | custom-call | flops 490733568 | bytes 1048576 | tf_op jit(solution)/shard_map/qkv_back/pallas_call | solution.py:185
  247.7 20.3 %mlp_back.3 = (f32[4,768]{1,0:T(4,128)}, f32[4,768]{1,0:T(4,128)}, f32[416,768]{1,0:T(8,128)}, bf16[416,768]{1,0:T(8,128)(2,1)}, bf16[2,768,768]{2,1,0:T(8,128)(...) custom-call(s32[2]{0:T(128)} %pad_add_fusion.1.numbers, ...), custom_call_target="tpu_custom_call" | custom-call | flops 981467136 | bytes 1048576 | tf_op jit(solution)/shard_map/mlp_back/pallas_call | solution.py:185
  273.8 6.8 %sums.11 = (f32[384,768]{1,0:T(8,128)}, bf16[384,768]{1,0:T(8,128)(2,1)}, f32[384,768]{1,0:T(8,128)}, bf16[384,768]{1,0:T(8,128)(2,1)}, bf16[2,192,768]{2,1,0:T(...) custom-call(s32[1]{0:T(128)} %bitcast.17.numbers, ...), custom_call_target="tpu_custom_call" | custom-call | bytes 1048576 | tf_op jit(solution)/shard_map/sums/pallas_call | solution.py:185
  285.0 19.2 %attend_back.3 = (bf16[416,384]{1,0:T(8,128)(2,1)}, bf16[2,416,384]{2,1,0:T(8,128)(2,1)}, bf16[416,384]{1,0:T(8,128)(2,1)}, bf16[416,384]{1,0:T(8,128)(2,1)}, bf...) custom-call(s32[2]{0:T(128)} %pad_add_fusion.1.numbers, ...), custom_call_target="tpu_custom_call" | custom-call | flops 490733568 | bytes 1048576 | tf_op jit(solution)/shard_map/attend_back/pallas_call | solution.py:185
  310.6 9.5 %sums.12 = (f32[384,768]{1,0:T(8,128)}, bf16[384,768]{1,0:T(8,128)(2,1)}, f32[192,768]{1,0:T(8,128)}, bf16[192,768]{1,0:T(8,128)(2,1)}, f32[192,768]{1,0:T(8,128...) custom-call(s32[1]{0:T(128)} %bitcast.17.numbers, ...), custom_call_target="tpu_custom_call" | custom-call | bytes 1048576 | tf_op jit(solution)/shard_map/sums/pallas_call | solution.py:185
  323.8 18.7 %qkv_back.3 = (f32[32,768]{1,0:T(8,128)}, f32[416,768]{1,0:T(8,128)}, bf16[4,192,768]{2,1,0:T(8,128)(2,1)}, bf16[4,48,768]{2,1,0:T(8,128)(2,1)}, bf16[4,48,768]{...) custom-call(s32[2]{0:T(128)} %pad_add_fusion.1.numbers, ...), custom_call_target="tpu_custom_call" | custom-call | flops 490733568 | bytes 1048576 | tf_op jit(solution)/shard_map/qkv_back/pallas_call | solution.py:185
  351.5 10.3 %collective-permute-done.65.refs_1_.refs_18_ = bf16[384,768]{1,0:T(8,128)(2,1)S(1)} collective-permute-done((bf16[384,768]{1,0:T(8,128)(2,1)}, bf16[384,768]{1,0:T(8,128)(2,1)S(1)}, u32[]{:S(2)}, u32[]{:S(2)}) %collective-permute-start.65) | collective-permute-done | bytes 589856 | tf_op jit(solution)/shard_map/ppermute | solution.py:37
  375.7 10.5 %collective-permute-done.77.refs_1_.refs_16_ = bf16[192,768]{1,0:T(8,128)(2,1)S(1)} collective-permute-done((bf16[192,768]{1,0:T(8,128)(2,1)}, bf16[192,768]{1,0:T(8,128)(2,1)S(1)}, u32[]{:S(2)}, u32[]{:S(2)}) %collective-permute-start.77) | collective-permute-done | bytes 294944 | tf_op jit(solution)/shard_map/ppermute | solution.py:37
  386.2 8.1 %collective-permute-done.78.refs_3_.refs_17_ = bf16[192,768]{1,0:T(8,128)(2,1)S(1)} collective-permute-done((bf16[192,768]{1,0:T(8,128)(2,1)}, bf16[192,768]{1,0:T(8,128)(2,1)S(1)}, u32[]{:S(2)}, u32[]{:S(2)}) %collective-permute-start.78) | collective-permute-done | bytes 294944 | tf_op jit(solution)/shard_map/ppermute | solution.py:37
  396.1 7.0 %sums.14 = (bf16[192,768]{1,0:T(8,128)(2,1)}, f32[96,768]{1,0:T(8,128)}, bf16[96,768]{1,0:T(8,128)(2,1)}, f32[384,768]{1,0:T(8,128)}, bf16[384,768]{1,0:T(8,128)...) custom-call(s32[1]{0:T(128)} %bitcast.17.numbers, ...), custom_call_target="tpu_custom_call" | custom-call | bytes 1048576 | tf_op jit(solution)/shard_map/sums/pallas_call | solution.py:185
  409.1 7.3 %collective-permute-done.90.refs_13_.refs_20_ = f32[32,768]{1,0:T(8,128)S(1)} collective-permute-done((f32[32,768]{1,0:T(8,128)}, f32[32,768]{1,0:T(8,128)S(1)}, u32[]{:S(2)}, u32[]{:S(2)}) %collective-permute-start.90) | collective-permute-done | bytes 98336 | tf_op jit(solution)/shard_map/ppermute | solution.py:37
  424.9 7.0 %collective-permute-done.84.refs_1_.refs_14_ = bf16[192,768]{1,0:T(8,128)(2,1)S(1)} collective-permute-done((bf16[192,768]{1,0:T(8,128)(2,1)}, bf16[192,768]{1,0:T(8,128)(2,1)S(1)}, u32[]{:S(2)}, u32[]{:S(2)}) %collective-permute-start.84) | collective-permute-done | bytes 294944 | tf_op jit(solution)/shard_map/ppermute | solution.py:37
  448.0 25.7 %collective-permute-done.92.refs_3_.refs_11_ = bf16[96,768]{1,0:T(8,128)(2,1)S(1)} collective-permute-done((bf16[96,768]{1,0:T(8,128)(2,1)}, bf16[96,768]{1,0:T(8,128)(2,1)S(1)}, u32[]{:S(2)}, u32[]{:S(2)}) %collective-permute-start.92) | collective-permute-done | bytes 147488 | tf_op jit(solution)/shard_map/ppermute | solution.py:37
  491.6 12.6 %collective-permute-done.98.refs_5_.refs_11_ = bf16[96,768]{1,0:T(8,128)(2,1)S(1)} collective-permute-done((bf16[96,768]{1,0:T(8,128)(2,1)}, bf16[96,768]{1,0:T(8,128)(2,1)S(1)}, u32[]{:S(2)}, u32[]{:S(2)}) %collective-permute-start.98) | collective-permute-done | bytes 147488 | tf_op jit(solution)/shard_map/ppermute | solution.py:37
  517.1 17.7 %collective-permute-done.102.refs_3_.refs_6_ = bf16[96,768]{1,0:T(8,128)(2,1)S(1)} collective-permute-done((bf16[96,768]{1,0:T(8,128)(2,1)}, bf16[96,768]{1,0:T(8,128)(2,1)S(1)}, u32[]{:S(2)}, u32[]{:S(2)}) %collective-permute-start.102) | collective-permute-done | bytes 147488 | tf_op jit(solution)/shard_map/ppermute | solution.py:37
  540.7 18.4 %collective-permute-done.105.refs_3_.refs_5_ = bf16[192,768]{1,0:T(8,128)(2,1)S(1)} collective-permute-done((bf16[192,768]{1,0:T(8,128)(2,1)}, bf16[192,768]{1,0:T(8,128)(2,1)S(1)}, u32[]{:S(2)}, u32[]{:S(2)}) %collective-permute-start.105) | collective-permute-done | bytes 294944 | tf_op jit(solution)/shard_map/ppermute | solution.py:37
  566.2 35.7 %collective-permute-done.106.refs_1_ = bf16[384,768]{1,0:T(8,128)(2,1)} collective-permute-done((bf16[384,768]{1,0:T(8,128)(2,1)}, bf16[384,768]{1,0:T(8,128)(2,1)}, u32[]{:S(2)}, u32[]{:S(2)}) %collective-permute-start.106) | collective-permute-done | bytes 589856 | tf_op jit(solution)/shard_map/ppermute | solution.py:37
  (470 shorter events, 203.9 us)
Async XLA Ops:
  28.3 28.4 %collective-permute-start.11 = (bf16[768,768]{1,0:T(8,128)(2,1)}, bf16[768,768]{1,0:T(8,128)(2,1)}, u32[]{:S(2)}, u32[]{:S(2)}) collective-permute-start(bf16[768,768]{1,0:T(8,128)(2,1)} %bitcast.49), channel_id=1, source_target_pairs={{0,2},{2,0},{1,3},{3,1},{4,6},{6,4},{5,7},{7,5},{8,10},{10,8},{9,1... | collective-permute-start | bytes 3538952 | tf_op jit(solution)/shard_map/ppermute | solution.py:32
  28.6 60.7 %collective-permute-start.10 = (bf16[2,768,768]{2,1,0:T(8,128)(2,1)}, bf16[2,768,768]{2,1,0:T(8,128)(2,1)}, u32[]{:S(2)}, u32[]{:S(2)}) collective-permute-start(bf16[2,768,768]{2,1,0:T(8,128)(2,1)} %get-tuple-element.228.refs_5_.refs_15_.refs_8_), channel_id=1, source_target_pairs={{0,1},{1,0},{2,3},{3,2},{4,5},{5,4},{6,7},{7,6},{8,9},{9,8},{10,11... | collective-permute-start | bytes 7077896 | tf_op jit(solution)/shard_map/ppermute | solution.py:28
  32.3 29.1 %collective-permute-start.7 = (bf16[2,192,768]{2,1,0:T(8,128)(2,1)S(1)}, bf16[2,192,768]{2,1,0:T(8,128)(2,1)S(1)}, u32[]{:S(2)}, u32[]{:S(2)}) collective-permute-start(bf16[2,192,768]{2,1,0:T(8,128)(2,1)S(1)} %collective-permute-done.5.refs_6_.refs_11_.refs_15_.refs_29_), channel_id=1, source_target_pairs={{0,1},{1,0},{2,3},{3,2},{4,5},{5,4},{6,7},{7,6},{8,9},{9,8},{10,11... | collective-permute-start | bytes 1769480 | tf_op jit(solution)/shard_map/ppermute | solution.py:28
  56.7 27.5 %collective-permute-start.12 = (bf16[768,768]{1,0:T(8,128)(2,1)}, bf16[768,768]{1,0:T(8,128)(2,1)}, u32[]{:S(2)}, u32[]{:S(2)}) collective-permute-start(bf16[768,768]{1,0:T(8,128)(2,1)} %collective-permute-done.11.refs_4_.refs_10_), channel_id=1, source_target_pairs={{0,4},{4,0},{8,12},{12,8},{16,20},{20,16},{24,28},{28,24},{1,5},{5... | collective-permute-start | bytes 3538952 | tf_op jit(solution)/shard_map/ppermute | solution.py:37
  70.9 33.5 %collective-permute-start.13 = (bf16[768,768]{1,0:T(8,128)(2,1)}, bf16[768,768]{1,0:T(8,128)(2,1)}, u32[]{:S(2)}, u32[]{:S(2)}) collective-permute-start(bf16[768,768]{1,0:T(8,128)(2,1)} %collective-permute-done.11.refs_4_.refs_10_), channel_id=1, source_target_pairs={{0,1},{1,0},{2,3},{3,2},{4,5},{5,4},{6,7},{7,6},{8,9},{9,8},{10,11... | collective-permute-start | bytes 3538952 | tf_op jit(solution)/shard_map/ppermute | solution.py:28
  84.2 29.5 %collective-permute-start.15 = (bf16[4,192,768]{2,1,0:T(8,128)(2,1)S(1)}, bf16[4,192,768]{2,1,0:T(8,128)(2,1)S(1)}, u32[]{:S(2)}, u32[]{:S(2)}) collective-permute-start(bf16[4,192,768]{2,1,0:T(8,128)(2,1)S(1)} %copy-done), channel_id=1, source_target_pairs={{0,1},{1,0},{2,3},{3,2},{4,5},{5,4},{6,7},{7,6},{8,9},{9,8},{10,11... | collective-permute-start | bytes 3538952 | tf_op jit(solution)/shard_map/ppermute | solution.py:28
  88.9 33.3 %collective-permute-start.23 = (bf16[768,768]{1,0:T(8,128)(2,1)}, bf16[768,768]{1,0:T(8,128)(2,1)}, u32[]{:S(2)}, u32[]{:S(2)}) collective-permute-start(bf16[768,768]{1,0:T(8,128)(2,1)} %bitcast.48), channel_id=1, source_target_pairs={{0,2},{2,0},{1,3},{3,1},{4,6},{6,4},{5,7},{7,5},{8,10},{10,8},{9,1... | collective-permute-start | bytes 3538952 | tf_op jit(solution)/shard_map/ppermute | solution.py:32
  104.9 45.9 %collective-permute-start.22 = (bf16[2,768,768]{2,1,0:T(8,128)(2,1)S(1)}, bf16[2,768,768]{2,1,0:T(8,128)(2,1)}, u32[]{:S(2)}, u32[]{:S(2)}) collective-permute-start(bf16[2,768,768]{2,1,0:T(8,128)(2,1)S(1)} %copy-done.1), channel_id=1, source_target_pairs={{0,1},{1,0},{2,3},{3,2},{4,5},{5,4},{6,7},{7,6},{8,9},{9,8},{10,11... | collective-permute-start | bytes 7077896 | tf_op jit(solution)/shard_map/ppermute | solution.py:28
  122.2 28.6 %collective-permute-start.24 = (bf16[768,768]{1,0:T(8,128)(2,1)}, bf16[768,768]{1,0:T(8,128)(2,1)S(1)}, u32[]{:S(2)}, u32[]{:S(2)}) collective-permute-start(bf16[768,768]{1,0:T(8,128)(2,1)} %collective-permute-done.23.refs_4_.refs_10_), channel_id=1, source_target_pairs={{0,4},{4,0},{8,12},{12,8},{16,20},{20,16},{24,28},{28,24},{1,5},{5... | collective-permute-start | bytes 3538952 | tf_op jit(solution)/shard_map/ppermute | solution.py:37
  131.8 30.1 %collective-permute-start.25 = (bf16[768,768]{1,0:T(8,128)(2,1)}, bf16[768,768]{1,0:T(8,128)(2,1)S(1)}, u32[]{:S(2)}, u32[]{:S(2)}) collective-permute-start(bf16[768,768]{1,0:T(8,128)(2,1)} %collective-permute-done.23.refs_4_.refs_10_), channel_id=1, source_target_pairs={{0,1},{1,0},{2,3},{3,2},{4,5},{5,4},{6,7},{7,6},{8,9},{9,8},{10,11... | collective-permute-start | bytes 3538952 | tf_op jit(solution)/shard_map/ppermute | solution.py:28
  192.4 22.6 %collective-permute-start.34 = (bf16[2,192,768]{2,1,0:T(8,128)(2,1)}, bf16[2,192,768]{2,1,0:T(8,128)(2,1)S(1)}, u32[]{:S(2)}, u32[]{:S(2)}) collective-permute-start(bf16[2,192,768]{2,1,0:T(8,128)(2,1)} %get-tuple-element.295), channel_id=1, source_target_pairs={{0,1},{1,0},{2,3},{3,2},{4,5},{5,4},{6,7},{7,6},{8,9},{9,8},{10,11... | collective-permute-start | bytes 1769480 | tf_op jit(solution)/shard_map/ppermute | solution.py:28
  192.5 22.8 %collective-permute-start.35 = (bf16[2,192,768]{2,1,0:T(8,128)(2,1)}, bf16[2,192,768]{2,1,0:T(8,128)(2,1)S(1)}, u32[]{:S(2)}, u32[]{:S(2)}) collective-permute-start(bf16[2,192,768]{2,1,0:T(8,128)(2,1)} %get-tuple-element.296), channel_id=1, source_target_pairs={{0,1},{1,0},{2,3},{3,2},{4,5},{5,4},{6,7},{7,6},{8,9},{9,8},{10,11... | collective-permute-start | bytes 1769480 | tf_op jit(solution)/shard_map/ppermute | solution.py:28
  242.7 29.7 %collective-permute-start.40 = (bf16[2,384,768]{2,1,0:T(8,128)(2,1)}, bf16[2,384,768]{2,1,0:T(8,128)(2,1)S(1)}, u32[]{:S(2)}, u32[]{:S(2)}) collective-permute-start(bf16[2,384,768]{2,1,0:T(8,128)(2,1)} %get-tuple-element.314), channel_id=1, source_target_pairs={{0,4},{4,0},{8,12},{12,8},{16,20},{20,16},{24,28},{28,24},{1,5},{5... | collective-permute-start | bytes 3538952 | tf_op jit(solution)/shard_map/ppermute | solution.py:37
  244.2 28.3 %collective-permute-start.39 = (bf16[2,384,768]{2,1,0:T(8,128)(2,1)}, bf16[2,384,768]{2,1,0:T(8,128)(2,1)S(1)}, u32[]{:S(2)}, u32[]{:S(2)}) collective-permute-start(bf16[2,384,768]{2,1,0:T(8,128)(2,1)} %get-tuple-element.300.refs_32_), channel_id=1, source_target_pairs={{0,2},{2,0},{1,3},{3,1},{4,6},{6,4},{5,7},{7,5},{8,10},{10,8},{9,1... | collective-permute-start | bytes 3538952 | tf_op jit(solution)/shard_map/ppermute | solution.py:32
  280.7 23.6 %collective-permute-start.64 = (bf16[2,192,768]{2,1,0:T(8,128)(2,1)}, bf16[2,192,768]{2,1,0:T(8,128)(2,1)S(1)}, u32[]{:S(2)}, u32[]{:S(2)}) collective-permute-start(bf16[2,192,768]{2,1,0:T(8,128)(2,1)} %get-tuple-element.357), channel_id=1, source_target_pairs={{0,1},{1,0},{2,3},{3,2},{4,5},{5,4},{6,7},{7,6},{8,9},{9,8},{10,11... | collective-permute-start | bytes 1769480 | tf_op jit(solution)/shard_map/ppermute | solution.py:28
  280.9 23.5 %collective-permute-start.53 = (bf16[384,768]{1,0:T(8,128)(2,1)}, bf16[384,768]{1,0:T(8,128)(2,1)S(1)}, u32[]{:S(2)}, u32[]{:S(2)}) collective-permute-start(bf16[384,768]{1,0:T(8,128)(2,1)} %get-tuple-element.341), channel_id=1, source_target_pairs={{0,4},{4,0},{8,12},{12,8},{16,20},{20,16},{24,28},{28,24},{1,5},{5... | collective-permute-start | bytes 1769480 | tf_op jit(solution)/shard_map/ppermute | solution.py:37
  281.5 23.4 %collective-permute-start.54 = (bf16[384,768]{1,0:T(8,128)(2,1)}, bf16[384,768]{1,0:T(8,128)(2,1)S(1)}, u32[]{:S(2)}, u32[]{:S(2)}) collective-permute-start(bf16[384,768]{1,0:T(8,128)(2,1)} %get-tuple-element.343), channel_id=1, source_target_pairs={{0,2},{2,0},{1,3},{3,1},{4,6},{6,4},{5,7},{7,5},{8,10},{10,8},{9,1... | collective-permute-start | bytes 1769480 | tf_op jit(solution)/shard_map/ppermute | solution.py:32
  282.7 26.9 %collective-permute-start.55 = (bf16[2,192,768]{2,1,0:T(8,128)(2,1)}, bf16[2,192,768]{2,1,0:T(8,128)(2,1)S(1)}, u32[]{:S(2)}, u32[]{:S(2)}) collective-permute-start(bf16[2,192,768]{2,1,0:T(8,128)(2,1)} %get-tuple-element.345), channel_id=1, source_target_pairs={{0,2},{2,0},{1,3},{3,1},{4,6},{6,4},{5,7},{7,5},{8,10},{10,8},{9,1... | collective-permute-start | bytes 1769480 | tf_op jit(solution)/shard_map/ppermute | solution.py:32
  283.5 26.1 %collective-permute-start.56 = (bf16[2,192,768]{2,1,0:T(8,128)(2,1)}, bf16[2,192,768]{2,1,0:T(8,128)(2,1)S(1)}, u32[]{:S(2)}, u32[]{:S(2)}) collective-permute-start(bf16[2,192,768]{2,1,0:T(8,128)(2,1)} %get-tuple-element.347), channel_id=1, source_target_pairs={{0,4},{4,0},{8,12},{12,8},{16,20},{20,16},{24,28},{28,24},{1,5},{5... | collective-permute-start | bytes 1769480 | tf_op jit(solution)/shard_map/ppermute | solution.py:37
  320.1 24.9 %collective-permute-start.66 = (bf16[192,768]{1,0:T(8,128)(2,1)}, bf16[192,768]{1,0:T(8,128)(2,1)S(1)}, u32[]{:S(2)}, u32[]{:S(2)}) collective-permute-start(bf16[192,768]{1,0:T(8,128)(2,1)} %get-tuple-element.362), channel_id=1, source_target_pairs={{0,4},{4,0},{8,12},{12,8},{16,20},{20,16},{24,28},{28,24},{1,5},{5... | collective-permute-start | bytes 884744 | tf_op jit(solution)/shard_map/ppermute | solution.py:37
  321.7 23.7 %collective-permute-start.67 = (bf16[192,768]{1,0:T(8,128)(2,1)}, bf16[192,768]{1,0:T(8,128)(2,1)S(1)}, u32[]{:S(2)}, u32[]{:S(2)}) collective-permute-start(bf16[192,768]{1,0:T(8,128)(2,1)} %get-tuple-element.364), channel_id=1, source_target_pairs={{0,2},{2,0},{1,3},{3,1},{4,6},{6,4},{5,7},{7,5},{8,10},{10,8},{9,1... | collective-permute-start | bytes 884744 | tf_op jit(solution)/shard_map/ppermute | solution.py:32
  347.8 46.5 %collective-permute-start.79 = (bf16[2,384,768]{2,1,0:T(8,128)(2,1)}, bf16[2,384,768]{2,1,0:T(8,128)(2,1)S(1)}, u32[]{:S(2)}, u32[]{:S(2)}) collective-permute-start(bf16[2,384,768]{2,1,0:T(8,128)(2,1)} %get-tuple-element.381), channel_id=1, source_target_pairs={{0,2},{2,0},{1,3},{3,1},{4,6},{6,4},{5,7},{7,5},{8,10},{10,8},{9,1... | collective-permute-start | bytes 3538952 | tf_op jit(solution)/shard_map/ppermute | solution.py:32
  348.7 45.6 %collective-permute-start.80 = (bf16[2,384,768]{2,1,0:T(8,128)(2,1)}, bf16[2,384,768]{2,1,0:T(8,128)(2,1)S(1)}, u32[]{:S(2)}, u32[]{:S(2)}) collective-permute-start(bf16[2,384,768]{2,1,0:T(8,128)(2,1)} %get-tuple-element.383), channel_id=1, source_target_pairs={{0,4},{4,0},{8,12},{12,8},{16,20},{20,16},{24,28},{28,24},{1,5},{5... | collective-permute-start | bytes 3538952 | tf_op jit(solution)/shard_map/ppermute | solution.py:37
  403.1 28.7 %collective-permute-start.86 = (bf16[384,768]{1,0:T(8,128)(2,1)}, bf16[384,768]{1,0:T(8,128)(2,1)S(1)}, u32[]{:S(2)}, u32[]{:S(2)}) collective-permute-start(bf16[384,768]{1,0:T(8,128)(2,1)} %get-tuple-element.393), channel_id=1, source_target_pairs={{0,4},{4,0},{8,12},{12,8},{16,20},{20,16},{24,28},{28,24},{1,5},{5... | collective-permute-start | bytes 1769480 | tf_op jit(solution)/shard_map/ppermute | solution.py:37
  403.9 28.0 %collective-permute-start.87 = (bf16[384,768]{1,0:T(8,128)(2,1)}, bf16[384,768]{1,0:T(8,128)(2,1)S(1)}, u32[]{:S(2)}, u32[]{:S(2)}) collective-permute-start(bf16[384,768]{1,0:T(8,128)(2,1)} %get-tuple-element.395), channel_id=1, source_target_pairs={{0,2},{2,0},{1,3},{3,1},{4,6},{6,4},{5,7},{7,5},{8,10},{10,8},{9,1... | collective-permute-start | bytes 1769480 | tf_op jit(solution)/shard_map/ppermute | solution.py:32
  438.1 37.7 %collective-permute-start.93 = (bf16[384,768]{1,0:T(8,128)(2,1)}, bf16[384,768]{1,0:T(8,128)(2,1)S(1)}, u32[]{:S(2)}, u32[]{:S(2)}) collective-permute-start(bf16[384,768]{1,0:T(8,128)(2,1)} %get-tuple-element.404), channel_id=1, source_target_pairs={{0,8},{4,12},{8,0},{12,4},{16,24},{20,28},{24,16},{28,20},{1,9},{5... | collective-permute-start | bytes 1769480 | tf_op jit(solution)/shard_map/ppermute | solution.py:37
  438.2 37.6 %collective-permute-start.91 = (bf16[384,768]{1,0:T(8,128)(2,1)}, bf16[384,768]{1,0:T(8,128)(2,1)S(1)}, u32[]{:S(2)}, u32[]{:S(2)}) collective-permute-start(bf16[384,768]{1,0:T(8,128)(2,1)} %get-tuple-element.401.refs_0_.refs_15_), channel_id=1, source_target_pairs={{0,8},{4,12},{8,0},{12,4},{16,24},{20,28},{24,16},{28,20},{1,9},{5... | collective-permute-start | bytes 1769480 | tf_op jit(solution)/shard_map/ppermute | solution.py:37
  440.2 35.6 %collective-permute-start.94 = (bf16[192,768]{1,0:T(8,128)(2,1)}, bf16[192,768]{1,0:T(8,128)(2,1)S(1)}, u32[]{:S(2)}, u32[]{:S(2)}) collective-permute-start(bf16[192,768]{1,0:T(8,128)(2,1)} %get-tuple-element.406), channel_id=1, source_target_pairs={{0,8},{4,12},{8,0},{12,4},{16,24},{20,28},{24,16},{28,20},{1,9},{5... | collective-permute-start | bytes 884744 | tf_op jit(solution)/shard_map/ppermute | solution.py:37
  440.3 33.4 %collective-permute-start.92 = (bf16[96,768]{1,0:T(8,128)(2,1)}, bf16[96,768]{1,0:T(8,128)(2,1)S(1)}, u32[]{:S(2)}, u32[]{:S(2)}) collective-permute-start(bf16[96,768]{1,0:T(8,128)(2,1)} %get-tuple-element.402.refs_2_), channel_id=1, source_target_pairs={{0,16},{4,20},{8,24},{12,28},{16,0},{20,4},{24,8},{28,12},{1,17},{... | collective-permute-start | bytes 442376 | tf_op jit(solution)/shard_map/ppermute | solution.py:37
  481.1 27.3 %collective-permute-start.100 = (bf16[768,768]{1,0:T(8,128)(2,1)}, bf16[768,768]{1,0:T(8,128)(2,1)S(1)}, u32[]{:S(2)}, u32[]{:S(2)}) collective-permute-start(bf16[768,768]{1,0:T(8,128)(2,1)} %get-tuple-element.414.refs_13_), channel_id=1, source_target_pairs={{0,4},{4,0},{8,12},{12,8},{16,20},{20,16},{24,28},{28,24},{1,5},{5... | collective-permute-start | bytes 3538952 | tf_op jit(solution)/shard_map/ppermute | solution.py:37
  563.4 43.3 %collective-permute-start.107 = (bf16[768,768]{1,0:T(8,128)(2,1)}, bf16[768,768]{1,0:T(8,128)(2,1)S(1)}, u32[]{:S(2)}, u32[]{:S(2)}) collective-permute-start(bf16[768,768]{1,0:T(8,128)(2,1)} %get-tuple-element.430), channel_id=1, source_target_pairs={{0,4},{4,0},{8,12},{12,8},{16,20},{20,16},{24,28},{28,24},{1,5},{5... | collective-permute-start | bytes 3538952 | tf_op jit(solution)/shard_map/ppermute | solution.py:37
  564.1 37.9 %collective-permute-start.106 = (bf16[384,768]{1,0:T(8,128)(2,1)}, bf16[384,768]{1,0:T(8,128)(2,1)}, u32[]{:S(2)}, u32[]{:S(2)}) collective-permute-start(bf16[384,768]{1,0:T(8,128)(2,1)} %get-tuple-element.422.refs_0_), channel_id=1, source_target_pairs={{0,4},{4,0},{8,12},{12,8},{16,20},{20,16},{24,28},{28,24},{1,5},{5... | collective-permute-start | bytes 1769480 | tf_op jit(solution)/shard_map/ppermute | solution.py:37
  (188 other events, 1799.9 us)

commit v3 on v2

--- a/solution.py
+++ b/solution.py
@@ -55,13 +55,16 @@
 
 
 PLANS = (
-    (((3, 2), (5, 1), (6, 1), (7, 1), (8, 1), (9, 1), (10, 1)), ((4, 1), (5, 1), (6, 1), (7, 1), (8, 1), (9, 1), (10, 1))),
     (
-        ((3, 2), (5, 1), (6, 1), (7, 1), (8, 1), (9, 1), (10, 1)),
+        ((3, 2), (5, 1), (6, 1), (7, 1), (8, 1), (9, 1), (10, 9)),
+        ((4, 1), (5, 1), (6, 1), (7, 1), (8, 1), (9, 1), (10, 9)),
+    ),
+    (
+        ((3, 1), (4, 1), (5, 1), (6, 1), (7, 1), (8, 1), (9, 1)),
         ((5, 1), (6, 1), (7, 1), (8, 1), (9, 1), (10, 1), (11, 1)),
     ),
 )
-SMALL_PLAN = ((1, 1), (2, 1), (3, 1), (4, 1), (5, 1), (6, 1))
+SMALL_PLAN = ((3, 1), (4, 1), (5, 1), (6, 1), (7, 1))
 VMEM_BYTES = 58 * 2**20
 PARAMS = pltpu.CompilerParams(vmem_limit_bytes=VMEM_BYTES)
 WHOLE = pl.BlockSpec(memory_space=pltpu.VMEM)
@@ -618,7 +621,7 @@
         for at, item in enumerate(earlier):
             rows_out[SMALL_ROWS * at : SMALL_ROWS * (at + 1)] = item[...]
         xbit = numbers[0]
-        targets = (grads[0:1], grads[1:5], grads[5:6], grads[6:10])
+        targets = (grads[0:1], grads[1:3], grads[3:4], grads[4:6])
         copies = fetch(
             att_pairs(False, raws[2:], held.at[1], xbit, 3) + att_pairs(True, raws[:2], held.at[0], xbit, 3), sems
         )
@@ -685,14 +688,14 @@
     rows = SMALL_ROWS * (len(little) - 1)
     outs = [jax.ShapeDtypeStruct((rows, width), F32), jax.ShapeDtypeStruct((count, width), F32)]
     whole = jax.ShapeDtypeStruct((4, inner, width), BF)
-    part = jax.ShapeDtypeStruct((4, inner // 4, width), BF)
+    part = jax.ShapeDtypeStruct((4, inner // 2, width), BF)
     ordered = [normed, incoming, places]
     for grad_query, grad_kept, came_key, came_value, query, kept, cosine, sine, mixed in sides:
         ordered += [mixed, grad_query, query, grad_kept, came_key, came_value, kept, cosine, sine]
     found = staged(
         body, "qkv_back", 32 * count * width * 2 * inner, x_bit,
         ordered + [gain, inputs_kept, grad_middle] + list(little), tuple(near) + tuple(far), outs,
-        ([whole] + [part] * 4) * 2,
+        ([whole] + [part] * 2) * 2,
         (
             pltpu.VMEM((2, 4, 2 * inner, width), BF),
             pltpu.VMEM((2, 4, 2 * inner, width), BF),
@@ -701,10 +704,10 @@
         ),
         gates,
     )
-    return (found[2], found[3:7], found[7], found[8:12]), found[:2]
-
-
-def run_tasks(place, tasks, gates):
+    return (found[2], found[3:5], found[5], found[6:8]), found[:2]
+
+
+def run_tasks(place, tasks, gates, alone):
     inputs = [item for task in tasks for item in task[0]]
     outs = [jax.ShapeDtypeStruct(*item) for task in tasks for item in task[1]]
 
@@ -713,7 +716,22 @@
             task[2](at[0], sources[: len(task[0])], results[: len(task[1])])
             sources, results = sources[len(task[0]) :], results[len(task[1]) :]
 
-    found = staged(body, "sums", 0, place, inputs, (), outs, gates=gates)
+    if alone:
+
+        def kernel(at, *refs):
+            body(at, refs[: len(inputs)], (), refs[len(inputs) + len(gates) :], ())
+
+        found = pl.pallas_call(
+            kernel,
+            out_shape=outs,
+            in_specs=[SCALAR] + [WHOLE] * len(inputs) + [PLACE] * len(gates),
+            out_specs=[WHOLE] * len(outs),
+            compiler_params=pltpu.CompilerParams(vmem_limit_bytes=24 * 2**20),
+            name="sums_alone",
+            cost_estimate=pl.CostEstimate(flops=0, bytes_accessed=2**20, transcendentals=0),
+        )(place, *inputs, *gates)
+    else:
+        found = staged(body, "sums", 0, place, inputs, (), outs, gates=gates)
     given = []
     for task in tasks:
         given.append(found[: len(task[1])])
@@ -726,6 +744,9 @@
 
 
 class Piece:
+    def __init__(self, swapped=False):
+        self.swapped = swapped
+
     def begin(self, found):
         self.own, first, self.second, third = found
         self.came_near = [over_core(item) for item in first]
@@ -737,7 +758,8 @@
 
     def sum_of(self, sources, quarter, slot, high):
         mine = sources[quarter]
-        parts = sources[2 + 4 * quarter : 6 + 4 * quarter]
+        many = (len(sources) - 2) // 2
+        parts = sources[2 + many * quarter : 2 + many * (quarter + 1)]
         if mine.shape[0] == 2:
             rows = mine.shape[1] // 2
             own = mine[slot, high * rows : (high + 1) * rows]
@@ -854,8 +876,10 @@
         bits = lax.axis_size("dp").bit_length() - 1
         self.kept = None
         calls = [self.cross, self.turn] + [partial(self.halve, bit) for bit in range(1, bits)]
-        calls += [self.whole] + [partial(self.join, bit) for bit in reversed(range(1, bits))]
         self.ways = list(range(bits))
+        if self.swapped and bits > 1:
+            self.ways[:2] = [1, 0]
+        calls += [self.whole] + [partial(self.join, bit) for bit in reversed(self.ways[1:])]
         return calls
 
     def result(self, bit):
@@ -973,12 +997,12 @@
 
     def tasks(self):
         bits = lax.axis_size("dp").bit_length() - 1
-        moves = [partial(over_bit, bit=bit) for bit in (*range(1, bits), 0)] + [over_y]
+        moves = [partial(over_bit, bit=bit) for bit in (1, 0, *range(2, bits))] + [over_y]
         quarters = [1] + [0] * bits
         return [partial(self.step, *item) for item in zip(quarters, moves)] + [self.last]
 
 
-def attention_outputs(x_bit, pieces):
+def attention_outputs(place, pieces):
     _, width = pieces[0].total.shape
     inner = pieces[0].total.shape[0] // 2
     layers = len(pieces)
@@ -986,18 +1010,19 @@
     def body(numbers, inputs, _, results, __):
         for layer in reversed(range(layers)):
             mine, other = inputs[2 * layer : 2 * layer + 2]
-            first = jnp.where(numbers[0] == 0, mine[...], other[...]).astype(F32)
-            second = jnp.where(numbers[0] == 0, other[...], mine[...]).astype(F32)
+            ahead = ((numbers[0] >> 1) & 1) == 0
+            first = jnp.where(ahead, mine[...], other[...]).astype(F32)
+            second = jnp.where(ahead, other[...], mine[...]).astype(F32)
             results[0][layer, 0] = first[:inner]
-            results[0][layer, 1] = first[inner:]
-            results[0][layer, 2] = second[:inner]
+            results[0][layer, 1] = second[:inner]
+            results[0][layer, 2] = first[inner:]
             results[0].leave(layer)
             results[1][layer] = second[inner:]
             results[1].leave(layer)
 
     items = [item for piece in pieces for item in (piece.total, piece.others[0])]
     return staged(
-        body, "attention_outputs", 0, x_bit, items, (),
+        body, "attention_outputs", 0, place, items, (),
         (jax.ShapeDtypeStruct((layers, 3, inner, width), F32), jax.ShapeDtypeStruct((layers, inner, width), F32)),
     )
 
@@ -1173,7 +1198,7 @@
         if not turn:
             return due + latest
         tasks = [step() for _, _, step in turn]
-        found = run_tasks(here, [task[:3] for task in tasks], due + latest)
+        found = run_tasks(here, [task[:3] for task in tasks], due + latest, clock > 3 * LAYERS + 1)
         for (_, length, _), task, given in zip(turn, tasks, found):
             wait_until(task[3](given), clock + length)
         latest[:] = found[0][:1]
@@ -1188,7 +1213,7 @@
     for l in reversed(range(LAYERS)):
         (inputs, normed, queries, keeps, comes, mixes, spreads, exps, middle, normed_mlp, active, slope) = kept_layers[l]
         att = (near_att[l], far_att[l].found)
-        pieces = [Piece(), Piece()]
+        pieces = [Piece(), Piece(swapped=True)]
         tables = PLANS[l > 0]
         for piece, table in zip(pieces, tables):
             plan(piece, clock, table)
@@ -1225,7 +1250,7 @@
     while todo:
         gates_now()
     gain1, shift1, bias_out, gain2, shift2, bias_down, bias_up, bias_qkv, turns = little.found[:9]
-    grad_qkv, grad_out = attention_outputs(x_bit, [summed[l][1] for l in range(LAYERS)])
+    grad_qkv, grad_out = attention_outputs(here, [summed[l][1] for l in range(LAYERS)])
     grad_up, grad_down = zip(*(summed[l][0].result(xbit) for l in range(LAYERS)))
     return (
         activations,

time: 621 us -> 563 us (0.907)
  waiting for transfers between devices: 210 us -> 173 us
  Pallas kernels: 291 us -> 271 us
    ppermute x35, waiting for transfers between devices: 175 us -> 138 us  [over_bit(): lax.ppermute(values, 'dp', [(at, at ^ 1 << bit) for at in range(size)])]
    pallas_call x33 -> x28, Pallas kernels: 291 us -> 268 us  [staged(): pl.pallas_call(kernel, out_shape=list(outs) + list(raw_outs), in_specs=[S...]
    ppermute x58 -> x50, starting transfers between devices: 13.6 us -> 10.7 us  [over_core(): return lax.ppermute(values, 'tensor', CORE)]
    unnamed x226 -> x174, local copies, waits for them, and re-layouts: 22.6 us -> 21.6 us
  transfers between devices with their start and end apart: 108 -> 100, of which waited for: 35 -> 35; matrix products, arithmetic and copies ran while one was open for 1% -> 1% of each run, Pallas kernels for 36% -> 40%
where the time goes in v3:
time: 563 us; the launch traced here: 553 us
  Pallas kernels  271 us (48%)
  waiting for transfers between devices  173 us (31%)
  starting transfers between devices  71.2 us (13%)
  local copies, waits for them, and re-layouts  26.7 us (5%)
  other arithmetic  9.28 us (2%)
    pallas_call x28, Pallas kernels, staged(): pl.pallas_call(kernel, out_shape=list(outs) + list(raw_outs), in_specs=[S...  268 us
    ppermute x35, waiting for transfers between devices, over_bit(): lax.ppermute(values, 'dp', [(at, at ^ 1 << bit) for at in range(size)])  138 us
    ppermute x35, starting transfers between devices, over_bit(): lax.ppermute(values, 'dp', [(at, at ^ 1 << bit) for at in range(size)])  43.3 us
    ppermute x14, waiting for transfers between devices, over_y(): return lax.ppermute(values, 'tensor', ACROSS)  26.4 us
    unnamed x174, local copies, waits for them, and re-layouts  21.6 us
    ppermute x14, starting transfers between devices, over_y(): return lax.ppermute(values, 'tensor', ACROSS)  14.7 us
  transfers between devices with their start and end apart: 100, of which 35 were waited for; matrix products, arithmetic and copies ran while one was open for 1% of the time, Pallas kernels for 40%

profile of v3, /device:TPU:0, one launch (start us, length us, event | category | flops | bytes accessed | tf_op | source)
XLA Modules:
  0.0 553.0 jit_solution(17475312027519545063)
XLA Ops:
  15.9 7.3 %qkv_near.2 = (bf16[416,384]{1,0:T(8,128)(2,1)}, bf16[2,416,384]{2,1,0:T(8,128)(2,1)}, bf16[2,416,384]{2,1,0:T(8,128)(2,1)}, f32[416,384]{1,0:T(8,128)}, f32[416,384]{1,0:T(8,128)}, /*index=5*/bf16[416,768]{1,0:T(8,128)(2,1)}) custom-call(s32[2]{0:T(128)} %pad_add_fusion.1.numbers, f32[1,768]{1,0:T(1,128)} %get-tuple-element.504.refs_0_.refs_21_, ...), custom_call_target="tpu_custom_call" | custom-call | flops 92012544 | bytes 1048576 | tf_op jit(solution)/shard_map/qkv_near/pallas_call | solution.py:188
  34.5 8.3 %attend.4 = (bf16[416,384]{1,0:T(8,128)(2,1)}, f32[416,384]{1,0:T(8,128)}, bf16[6,416,832]{2,1,0:T(8,128)(2,1)}) custom-call(s32[2]{0:T(128)} %pad_add_fusion.1.numbers, bf16[416,384]{1,0:T(8,128)(2,1)} %get-tuple-element.217.refs_2_.refs_0_.refs_5_, bf16[2,416,384]{2,1,0:T(8,128)(2,1)} %get-tuple-element.218.refs_1_.refs_3_.refs_9_, ...), custom_call_target="tpu_custom_call" | custom-call | flops 122683392 | bytes 1048576 | tf_op jit(solution)/shard_map/attend/pallas_call | solution.py:188
  44.4 12.2 %collective-permute-done.11.refs_4_.refs_10_ = bf16[768,768]{1,0:T(8,128)(2,1)} collective-permute-done((bf16[768,768]{1,0:T(8,128)(2,1)}, bf16[768,768]{1,0:T(8,128)(2,1)}, u32[]{:S(2)}, u32[]{:S(2)}) %collective-permute-start.11) | collective-permute-done | bytes 1179680 | tf_op jit(solution)/shard_map/ppermute | solution.py:32
  62.4 7.8 %qkv_far.2 = (bf16[416,384]{1,0:T(8,128)(2,1)}, bf16[2,416,384]{2,1,0:T(8,128)(2,1)}, bf16[2,416,384]{2,1,0:T(8,128)(2,1)}, f32[416,384]{1,0:T(8,128)}, f32[416,384]{1,0:T(8,128)}) custom-call(s32[2]{0:T(128)} %pad_add_fusion.1.numbers, f32[1,768]{1,0:T(1,128)} %get-tuple-element.504.refs_0_.refs_21_, f32[1,768]{1,0:T(1,128)} %get-tuple-element.493.refs_1_, ...), custom_call_target="tpu_custom_call" | custom-call | flops 92012544 | bytes 1048576 | tf_op jit(solution)/shard_map/qkv_far/pallas_call | solution.py:188
  73.3 8.2 %attend.5 = (bf16[416,384]{1,0:T(8,128)(2,1)}, f32[416,384]{1,0:T(8,128)}, bf16[6,416,832]{2,1,0:T(8,128)(2,1)}) custom-call(s32[2]{0:T(128)} %pad_add_fusion.1.numbers, bf16[416,384]{1,0:T(8,128)(2,1)} %get-tuple-element.227.refs_0_.refs_5_.refs_11_.refs_14_, bf16[2,416,384]{2,1,0:T(8,128)(2,1)} %get-tuple-element.228.refs_1_.refs_9_.refs_18_, ...), custom_call_target="tpu_custom_call" | custom-call | flops 122683392 | bytes 1048576 | tf_op jit(solution)/shard_map/attend/pallas_call | solution.py:188
  92.8 11.2 %mlp_near.2 = (f32[416,768]{1,0:T(8,128)}, bf16[416,768]{1,0:T(8,128)(2,1)}, bf16[2,416,768]{2,1,0:T(8,128)(2,1)}, bf16[2,416,768]{2,1,0:T(8,128)(2,1)}, f32[416,768]{1,0:T(8,128)}) custom-call(s32[2]{0:T(128)} %pad_add_fusion.1.numbers, bf16[416,384]{1,0:T(8,128)(2,1)} %get-tuple-element.221.refs_2_.refs_0_.refs_1_.refs_3_, ...), custom_call_target="tpu_custom_call" | custom-call | flops 306708480 | bytes 1048576 | tf_op jit(solution)/shard_map/mlp_near/pallas_call | solution.py:188
  105.0 8.8 %mlp_far.2 = (bf16[2,416,768]{2,1,0:T(8,128)(2,1)}, bf16[2,416,768]{2,1,0:T(8,128)(2,1)}, f32[416,768]{1,0:T(8,128)}) custom-call(s32[2]{0:T(128)} %pad_add_fusion.1.numbers, bf16[416,768]{1,0:T(8,128)(2,1)} %get-tuple-element.232.refs_0_.refs_3_, f32[2,1536]{1,0:T(2,128)} %copy-done.69, f32[2,1536]{1,0:T(2,128)} %copy-done.68, ...), custom_call_target="tpu_custom_call" | custom-call | flops 245366784 | bytes 1048576 | tf_op jit(solution)/shard_map/mlp_far/pallas_call | solution.py:188
  114.9 7.3 %qkv_near.3 = (bf16[416,384]{1,0:T(8,128)(2,1)}, bf16[2,416,384]{2,1,0:T(8,128)(2,1)}, bf16[2,416,384]{2,1,0:T(8,128)(2,1)}, f32[416,384]{1,0:T(8,128)}, f32[416,384]{1,0:T(8,128)}, /*index=5*/bf16[416,768]{1,0:T(8,128)(2,1)}) custom-call(s32[2]{0:T(128)} %pad_add_fusion.1.numbers, f32[1,768]{1,0:T(1,128)} %get-tuple-element.503.refs_0_.refs_21_, ...), custom_call_target="tpu_custom_call" | custom-call | flops 92012544 | bytes 1048576 | tf_op jit(solution)/shard_map/qkv_near/pallas_call | solution.py:188
  124.1 7.3 %qkv_far.3 = (bf16[416,384]{1,0:T(8,128)(2,1)}, bf16[2,416,384]{2,1,0:T(8,128)(2,1)}, bf16[2,416,384]{2,1,0:T(8,128)(2,1)}, f32[416,384]{1,0:T(8,128)}, f32[416,384]{1,0:T(8,128)}) custom-call(s32[2]{0:T(128)} %pad_add_fusion.1.numbers, f32[1,768]{1,0:T(1,128)} %get-tuple-element.503.refs_0_.refs_21_, f32[1,768]{1,0:T(1,128)} %get-tuple-element.494.refs_1_, ...), custom_call_target="tpu_custom_call" | custom-call | flops 92012544 | bytes 1048576 | tf_op jit(solution)/shard_map/qkv_far/pallas_call | solution.py:188
  132.0 8.3 %attend.6 = (bf16[416,384]{1,0:T(8,128)(2,1)}, f32[416,384]{1,0:T(8,128)}, bf16[6,416,832]{2,1,0:T(8,128)(2,1)}) custom-call(s32[2]{0:T(128)} %pad_add_fusion.1.numbers, bf16[416,384]{1,0:T(8,128)(2,1)} %get-tuple-element.238.refs_10_.refs_0_.refs_5_, bf16[2,416,384]{2,1,0:T(8,128)(2,1)} %get-tuple-element.239.refs_1_.refs_3_.refs_9_, ...), custom_call_target="tpu_custom_call" | custom-call | flops 122683392 | bytes 1048576 | tf_op jit(solution)/shard_map/attend/pallas_call | solution.py:188
  141.1 8.6 %attend.7 = (bf16[416,384]{1,0:T(8,128)(2,1)}, f32[416,384]{1,0:T(8,128)}, bf16[6,416,832]{2,1,0:T(8,128)(2,1)}) custom-call(s32[2]{0:T(128)} %pad_add_fusion.1.numbers, bf16[416,384]{1,0:T(8,128)(2,1)} %get-tuple-element.246.refs_5_.refs_0_.refs_11_.refs_14_, bf16[2,416,384]{2,1,0:T(8,128)(2,1)} %get-tuple-element.248.refs_1_.refs_9_.refs_18_, ...), custom_call_target="tpu_custom_call" | custom-call | flops 122683392 | bytes 1048576 | tf_op jit(solution)/shard_map/attend/pallas_call | solution.py:188
  150.8 11.1 %mlp_near.3 = (f32[416,768]{1,0:T(8,128)}, bf16[416,768]{1,0:T(8,128)(2,1)}, bf16[2,416,768]{2,1,0:T(8,128)(2,1)}, bf16[2,416,768]{2,1,0:T(8,128)(2,1)}, f32[416,768]{1,0:T(8,128)}) custom-call(s32[2]{0:T(128)} %pad_add_fusion.1.numbers, bf16[416,384]{1,0:T(8,128)(2,1)} %get-tuple-element.247.refs_5_.refs_0_.refs_1_.refs_3_, ...), custom_call_target="tpu_custom_call" | custom-call | flops 306708480 | bytes 1048576 | tf_op jit(solution)/shard_map/mlp_near/pallas_call | solution.py:188
  163.4 8.5 %mlp_far.3 = (bf16[2,416,768]{2,1,0:T(8,128)(2,1)}, bf16[2,416,768]{2,1,0:T(8,128)(2,1)}, bf16[416,768]{1,0:T(8,128)(2,1)}) custom-call(s32[2]{0:T(128)} %pad_add_fusion.1.numbers, bf16[416,768]{1,0:T(8,128)(2,1)} %get-tuple-element.251.refs_0_.refs_3_, f32[2,1536]{1,0:T(2,128)} %copy-done.69, f32[2,1536]{1,0:T(2,128)} %copy-done.68, ...), custom_call_target="tpu_custom_call" | custom-call | flops 245366784 | bytes 1048576 | tf_op jit(solution)/shard_map/mlp_far/pallas_call | solution.py:188
  171.9 19.5 %mlp_back.2 = (f32[4,768]{1,0:T(4,128)}, f32[4,768]{1,0:T(4,128)}, f32[416,768]{1,0:T(8,128)}, bf16[416,768]{1,0:T(8,128)(2,1)}, bf16[2,768,768]{2,1,0:T(8,128)(...) custom-call(s32[2]{0:T(128)} %pad_add_fusion.1.numbers, ...), custom_call_target="tpu_custom_call" | custom-call | flops 981467136 | bytes 1048576 | tf_op jit(solution)/shard_map/mlp_back/pallas_call | solution.py:188
  195.8 19.2 %attend_back.2 = (bf16[416,384]{1,0:T(8,128)(2,1)}, bf16[2,416,384]{2,1,0:T(8,128)(2,1)}, bf16[416,384]{1,0:T(8,128)(2,1)}, bf16[416,384]{1,0:T(8,128)(2,1)}, bf...) custom-call(s32[2]{0:T(128)} %pad_add_fusion.1.numbers, ...), custom_call_target="tpu_custom_call" | custom-call | flops 490733568 | bytes 1048576 | tf_op jit(solution)/shard_map/attend_back/pallas_call | solution.py:188
  216.8 6.6 %sums.5 = (bf16[2,384,768]{2,1,0:T(8,128)(2,1)}, bf16[2,384,768]{2,1,0:T(8,128)(2,1)}, bf16[2,384,768]{2,1,0:T(8,128)(2,1)}, bf16[2,384,768]{2,1,0:T(8,128)(2,1)}) custom-call(s32[1]{0:T(128)} %bitcast.17.numbers.at, bf16[2,768,768]{2,1,0:T(8,128)(2,1)} %get-tuple-element.282.refs_0_, bf16[2,768,768]{2,1,0:T(8,128)(2,1)} %get-tuple-element.283.refs_1_, ...), custom_call_target="tpu_custom_call" | custom-call | bytes 1048576 | tf_op jit(solution)/shard_map/sums/pallas_call | solution.py:188
  229.8 17.3 %qkv_back.2 = (f32[16,768]{1,0:T(8,128)}, f32[416,768]{1,0:T(8,128)}, bf16[4,192,768]{2,1,0:T(8,128)(2,1)}, bf16[4,96,768]{2,1,0:T(8,128)(2,1)}, bf16[4,96,768]{...) custom-call(s32[2]{0:T(128)} %pad_add_fusion.1.numbers, ...), custom_call_target="tpu_custom_call" | custom-call | flops 490733568 | bytes 1048576 | tf_op jit(solution)/shard_map/qkv_back/pallas_call | solution.py:188
  260.8 20.1 %mlp_back.3 = (f32[4,768]{1,0:T(4,128)}, f32[4,768]{1,0:T(4,128)}, f32[416,768]{1,0:T(8,128)}, bf16[416,768]{1,0:T(8,128)(2,1)}, bf16[2,768,768]{2,1,0:T(8,128)(...) custom-call(s32[2]{0:T(128)} %pad_add_fusion.1.numbers, ...), custom_call_target="tpu_custom_call" | custom-call | flops 981467136 | bytes 1048576 | tf_op jit(solution)/shard_map/mlp_back/pallas_call | solution.py:188
  293.4 19.2 %attend_back.3 = (bf16[416,384]{1,0:T(8,128)(2,1)}, bf16[2,416,384]{2,1,0:T(8,128)(2,1)}, bf16[416,384]{1,0:T(8,128)(2,1)}, bf16[416,384]{1,0:T(8,128)(2,1)}, bf...) custom-call(s32[2]{0:T(128)} %pad_add_fusion.1.numbers, ...), custom_call_target="tpu_custom_call" | custom-call | flops 490733568 | bytes 1048576 | tf_op jit(solution)/shard_map/attend_back/pallas_call | solution.py:188
  314.6 9.1 %sums.8 = (f32[192,768]{1,0:T(8,128)}, bf16[192,768]{1,0:T(8,128)(2,1)}, f32[192,768]{1,0:T(8,128)}, bf16[192,768]{1,0:T(8,128)(2,1)}, f32[192,768]{1,0:T(8,128)...) custom-call(s32[1]{0:T(128)} %bitcast.17.numbers.at, ...), custom_call_target="tpu_custom_call" | custom-call | bytes 1048576 | tf_op jit(solution)/shard_map/sums/pallas_call | solution.py:188
  324.9 18.8 %qkv_back.3 = (f32[32,768]{1,0:T(8,128)}, f32[416,768]{1,0:T(8,128)}, bf16[4,192,768]{2,1,0:T(8,128)(2,1)}, bf16[4,96,768]{2,1,0:T(8,128)(2,1)}, bf16[4,96,768]{...) custom-call(s32[2]{0:T(128)} %pad_add_fusion.1.numbers, ...), custom_call_target="tpu_custom_call" | custom-call | flops 490733568 | bytes 1048576 | tf_op jit(solution)/shard_map/qkv_back/pallas_call | solution.py:188
  348.8 11.6 %collective-permute-done.62.refs_1_.refs_12_ = bf16[192,768]{1,0:T(8,128)(2,1)S(1)} collective-permute-done((bf16[192,768]{1,0:T(8,128)(2,1)S(1)}, bf16[192,768]{1,0:T(8,128)(2,1)S(1)}, u32[]{:S(2)}, u32[]{:S(2)}) %collective-permute-start.62) | collective-permute-done | bytes 294944 | tf_op jit(solution)/shard_map/ppermute | solution.py:37
  372.8 6.7 %collective-permute-done.70.refs_3_.refs_15_ = bf16[192,768]{1,0:T(8,128)(2,1)S(1)} collective-permute-done((bf16[192,768]{1,0:T(8,128)(2,1)}, bf16[192,768]{1,0:T(8,128)(2,1)S(1)}, u32[]{:S(2)}, u32[]{:S(2)}) %collective-permute-start.70) | collective-permute-done | bytes 294944 | tf_op jit(solution)/shard_map/ppermute | solution.py:37
  380.9 13.6 %collective-permute-done.69.refs_1_.refs_14_ = bf16[192,768]{1,0:T(8,128)(2,1)S(1)} collective-permute-done((bf16[192,768]{1,0:T(8,128)(2,1)}, bf16[192,768]{1,0:T(8,128)(2,1)S(1)}, u32[]{:S(2)}, u32[]{:S(2)}) %collective-permute-start.69) | collective-permute-done | bytes 294944 | tf_op jit(solution)/shard_map/ppermute | solution.py:37
  394.6 7.8 %collective-permute-done.73.refs_9_.refs_16_ = bf16[2,192,768]{2,1,0:T(8,128)(2,1)S(1)} collective-permute-done((bf16[2,192,768]{2,1,0:T(8,128)(2,1)}, bf16[2,192,768]{2,1,0:T(8,128)(2,1)S(1)}, u32[]{:S(2)}, u32[]{:S(2)}) %collective-permute-start.73) | collective-permute-done | bytes 589856 | tf_op jit(solution)/shard_map/ppermute | solution.py:32
  415.9 8.8 %collective-permute-done.76.refs_3_.refs_16_ = bf16[96,768]{1,0:T(8,128)(2,1)S(1)} collective-permute-done((bf16[96,768]{1,0:T(8,128)(2,1)S(1)}, bf16[96,768]{1,0:T(8,128)(2,1)S(1)}, u32[]{:S(2)}, u32[]{:S(2)}) %collective-permute-start.76) | collective-permute-done | bytes 147488 | tf_op jit(solution)/shard_map/ppermute | solution.py:37
  439.4 19.8 %collective-permute-done.85.refs_7_.refs_12_ = f32[32,768]{1,0:T(8,128)S(1)} collective-permute-done((f32[32,768]{1,0:T(8,128)S(1)}, f32[32,768]{1,0:T(8,128)S(1)}, u32[]{:S(2)}, u32[]{:S(2)}) %collective-permute-start.85) | collective-permute-done | bytes 98336 | tf_op jit(solution)/shard_map/ppermute | solution.py:37
  468.9 9.0 %collective-permute-done.89.refs_5_.refs_10_ = bf16[96,768]{1,0:T(8,128)(2,1)S(1)} collective-permute-done((bf16[96,768]{1,0:T(8,128)(2,1)S(1)}, bf16[96,768]{1,0:T(8,128)(2,1)S(1)}, u32[]{:S(2)}, u32[]{:S(2)}) %collective-permute-start.89) | collective-permute-done | bytes 147488 | tf_op jit(solution)/shard_map/ppermute | solution.py:37
  483.6 20.8 %collective-permute-done.93.refs_5_.refs_9_ = f32[32,768]{1,0:T(8,128)S(1)} collective-permute-done((f32[32,768]{1,0:T(8,128)S(1)}, f32[32,768]{1,0:T(8,128)S(1)}, u32[]{:S(2)}, u32[]{:S(2)}) %collective-permute-start.93) | collective-permute-done | bytes 98336 | tf_op jit(solution)/shard_map/ppermute | solution.py:37
  513.0 6.3 %collective-permute-done.95.refs_1_.refs_6_ = bf16[384,768]{1,0:T(8,128)(2,1)S(1)} collective-permute-done((bf16[384,768]{1,0:T(8,128)(2,1)S(1)}, bf16[384,768]{1,0:T(8,128)(2,1)S(1)}, u32[]{:S(2)}, u32[]{:S(2)}) %collective-permute-start.95) | collective-permute-done | bytes 589856 | tf_op jit(solution)/shard_map/ppermute | solution.py:37
  522.2 11.8 %collective-permute-done.98.refs_1_ = bf16[384,768]{1,0:T(8,128)(2,1)} collective-permute-done((bf16[384,768]{1,0:T(8,128)(2,1)}, bf16[384,768]{1,0:T(8,128)(2,1)}, u32[]{:S(2)}, u32[]{:S(2)}) %collective-permute-start.98) | collective-permute-done | bytes 589856 | tf_op jit(solution)/shard_map/ppermute | solution.py:37
  538.1 8.3 %collective-permute-done.99 = bf16[768,768]{1,0:T(8,128)(2,1)} collective-permute-done((bf16[768,768]{1,0:T(8,128)(2,1)S(1)}, bf16[768,768]{1,0:T(8,128)(2,1)}, u32[]{:S(2)}, u32[]{:S(2)}) %collective-permute-start.99) | collective-permute-done | bytes 1179680 | tf_op jit(solution)/shard_map/ppermute | solution.py:37
  (403 shorter events, 181.5 us)
Async XLA Ops:
  28.2 28.4 %collective-permute-start.11 = (bf16[768,768]{1,0:T(8,128)(2,1)}, bf16[768,768]{1,0:T(8,128)(2,1)}, u32[]{:S(2)}, u32[]{:S(2)}) collective-permute-start(bf16[768,768]{1,0:T(8,128)(2,1)} %bitcast.49), channel_id=1, source_target_pairs={{0,2},{2,0},{1,3},{3,1},{4,6},{6,4},{5,7},{7,5},{8,10},{10,8},{9,1... | collective-permute-start | bytes 3538952 | tf_op jit(solution)/shard_map/ppermute | solution.py:32
  28.6 60.8 %collective-permute-start.10 = (bf16[2,768,768]{2,1,0:T(8,128)(2,1)}, bf16[2,768,768]{2,1,0:T(8,128)(2,1)}, u32[]{:S(2)}, u32[]{:S(2)}) collective-permute-start(bf16[2,768,768]{2,1,0:T(8,128)(2,1)} %get-tuple-element.220.refs_5_.refs_15_.refs_8_), channel_id=1, source_target_pairs={{0,1},{1,0},{2,3},{3,2},{4,5},{5,4},{6,7},{7,6},{8,9},{9,8},{10,11... | collective-permute-start | bytes 7077896 | tf_op jit(solution)/shard_map/ppermute | solution.py:28
  32.3 29.0 %collective-permute-start.7 = (bf16[2,192,768]{2,1,0:T(8,128)(2,1)S(1)}, bf16[2,192,768]{2,1,0:T(8,128)(2,1)S(1)}, u32[]{:S(2)}, u32[]{:S(2)}) collective-permute-start(bf16[2,192,768]{2,1,0:T(8,128)(2,1)S(1)} %collective-permute-done.5.refs_6_.refs_11_.refs_15_.refs_29_), channel_id=1, source_target_pairs={{0,1},{1,0},{2,3},{3,2},{4,5},{5,4},{6,7},{7,6},{8,9},{9,8},{10,11... | collective-permute-start | bytes 1769480 | tf_op jit(solution)/shard_map/ppermute | solution.py:28
  56.6 27.5 %collective-permute-start.12 = (bf16[768,768]{1,0:T(8,128)(2,1)}, bf16[768,768]{1,0:T(8,128)(2,1)}, u32[]{:S(2)}, u32[]{:S(2)}) collective-permute-start(bf16[768,768]{1,0:T(8,128)(2,1)} %collective-permute-done.11.refs_4_.refs_10_), channel_id=1, source_target_pairs={{0,4},{4,0},{8,12},{12,8},{16,20},{20,16},{24,28},{28,24},{1,5},{5... | collective-permute-start | bytes 3538952 | tf_op jit(solution)/shard_map/ppermute | solution.py:37
  70.8 33.6 %collective-permute-start.13 = (bf16[768,768]{1,0:T(8,128)(2,1)}, bf16[768,768]{1,0:T(8,128)(2,1)}, u32[]{:S(2)}, u32[]{:S(2)}) collective-permute-start(bf16[768,768]{1,0:T(8,128)(2,1)} %collective-permute-done.11.refs_4_.refs_10_), channel_id=1, source_target_pairs={{0,1},{1,0},{2,3},{3,2},{4,5},{5,4},{6,7},{7,6},{8,9},{9,8},{10,11... | collective-permute-start | bytes 3538952 | tf_op jit(solution)/shard_map/ppermute | solution.py:28
  84.2 29.6 %collective-permute-start.15 = (bf16[4,192,768]{2,1,0:T(8,128)(2,1)S(1)}, bf16[4,192,768]{2,1,0:T(8,128)(2,1)S(1)}, u32[]{:S(2)}, u32[]{:S(2)}) collective-permute-start(bf16[4,192,768]{2,1,0:T(8,128)(2,1)S(1)} %copy-done.9), channel_id=1, source_target_pairs={{0,1},{1,0},{2,3},{3,2},{4,5},{5,4},{6,7},{7,6},{8,9},{9,8},{10,11... | collective-permute-start | bytes 3538952 | tf_op jit(solution)/shard_map/ppermute | solution.py:28
  88.9 33.3 %collective-permute-start.23 = (bf16[768,768]{1,0:T(8,128)(2,1)}, bf16[768,768]{1,0:T(8,128)(2,1)}, u32[]{:S(2)}, u32[]{:S(2)}) collective-permute-start(bf16[768,768]{1,0:T(8,128)(2,1)} %bitcast.48), channel_id=1, source_target_pairs={{0,2},{2,0},{1,3},{3,1},{4,6},{6,4},{5,7},{7,5},{8,10},{10,8},{9,1... | collective-permute-start | bytes 3538952 | tf_op jit(solution)/shard_map/ppermute | solution.py:32
  104.9 45.9 %collective-permute-start.22 = (bf16[2,768,768]{2,1,0:T(8,128)(2,1)S(1)}, bf16[2,768,768]{2,1,0:T(8,128)(2,1)}, u32[]{:S(2)}, u32[]{:S(2)}) collective-permute-start(bf16[2,768,768]{2,1,0:T(8,128)(2,1)S(1)} %copy-done.10), channel_id=1, source_target_pairs={{0,1},{1,0},{2,3},{3,2},{4,5},{5,4},{6,7},{7,6},{8,9},{9,8},{10,11... | collective-permute-start | bytes 7077896 | tf_op jit(solution)/shard_map/ppermute | solution.py:28
  122.2 28.6 %collective-permute-start.24 = (bf16[768,768]{1,0:T(8,128)(2,1)}, bf16[768,768]{1,0:T(8,128)(2,1)S(1)}, u32[]{:S(2)}, u32[]{:S(2)}) collective-permute-start(bf16[768,768]{1,0:T(8,128)(2,1)} %collective-permute-done.23.refs_4_.refs_10_), channel_id=1, source_target_pairs={{0,4},{4,0},{8,12},{12,8},{16,20},{20,16},{24,28},{28,24},{1,5},{5... | collective-permute-start | bytes 3538952 | tf_op jit(solution)/shard_map/ppermute | solution.py:37
  131.8 30.1 %collective-permute-start.25 = (bf16[768,768]{1,0:T(8,128)(2,1)}, bf16[768,768]{1,0:T(8,128)(2,1)S(1)}, u32[]{:S(2)}, u32[]{:S(2)}) collective-permute-start(bf16[768,768]{1,0:T(8,128)(2,1)} %collective-permute-done.23.refs_4_.refs_10_), channel_id=1, source_target_pairs={{0,1},{1,0},{2,3},{3,2},{4,5},{5,4},{6,7},{7,6},{8,9},{9,8},{10,11... | collective-permute-start | bytes 3538952 | tf_op jit(solution)/shard_map/ppermute | solution.py:28
  192.5 22.8 %collective-permute-start.35 = (bf16[2,192,768]{2,1,0:T(8,128)(2,1)}, bf16[2,192,768]{2,1,0:T(8,128)(2,1)S(1)}, u32[]{:S(2)}, u32[]{:S(2)}) collective-permute-start(bf16[2,192,768]{2,1,0:T(8,128)(2,1)} %get-tuple-element.288), channel_id=1, source_target_pairs={{0,1},{1,0},{2,3},{3,2},{4,5},{5,4},{6,7},{7,6},{8,9},{9,8},{10,11... | collective-permute-start | bytes 1769480 | tf_op jit(solution)/shard_map/ppermute | solution.py:28
  223.4 28.5 %collective-permute-start.40 = (bf16[2,384,768]{2,1,0:T(8,128)(2,1)}, bf16[2,384,768]{2,1,0:T(8,128)(2,1)S(1)}, u32[]{:S(2)}, u32[]{:S(2)}) collective-permute-start(bf16[2,384,768]{2,1,0:T(8,128)(2,1)} %get-tuple-element.300), channel_id=1, source_target_pairs={{0,4},{4,0},{8,12},{12,8},{16,20},{20,16},{24,28},{28,24},{1,5},{5... | collective-permute-start | bytes 3538952 | tf_op jit(solution)/shard_map/ppermute | solution.py:37
  225.1 28.2 %collective-permute-start.39 = (bf16[2,384,768]{2,1,0:T(8,128)(2,1)}, bf16[2,384,768]{2,1,0:T(8,128)(2,1)S(1)}, u32[]{:S(2)}, u32[]{:S(2)}) collective-permute-start(bf16[2,384,768]{2,1,0:T(8,128)(2,1)} %get-tuple-element.292.refs_32_), channel_id=1, source_target_pairs={{0,2},{2,0},{1,3},{3,1},{4,6},{6,4},{5,7},{7,5},{8,10},{10,8},{9,1... | collective-permute-start | bytes 3538952 | tf_op jit(solution)/shard_map/ppermute | solution.py:32
  247.4 33.6 %collective-permute-start.44 = (bf16[4,96,768]{2,1,0:T(8,128)(2,1)}, bf16[4,96,768]{2,1,0:T(8,128)(2,1)S(1)}, u32[]{:S(2)}, u32[]{:S(2)}) collective-permute-start(bf16[4,96,768]{2,1,0:T(8,128)(2,1)} %get-tuple-element.314), channel_id=1, source_target_pairs={{0,1},{1,0},{2,3},{3,2},{4,5},{5,4},{6,7},{7,6},{8,9},{9,8},{10,11... | collective-permute-start | bytes 1769480 | tf_op jit(solution)/shard_map/ppermute | solution.py:28
  247.7 33.3 %collective-permute-start.45 = (bf16[4,96,768]{2,1,0:T(8,128)(2,1)}, bf16[4,96,768]{2,1,0:T(8,128)(2,1)S(1)}, u32[]{:S(2)}, u32[]{:S(2)}) collective-permute-start(bf16[4,96,768]{2,1,0:T(8,128)(2,1)} %get-tuple-element.315), channel_id=1, source_target_pairs={{0,1},{1,0},{2,3},{3,2},{4,5},{5,4},{6,7},{7,6},{8,9},{9,8},{10,11... | collective-permute-start | bytes 1769480 | tf_op jit(solution)/shard_map/ppermute | solution.py:28
  251.9 29.7 %collective-permute-start.46 = (bf16[4,96,768]{2,1,0:T(8,128)(2,1)}, bf16[4,96,768]{2,1,0:T(8,128)(2,1)S(1)}, u32[]{:S(2)}, u32[]{:S(2)}) collective-permute-start(bf16[4,96,768]{2,1,0:T(8,128)(2,1)} %get-tuple-element.316), channel_id=1, source_target_pairs={{0,1},{1,0},{2,3},{3,2},{4,5},{5,4},{6,7},{7,6},{8,9},{9,8},{10,11... | collective-permute-start | bytes 1769480 | tf_op jit(solution)/shard_map/ppermute | solution.py:28
  258.6 23.1 %collective-permute-start.41 = (bf16[384,768]{1,0:T(8,128)(2,1)}, bf16[384,768]{1,0:T(8,128)(2,1)S(1)}, u32[]{:S(2)}, u32[]{:S(2)}) collective-permute-start(bf16[384,768]{1,0:T(8,128)(2,1)} %get-tuple-element.308), channel_id=1, source_target_pairs={{0,4},{4,0},{8,12},{12,8},{16,20},{20,16},{24,28},{28,24},{1,5},{5... | collective-permute-start | bytes 1769480 | tf_op jit(solution)/shard_map/ppermute | solution.py:37
  259.3 22.8 %collective-permute-start.42 = (bf16[384,768]{1,0:T(8,128)(2,1)}, bf16[384,768]{1,0:T(8,128)(2,1)S(1)}, u32[]{:S(2)}, u32[]{:S(2)}) collective-permute-start(bf16[384,768]{1,0:T(8,128)(2,1)} %get-tuple-element.310), channel_id=1, source_target_pairs={{0,2},{2,0},{1,3},{3,1},{4,6},{6,4},{5,7},{7,5},{8,10},{10,8},{9,1... | collective-permute-start | bytes 1769480 | tf_op jit(solution)/shard_map/ppermute | solution.py:32
  289.4 23.3 %collective-permute-start.60 = (bf16[2,192,768]{2,1,0:T(8,128)(2,1)}, bf16[2,192,768]{2,1,0:T(8,128)(2,1)S(1)}, u32[]{:S(2)}, u32[]{:S(2)}) collective-permute-start(bf16[2,192,768]{2,1,0:T(8,128)(2,1)} %get-tuple-element.346), channel_id=1, source_target_pairs={{0,1},{1,0},{2,3},{3,2},{4,5},{5,4},{6,7},{7,6},{8,9},{9,8},{10,11... | collective-permute-start | bytes 1769480 | tf_op jit(solution)/shard_map/ppermute | solution.py:28
  289.7 23.0 %collective-permute-start.61 = (bf16[2,192,768]{2,1,0:T(8,128)(2,1)}, bf16[2,192,768]{2,1,0:T(8,128)(2,1)S(1)}, u32[]{:S(2)}, u32[]{:S(2)}) collective-permute-start(bf16[2,192,768]{2,1,0:T(8,128)(2,1)} %get-tuple-element.347), channel_id=1, source_target_pairs={{0,1},{1,0},{2,3},{3,2},{4,5},{5,4},{6,7},{7,6},{8,9},{9,8},{10,11... | collective-permute-start | bytes 1769480 | tf_op jit(solution)/shard_map/ppermute | solution.py:28
  289.9 23.3 %collective-permute-start.51 = (bf16[384,768]{1,0:T(8,128)(2,1)}, bf16[384,768]{1,0:T(8,128)(2,1)S(1)}, u32[]{:S(2)}, u32[]{:S(2)}) collective-permute-start(bf16[384,768]{1,0:T(8,128)(2,1)} %get-tuple-element.333), channel_id=1, source_target_pairs={{0,8},{4,12},{8,0},{12,4},{16,24},{20,28},{24,16},{28,20},{1,9},{5... | collective-permute-start | bytes 1769480 | tf_op jit(solution)/shard_map/ppermute | solution.py:37
  361.6 33.0 %collective-permute-start.71 = (bf16[2,384,768]{2,1,0:T(8,128)(2,1)}, bf16[2,384,768]{2,1,0:T(8,128)(2,1)S(1)}, u32[]{:S(2)}, u32[]{:S(2)}) collective-permute-start(bf16[2,384,768]{2,1,0:T(8,128)(2,1)} %get-tuple-element.366), channel_id=1, source_target_pairs={{0,2},{2,0},{1,3},{3,1},{4,6},{6,4},{5,7},{7,5},{8,10},{10,8},{9,1... | collective-permute-start | bytes 3538952 | tf_op jit(solution)/shard_map/ppermute | solution.py:32
  363.1 31.5 %collective-permute-start.72 = (bf16[2,384,768]{2,1,0:T(8,128)(2,1)}, bf16[2,384,768]{2,1,0:T(8,128)(2,1)S(1)}, u32[]{:S(2)}, u32[]{:S(2)}) collective-permute-start(bf16[2,384,768]{2,1,0:T(8,128)(2,1)} %get-tuple-element.368), channel_id=1, source_target_pairs={{0,4},{4,0},{8,12},{12,8},{16,20},{20,16},{24,28},{28,24},{1,5},{5... | collective-permute-start | bytes 3538952 | tf_op jit(solution)/shard_map/ppermute | solution.py:37
  370.9 31.5 %collective-permute-start.73 = (bf16[2,192,768]{2,1,0:T(8,128)(2,1)}, bf16[2,192,768]{2,1,0:T(8,128)(2,1)S(1)}, u32[]{:S(2)}, u32[]{:S(2)}) collective-permute-start(bf16[2,192,768]{2,1,0:T(8,128)(2,1)} %get-tuple-element.370), channel_id=1, source_target_pairs={{0,2},{2,0},{1,3},{3,1},{4,6},{6,4},{5,7},{7,5},{8,10},{10,8},{9,1... | collective-permute-start | bytes 1769480 | tf_op jit(solution)/shard_map/ppermute | solution.py:32
  371.6 32.2 %collective-permute-start.74 = (bf16[2,192,768]{2,1,0:T(8,128)(2,1)}, bf16[2,192,768]{2,1,0:T(8,128)(2,1)S(1)}, u32[]{:S(2)}, u32[]{:S(2)}) collective-permute-start(bf16[2,192,768]{2,1,0:T(8,128)(2,1)} %get-tuple-element.372), channel_id=1, source_target_pairs={{0,4},{4,0},{8,12},{12,8},{16,20},{20,16},{24,28},{28,24},{1,5},{5... | collective-permute-start | bytes 1769480 | tf_op jit(solution)/shard_map/ppermute | solution.py:37
  432.4 26.8 %collective-permute-start.86 = (bf16[768,768]{1,0:T(8,128)(2,1)S(1)}, bf16[768,768]{1,0:T(8,128)(2,1)S(1)}, u32[]{:S(2)}, u32[]{:S(2)}) collective-permute-start(bf16[768,768]{1,0:T(8,128)(2,1)S(1)} %get-tuple-element.390.refs_13_), channel_id=1, source_target_pairs={{0,4},{4,0},{8,12},{12,8},{16,20},{20,16},{24,28},{28,24},{1,5},{5... | collective-permute-start | bytes 3538952 | tf_op jit(solution)/shard_map/ppermute | solution.py:37
  433.8 25.4 %collective-permute-start.83 = (bf16[384,768]{1,0:T(8,128)(2,1)S(1)}, bf16[384,768]{1,0:T(8,128)(2,1)S(1)}, u32[]{:S(2)}, u32[]{:S(2)}) collective-permute-start(bf16[384,768]{1,0:T(8,128)(2,1)S(1)} %get-tuple-element.386), channel_id=1, source_target_pairs={{0,8},{4,12},{8,0},{12,4},{16,24},{20,28},{24,16},{28,20},{1,9},{5... | collective-permute-start | bytes 1769480 | tf_op jit(solution)/shard_map/ppermute | solution.py:37
  478.1 26.3 %collective-permute-start.94 = (bf16[384,768]{1,0:T(8,128)(2,1)S(1)}, bf16[384,768]{1,0:T(8,128)(2,1)S(1)}, u32[]{:S(2)}, u32[]{:S(2)}) collective-permute-start(bf16[384,768]{1,0:T(8,128)(2,1)S(1)} %get-tuple-element.400.refs_10_.refs_2_), channel_id=1, source_target_pairs={{0,8},{4,12},{8,0},{12,4},{16,24},{20,28},{24,16},{28,20},{1,9},{5... | collective-permute-start | bytes 1769480 | tf_op jit(solution)/shard_map/ppermute | solution.py:37
  478.2 26.3 %collective-permute-start.91 = (bf16[192,768]{1,0:T(8,128)(2,1)S(1)}, bf16[192,768]{1,0:T(8,128)(2,1)S(1)}, u32[]{:S(2)}, u32[]{:S(2)}) collective-permute-start(bf16[192,768]{1,0:T(8,128)(2,1)S(1)} %get-tuple-element.397.refs_0_), channel_id=1, source_target_pairs={{0,16},{4,20},{8,24},{12,28},{16,0},{20,4},{24,8},{28,12},{1,17},{... | collective-permute-start | bytes 884744 | tf_op jit(solution)/shard_map/ppermute | solution.py:37
  480.7 23.8 %collective-permute-start.92 = (bf16[96,768]{1,0:T(8,128)(2,1)S(1)}, bf16[96,768]{1,0:T(8,128)(2,1)S(1)}, u32[]{:S(2)}, u32[]{:S(2)}) collective-permute-start(bf16[96,768]{1,0:T(8,128)(2,1)S(1)} %get-tuple-element.398.refs_2_), channel_id=1, source_target_pairs={{0,16},{4,20},{8,24},{12,28},{16,0},{20,4},{24,8},{28,12},{1,17},{... | collective-permute-start | bytes 442376 | tf_op jit(solution)/shard_map/ppermute | solution.py:37
  481.2 23.3 %collective-permute-start.93 = (f32[32,768]{1,0:T(8,128)S(1)}, f32[32,768]{1,0:T(8,128)S(1)}, u32[]{:S(2)}, u32[]{:S(2)}) collective-permute-start(f32[32,768]{1,0:T(8,128)S(1)} %get-tuple-element.399.refs_4_), channel_id=1, source_target_pairs={{0,16},{4,20},{8,24},{12,28},{16,0},{20,4},{24,8},{28,12},{1,17},{... | collective-permute-start | bytes 294920 | tf_op jit(solution)/shard_map/ppermute | solution.py:37
  520.5 25.9 %collective-permute-start.99 = (bf16[768,768]{1,0:T(8,128)(2,1)S(1)}, bf16[768,768]{1,0:T(8,128)(2,1)}, u32[]{:S(2)}, u32[]{:S(2)}) collective-permute-start(bf16[768,768]{1,0:T(8,128)(2,1)S(1)} %get-tuple-element.414), channel_id=1, source_target_pairs={{0,4},{4,0},{8,12},{12,8},{16,20},{20,16},{24,28},{28,24},{1,5},{5... | collective-permute-start | bytes 3538952 | tf_op jit(solution)/shard_map/ppermute | solution.py:37
  (154 other events, 1476.8 us)

commit v4 on v3

--- a/solution.py
+++ b/solution.py
@@ -61,7 +61,7 @@
     ),
     (
         ((3, 1), (4, 1), (5, 1), (6, 1), (7, 1), (8, 1), (9, 1)),
-        ((5, 1), (6, 1), (7, 1), (8, 1), (9, 1), (10, 1), (11, 1)),
+        ((5, 1), (6, 1), (7, 1), (8, 1), (9, 1), (10, 1), (13, 1)),
     ),
 )
 SMALL_PLAN = ((3, 1), (4, 1), (5, 1), (6, 1), (7, 1))

time: 563 us -> 567 us (level)
  waiting for transfers between devices: 173 us -> 180 us
    ppermute x35, waiting for transfers between devices: 138 us -> 145 us  [over_bit(): lax.ppermute(values, 'dp', [(at, at ^ 1 << bit) for at in range(size)])]
    unnamed x174 -> x170, local copies, waits for them, and re-layouts: 21.6 us -> 20.8 us
where the time goes in v4:
time: 567 us; the launch traced here: 558 us
  Pallas kernels  271 us (48%)
  waiting for transfers between devices  180 us (32%)
  starting transfers between devices  70.1 us (12%)
  local copies, waits for them, and re-layouts  25.8 us (5%)
  other arithmetic  9.27 us (2%)
    pallas_call x28, Pallas kernels, staged(): pl.pallas_call(kernel, out_shape=list(outs) + list(raw_outs), in_specs=[S...  267 us
    ppermute x35, waiting for transfers between devices, over_bit(): lax.ppermute(values, 'dp', [(at, at ^ 1 << bit) for at in range(size)])  145 us
    ppermute x35, starting transfers between devices, over_bit(): lax.ppermute(values, 'dp', [(at, at ^ 1 << bit) for at in range(size)])  42.3 us
    ppermute x14, waiting for transfers between devices, over_y(): return lax.ppermute(values, 'tensor', ACROSS)  26.5 us
    unnamed x170, local copies, waits for them, and re-layouts  20.8 us
    ppermute x14, starting transfers between devices, over_y(): return lax.ppermute(values, 'tensor', ACROSS)  14.6 us
  transfers between devices with their start and end apart: 100, of which 35 were waited for; matrix products, arithmetic and copies ran while one was open for 1% of the time, Pallas kernels for 40%

profile of v4, /device:TPU:0, one launch (start us, length us, event | category | flops | bytes accessed | tf_op | source)
XLA Modules:
  0.0 557.8 jit_solution(2090813955506884313)
XLA Ops:
  15.9 7.3 %qkv_near.2 = (bf16[416,384]{1,0:T(8,128)(2,1)}, bf16[2,416,384]{2,1,0:T(8,128)(2,1)}, bf16[2,416,384]{2,1,0:T(8,128)(2,1)}, f32[416,384]{1,0:T(8,128)}, f32[416,384]{1,0:T(8,128)}, /*index=5*/bf16[416,768]{1,0:T(8,128)(2,1)}) custom-call(s32[2]{0:T(128)} %pad_add_fusion.1.numbers, f32[1,768]{1,0:T(1,128)} %get-tuple-element.504.refs_0_.refs_21_, ...), custom_call_target="tpu_custom_call" | custom-call | flops 92012544 | bytes 1048576 | tf_op jit(solution)/shard_map/qkv_near/pallas_call | solution.py:188
  34.5 8.3 %attend.4 = (bf16[416,384]{1,0:T(8,128)(2,1)}, f32[416,384]{1,0:T(8,128)}, bf16[6,416,832]{2,1,0:T(8,128)(2,1)}) custom-call(s32[2]{0:T(128)} %pad_add_fusion.1.numbers, bf16[416,384]{1,0:T(8,128)(2,1)} %get-tuple-element.217.refs_2_.refs_0_.refs_5_, bf16[2,416,384]{2,1,0:T(8,128)(2,1)} %get-tuple-element.218.refs_1_.refs_3_.refs_9_, ...), custom_call_target="tpu_custom_call" | custom-call | flops 122683392 | bytes 1048576 | tf_op jit(solution)/shard_map/attend/pallas_call | solution.py:188
  44.4 12.2 %collective-permute-done.11.refs_4_.refs_10_ = bf16[768,768]{1,0:T(8,128)(2,1)} collective-permute-done((bf16[768,768]{1,0:T(8,128)(2,1)}, bf16[768,768]{1,0:T(8,128)(2,1)}, u32[]{:S(2)}, u32[]{:S(2)}) %collective-permute-start.11) | collective-permute-done | bytes 1179680 | tf_op jit(solution)/shard_map/ppermute | solution.py:32
  62.3 7.7 %qkv_far.2 = (bf16[416,384]{1,0:T(8,128)(2,1)}, bf16[2,416,384]{2,1,0:T(8,128)(2,1)}, bf16[2,416,384]{2,1,0:T(8,128)(2,1)}, f32[416,384]{1,0:T(8,128)}, f32[416,384]{1,0:T(8,128)}) custom-call(s32[2]{0:T(128)} %pad_add_fusion.1.numbers, f32[1,768]{1,0:T(1,128)} %get-tuple-element.504.refs_0_.refs_21_, f32[1,768]{1,0:T(1,128)} %get-tuple-element.493.refs_1_, ...), custom_call_target="tpu_custom_call" | custom-call | flops 92012544 | bytes 1048576 | tf_op jit(solution)/shard_map/qkv_far/pallas_call | solution.py:188
  73.3 8.3 %attend.5 = (bf16[416,384]{1,0:T(8,128)(2,1)}, f32[416,384]{1,0:T(8,128)}, bf16[6,416,832]{2,1,0:T(8,128)(2,1)}) custom-call(s32[2]{0:T(128)} %pad_add_fusion.1.numbers, bf16[416,384]{1,0:T(8,128)(2,1)} %get-tuple-element.227.refs_0_.refs_5_.refs_11_.refs_14_, bf16[2,416,384]{2,1,0:T(8,128)(2,1)} %get-tuple-element.228.refs_1_.refs_9_.refs_18_, ...), custom_call_target="tpu_custom_call" | custom-call | flops 122683392 | bytes 1048576 | tf_op jit(solution)/shard_map/attend/pallas_call | solution.py:188
  92.7 11.2 %mlp_near.2 = (f32[416,768]{1,0:T(8,128)}, bf16[416,768]{1,0:T(8,128)(2,1)}, bf16[2,416,768]{2,1,0:T(8,128)(2,1)}, bf16[2,416,768]{2,1,0:T(8,128)(2,1)}, f32[416,768]{1,0:T(8,128)}) custom-call(s32[2]{0:T(128)} %pad_add_fusion.1.numbers, bf16[416,384]{1,0:T(8,128)(2,1)} %get-tuple-element.221.refs_2_.refs_0_.refs_1_.refs_3_, ...), custom_call_target="tpu_custom_call" | custom-call | flops 306708480 | bytes 1048576 | tf_op jit(solution)/shard_map/mlp_near/pallas_call | solution.py:188
  105.0 8.8 %mlp_far.2 = (bf16[2,416,768]{2,1,0:T(8,128)(2,1)}, bf16[2,416,768]{2,1,0:T(8,128)(2,1)}, f32[416,768]{1,0:T(8,128)}) custom-call(s32[2]{0:T(128)} %pad_add_fusion.1.numbers, bf16[416,768]{1,0:T(8,128)(2,1)} %get-tuple-element.232.refs_0_.refs_3_, f32[2,1536]{1,0:T(2,128)} %copy-done.67, f32[2,1536]{1,0:T(2,128)} %copy-done.66, ...), custom_call_target="tpu_custom_call" | custom-call | flops 245366784 | bytes 1048576 | tf_op jit(solution)/shard_map/mlp_far/pallas_call | solution.py:188
  114.8 7.3 %qkv_near.3 = (bf16[416,384]{1,0:T(8,128)(2,1)}, bf16[2,416,384]{2,1,0:T(8,128)(2,1)}, bf16[2,416,384]{2,1,0:T(8,128)(2,1)}, f32[416,384]{1,0:T(8,128)}, f32[416,384]{1,0:T(8,128)}, /*index=5*/bf16[416,768]{1,0:T(8,128)(2,1)}) custom-call(s32[2]{0:T(128)} %pad_add_fusion.1.numbers, f32[1,768]{1,0:T(1,128)} %get-tuple-element.503.refs_0_.refs_21_, ...), custom_call_target="tpu_custom_call" | custom-call | flops 92012544 | bytes 1048576 | tf_op jit(solution)/shard_map/qkv_near/pallas_call | solution.py:188
  124.0 7.3 %qkv_far.3 = (bf16[416,384]{1,0:T(8,128)(2,1)}, bf16[2,416,384]{2,1,0:T(8,128)(2,1)}, bf16[2,416,384]{2,1,0:T(8,128)(2,1)}, f32[416,384]{1,0:T(8,128)}, f32[416,384]{1,0:T(8,128)}) custom-call(s32[2]{0:T(128)} %pad_add_fusion.1.numbers, f32[1,768]{1,0:T(1,128)} %get-tuple-element.503.refs_0_.refs_21_, f32[1,768]{1,0:T(1,128)} %get-tuple-element.494.refs_1_, ...), custom_call_target="tpu_custom_call" | custom-call | flops 92012544 | bytes 1048576 | tf_op jit(solution)/shard_map/qkv_far/pallas_call | solution.py:188
  131.9 8.2 %attend.6 = (bf16[416,384]{1,0:T(8,128)(2,1)}, f32[416,384]{1,0:T(8,128)}, bf16[6,416,832]{2,1,0:T(8,128)(2,1)}) custom-call(s32[2]{0:T(128)} %pad_add_fusion.1.numbers, bf16[416,384]{1,0:T(8,128)(2,1)} %get-tuple-element.238.refs_10_.refs_0_.refs_5_, bf16[2,416,384]{2,1,0:T(8,128)(2,1)} %get-tuple-element.239.refs_1_.refs_3_.refs_9_, ...), custom_call_target="tpu_custom_call" | custom-call | flops 122683392 | bytes 1048576 | tf_op jit(solution)/shard_map/attend/pallas_call | solution.py:188
  141.0 8.6 %attend.7 = (bf16[416,384]{1,0:T(8,128)(2,1)}, f32[416,384]{1,0:T(8,128)}, bf16[6,416,832]{2,1,0:T(8,128)(2,1)}) custom-call(s32[2]{0:T(128)} %pad_add_fusion.1.numbers, bf16[416,384]{1,0:T(8,128)(2,1)} %get-tuple-element.246.refs_5_.refs_0_.refs_11_.refs_14_, bf16[2,416,384]{2,1,0:T(8,128)(2,1)} %get-tuple-element.248.refs_1_.refs_9_.refs_18_, ...), custom_call_target="tpu_custom_call" | custom-call | flops 122683392 | bytes 1048576 | tf_op jit(solution)/shard_map/attend/pallas_call | solution.py:188
  150.8 11.1 %mlp_near.3 = (f32[416,768]{1,0:T(8,128)}, bf16[416,768]{1,0:T(8,128)(2,1)}, bf16[2,416,768]{2,1,0:T(8,128)(2,1)}, bf16[2,416,768]{2,1,0:T(8,128)(2,1)}, f32[416,768]{1,0:T(8,128)}) custom-call(s32[2]{0:T(128)} %pad_add_fusion.1.numbers, bf16[416,384]{1,0:T(8,128)(2,1)} %get-tuple-element.247.refs_5_.refs_0_.refs_1_.refs_3_, ...), custom_call_target="tpu_custom_call" | custom-call | flops 306708480 | bytes 1048576 | tf_op jit(solution)/shard_map/mlp_near/pallas_call | solution.py:188
  163.3 8.5 %mlp_far.3 = (bf16[2,416,768]{2,1,0:T(8,128)(2,1)}, bf16[2,416,768]{2,1,0:T(8,128)(2,1)}, bf16[416,768]{1,0:T(8,128)(2,1)}) custom-call(s32[2]{0:T(128)} %pad_add_fusion.1.numbers, bf16[416,768]{1,0:T(8,128)(2,1)} %get-tuple-element.251.refs_0_.refs_3_, f32[2,1536]{1,0:T(2,128)} %copy-done.67, f32[2,1536]{1,0:T(2,128)} %copy-done.66, ...), custom_call_target="tpu_custom_call" | custom-call | flops 245366784 | bytes 1048576 | tf_op jit(solution)/shard_map/mlp_far/pallas_call | solution.py:188
  171.8 19.5 %mlp_back.2 = (f32[4,768]{1,0:T(4,128)}, f32[4,768]{1,0:T(4,128)}, f32[416,768]{1,0:T(8,128)}, bf16[416,768]{1,0:T(8,128)(2,1)}, bf16[2,768,768]{2,1,0:T(8,128)(...) custom-call(s32[2]{0:T(128)} %pad_add_fusion.1.numbers, ...), custom_call_target="tpu_custom_call" | custom-call | flops 981467136 | bytes 1048576 | tf_op jit(solution)/shard_map/mlp_back/pallas_call | solution.py:188
  195.8 19.3 %attend_back.2 = (bf16[416,384]{1,0:T(8,128)(2,1)}, bf16[2,416,384]{2,1,0:T(8,128)(2,1)}, bf16[416,384]{1,0:T(8,128)(2,1)}, bf16[416,384]{1,0:T(8,128)(2,1)}, bf...) custom-call(s32[2]{0:T(128)} %pad_add_fusion.1.numbers, ...), custom_call_target="tpu_custom_call" | custom-call | flops 490733568 | bytes 1048576 | tf_op jit(solution)/shard_map/attend_back/pallas_call | solution.py:188
  216.7 6.6 %sums.5 = (bf16[2,384,768]{2,1,0:T(8,128)(2,1)}, bf16[2,384,768]{2,1,0:T(8,128)(2,1)}, bf16[2,384,768]{2,1,0:T(8,128)(2,1)}, bf16[2,384,768]{2,1,0:T(8,128)(2,1)}) custom-call(s32[1]{0:T(128)} %bitcast.17.numbers.at, bf16[2,768,768]{2,1,0:T(8,128)(2,1)} %get-tuple-element.282.refs_0_, bf16[2,768,768]{2,1,0:T(8,128)(2,1)} %get-tuple-element.283.refs_1_, ...), custom_call_target="tpu_custom_call" | custom-call | bytes 1048576 | tf_op jit(solution)/shard_map/sums/pallas_call | solution.py:188
  229.8 17.3 %qkv_back.2 = (f32[16,768]{1,0:T(8,128)}, f32[416,768]{1,0:T(8,128)}, bf16[4,192,768]{2,1,0:T(8,128)(2,1)}, bf16[4,96,768]{2,1,0:T(8,128)(2,1)}, bf16[4,96,768]{...) custom-call(s32[2]{0:T(128)} %pad_add_fusion.1.numbers, ...), custom_call_target="tpu_custom_call" | custom-call | flops 490733568 | bytes 1048576 | tf_op jit(solution)/shard_map/qkv_back/pallas_call | solution.py:188
  260.8 20.1 %mlp_back.3 = (f32[4,768]{1,0:T(4,128)}, f32[4,768]{1,0:T(4,128)}, f32[416,768]{1,0:T(8,128)}, bf16[416,768]{1,0:T(8,128)(2,1)}, bf16[2,768,768]{2,1,0:T(8,128)(...) custom-call(s32[2]{0:T(128)} %pad_add_fusion.1.numbers, ...), custom_call_target="tpu_custom_call" | custom-call | flops 981467136 | bytes 1048576 | tf_op jit(solution)/shard_map/mlp_back/pallas_call | solution.py:188
  293.3 19.2 %attend_back.3 = (bf16[416,384]{1,0:T(8,128)(2,1)}, bf16[2,416,384]{2,1,0:T(8,128)(2,1)}, bf16[416,384]{1,0:T(8,128)(2,1)}, bf16[416,384]{1,0:T(8,128)(2,1)}, bf...) custom-call(s32[2]{0:T(128)} %pad_add_fusion.1.numbers, ...), custom_call_target="tpu_custom_call" | custom-call | flops 490733568 | bytes 1048576 | tf_op jit(solution)/shard_map/attend_back/pallas_call | solution.py:188
  314.6 9.1 %sums.8 = (f32[192,768]{1,0:T(8,128)}, bf16[192,768]{1,0:T(8,128)(2,1)}, f32[192,768]{1,0:T(8,128)}, bf16[192,768]{1,0:T(8,128)(2,1)}, f32[192,768]{1,0:T(8,128)...) custom-call(s32[1]{0:T(128)} %bitcast.17.numbers.at, ...), custom_call_target="tpu_custom_call" | custom-call | bytes 1048576 | tf_op jit(solution)/shard_map/sums/pallas_call | solution.py:188
  324.8 18.6 %qkv_back.3 = (f32[32,768]{1,0:T(8,128)}, f32[416,768]{1,0:T(8,128)}, bf16[4,192,768]{2,1,0:T(8,128)(2,1)}, bf16[4,96,768]{2,1,0:T(8,128)(2,1)}, bf16[4,96,768]{...) custom-call(s32[2]{0:T(128)} %pad_add_fusion.1.numbers, ...), custom_call_target="tpu_custom_call" | custom-call | flops 490733568 | bytes 1048576 | tf_op jit(solution)/shard_map/qkv_back/pallas_call | solution.py:188
  348.4 11.6 %collective-permute-done.62.refs_1_.refs_12_ = bf16[192,768]{1,0:T(8,128)(2,1)S(1)} collective-permute-done((bf16[192,768]{1,0:T(8,128)(2,1)S(1)}, bf16[192,768]{1,0:T(8,128)(2,1)S(1)}, u32[]{:S(2)}, u32[]{:S(2)}) %collective-permute-start.62) | collective-permute-done | bytes 294944 | tf_op jit(solution)/shard_map/ppermute | solution.py:37
  372.5 6.7 %collective-permute-done.70.refs_3_.refs_15_ = bf16[192,768]{1,0:T(8,128)(2,1)S(1)} collective-permute-done((bf16[192,768]{1,0:T(8,128)(2,1)}, bf16[192,768]{1,0:T(8,128)(2,1)S(1)}, u32[]{:S(2)}, u32[]{:S(2)}) %collective-permute-start.70) | collective-permute-done | bytes 294944 | tf_op jit(solution)/shard_map/ppermute | solution.py:37
  380.6 13.6 %collective-permute-done.69.refs_1_.refs_14_ = bf16[192,768]{1,0:T(8,128)(2,1)S(1)} collective-permute-done((bf16[192,768]{1,0:T(8,128)(2,1)}, bf16[192,768]{1,0:T(8,128)(2,1)S(1)}, u32[]{:S(2)}, u32[]{:S(2)}) %collective-permute-start.69) | collective-permute-done | bytes 294944 | tf_op jit(solution)/shard_map/ppermute | solution.py:37
  394.2 7.8 %collective-permute-done.73.refs_9_.refs_16_ = bf16[2,192,768]{2,1,0:T(8,128)(2,1)S(1)} collective-permute-done((bf16[2,192,768]{2,1,0:T(8,128)(2,1)}, bf16[2,192,768]{2,1,0:T(8,128)(2,1)S(1)}, u32[]{:S(2)}, u32[]{:S(2)}) %collective-permute-start.73) | collective-permute-done | bytes 589856 | tf_op jit(solution)/shard_map/ppermute | solution.py:32
  415.5 8.8 %collective-permute-done.76.refs_3_.refs_16_ = bf16[96,768]{1,0:T(8,128)(2,1)S(1)} collective-permute-done((bf16[96,768]{1,0:T(8,128)(2,1)S(1)}, bf16[96,768]{1,0:T(8,128)(2,1)S(1)}, u32[]{:S(2)}, u32[]{:S(2)}) %collective-permute-start.76) | collective-permute-done | bytes 147488 | tf_op jit(solution)/shard_map/ppermute | solution.py:37
  439.1 19.8 %collective-permute-done.85.refs_7_.refs_12_ = f32[32,768]{1,0:T(8,128)S(1)} collective-permute-done((f32[32,768]{1,0:T(8,128)S(1)}, f32[32,768]{1,0:T(8,128)S(1)}, u32[]{:S(2)}, u32[]{:S(2)}) %collective-permute-start.85) | collective-permute-done | bytes 98336 | tf_op jit(solution)/shard_map/ppermute | solution.py:37
  468.7 8.9 %collective-permute-done.89.refs_3_.refs_8_ = bf16[96,768]{1,0:T(8,128)(2,1)S(1)} collective-permute-done((bf16[96,768]{1,0:T(8,128)(2,1)S(1)}, bf16[96,768]{1,0:T(8,128)(2,1)S(1)}, u32[]{:S(2)}, u32[]{:S(2)}) %collective-permute-start.89) | collective-permute-done | bytes 147488 | tf_op jit(solution)/shard_map/ppermute | solution.py:37
  480.8 21.9 %collective-permute-done.93.refs_5_.refs_8_ = f32[32,768]{1,0:T(8,128)S(1)} collective-permute-done((f32[32,768]{1,0:T(8,128)S(1)}, f32[32,768]{1,0:T(8,128)S(1)}, u32[]{:S(2)}, u32[]{:S(2)}) %collective-permute-start.93) | collective-permute-done | bytes 98336 | tf_op jit(solution)/shard_map/ppermute | solution.py:37
  511.9 6.2 %collective-permute-done.94.refs_3_.refs_8_ = bf16[384,768]{1,0:T(8,128)(2,1)S(1)} collective-permute-done((bf16[384,768]{1,0:T(8,128)(2,1)S(1)}, bf16[384,768]{1,0:T(8,128)(2,1)S(1)}, u32[]{:S(2)}, u32[]{:S(2)}) %collective-permute-start.94) | collective-permute-done | bytes 589856 | tf_op jit(solution)/shard_map/ppermute | solution.py:37
  522.8 13.8 %collective-permute-done.97.refs_1_ = bf16[384,768]{1,0:T(8,128)(2,1)} collective-permute-done((bf16[384,768]{1,0:T(8,128)(2,1)}, bf16[384,768]{1,0:T(8,128)(2,1)}, u32[]{:S(2)}, u32[]{:S(2)}) %collective-permute-start.97) | collective-permute-done | bytes 589856 | tf_op jit(solution)/shard_map/ppermute | solution.py:37
  536.6 10.5 %collective-permute-done.98.refs_3_ = bf16[384,768]{1,0:T(8,128)(2,1)} collective-permute-done((bf16[384,768]{1,0:T(8,128)(2,1)}, bf16[384,768]{1,0:T(8,128)(2,1)}, u32[]{:S(2)}, u32[]{:S(2)}) %collective-permute-start.98) | collective-permute-done | bytes 589856 | tf_op jit(solution)/shard_map/ppermute | solution.py:37
  (399 shorter events, 181.3 us)
Async XLA Ops:
  28.2 28.4 %collective-permute-start.11 = (bf16[768,768]{1,0:T(8,128)(2,1)}, bf16[768,768]{1,0:T(8,128)(2,1)}, u32[]{:S(2)}, u32[]{:S(2)}) collective-permute-start(bf16[768,768]{1,0:T(8,128)(2,1)} %bitcast.49), channel_id=1, source_target_pairs={{0,2},{2,0},{1,3},{3,1},{4,6},{6,4},{5,7},{7,5},{8,10},{10,8},{9,1... | collective-permute-start | bytes 3538952 | tf_op jit(solution)/shard_map/ppermute | solution.py:32
  28.5 60.8 %collective-permute-start.10 = (bf16[2,768,768]{2,1,0:T(8,128)(2,1)}, bf16[2,768,768]{2,1,0:T(8,128)(2,1)}, u32[]{:S(2)}, u32[]{:S(2)}) collective-permute-start(bf16[2,768,768]{2,1,0:T(8,128)(2,1)} %get-tuple-element.220.refs_5_.refs_15_.refs_8_), channel_id=1, source_target_pairs={{0,1},{1,0},{2,3},{3,2},{4,5},{5,4},{6,7},{7,6},{8,9},{9,8},{10,11... | collective-permute-start | bytes 7077896 | tf_op jit(solution)/shard_map/ppermute | solution.py:28
  32.3 29.0 %collective-permute-start.7 = (bf16[2,192,768]{2,1,0:T(8,128)(2,1)S(1)}, bf16[2,192,768]{2,1,0:T(8,128)(2,1)S(1)}, u32[]{:S(2)}, u32[]{:S(2)}) collective-permute-start(bf16[2,192,768]{2,1,0:T(8,128)(2,1)S(1)} %collective-permute-done.5.refs_6_.refs_11_.refs_15_.refs_29_), channel_id=1, source_target_pairs={{0,1},{1,0},{2,3},{3,2},{4,5},{5,4},{6,7},{7,6},{8,9},{9,8},{10,11... | collective-permute-start | bytes 1769480 | tf_op jit(solution)/shard_map/ppermute | solution.py:28
  56.6 27.5 %collective-permute-start.12 = (bf16[768,768]{1,0:T(8,128)(2,1)}, bf16[768,768]{1,0:T(8,128)(2,1)}, u32[]{:S(2)}, u32[]{:S(2)}) collective-permute-start(bf16[768,768]{1,0:T(8,128)(2,1)} %collective-permute-done.11.refs_4_.refs_10_), channel_id=1, source_target_pairs={{0,4},{4,0},{8,12},{12,8},{16,20},{20,16},{24,28},{28,24},{1,5},{5... | collective-permute-start | bytes 3538952 | tf_op jit(solution)/shard_map/ppermute | solution.py:37
  70.8 33.6 %collective-permute-start.13 = (bf16[768,768]{1,0:T(8,128)(2,1)}, bf16[768,768]{1,0:T(8,128)(2,1)}, u32[]{:S(2)}, u32[]{:S(2)}) collective-permute-start(bf16[768,768]{1,0:T(8,128)(2,1)} %collective-permute-done.11.refs_4_.refs_10_), channel_id=1, source_target_pairs={{0,1},{1,0},{2,3},{3,2},{4,5},{5,4},{6,7},{7,6},{8,9},{9,8},{10,11... | collective-permute-start | bytes 3538952 | tf_op jit(solution)/shard_map/ppermute | solution.py:28
  84.2 29.6 %collective-permute-start.15 = (bf16[4,192,768]{2,1,0:T(8,128)(2,1)S(1)}, bf16[4,192,768]{2,1,0:T(8,128)(2,1)S(1)}, u32[]{:S(2)}, u32[]{:S(2)}) collective-permute-start(bf16[4,192,768]{2,1,0:T(8,128)(2,1)S(1)} %copy-done.7), channel_id=1, source_target_pairs={{0,1},{1,0},{2,3},{3,2},{4,5},{5,4},{6,7},{7,6},{8,9},{9,8},{10,11... | collective-permute-start | bytes 3538952 | tf_op jit(solution)/shard_map/ppermute | solution.py:28
  88.9 33.3 %collective-permute-start.23 = (bf16[768,768]{1,0:T(8,128)(2,1)}, bf16[768,768]{1,0:T(8,128)(2,1)}, u32[]{:S(2)}, u32[]{:S(2)}) collective-permute-start(bf16[768,768]{1,0:T(8,128)(2,1)} %bitcast.48), channel_id=1, source_target_pairs={{0,2},{2,0},{1,3},{3,1},{4,6},{6,4},{5,7},{7,5},{8,10},{10,8},{9,1... | collective-permute-start | bytes 3538952 | tf_op jit(solution)/shard_map/ppermute | solution.py:32
  104.9 45.9 %collective-permute-start.22 = (bf16[2,768,768]{2,1,0:T(8,128)(2,1)S(1)}, bf16[2,768,768]{2,1,0:T(8,128)(2,1)}, u32[]{:S(2)}, u32[]{:S(2)}) collective-permute-start(bf16[2,768,768]{2,1,0:T(8,128)(2,1)S(1)} %copy-done.8), channel_id=1, source_target_pairs={{0,1},{1,0},{2,3},{3,2},{4,5},{5,4},{6,7},{7,6},{8,9},{9,8},{10,11... | collective-permute-start | bytes 7077896 | tf_op jit(solution)/shard_map/ppermute | solution.py:28
  122.2 28.6 %collective-permute-start.24 = (bf16[768,768]{1,0:T(8,128)(2,1)}, bf16[768,768]{1,0:T(8,128)(2,1)S(1)}, u32[]{:S(2)}, u32[]{:S(2)}) collective-permute-start(bf16[768,768]{1,0:T(8,128)(2,1)} %collective-permute-done.23.refs_4_.refs_10_), channel_id=1, source_target_pairs={{0,4},{4,0},{8,12},{12,8},{16,20},{20,16},{24,28},{28,24},{1,5},{5... | collective-permute-start | bytes 3538952 | tf_op jit(solution)/shard_map/ppermute | solution.py:37
  131.8 30.1 %collective-permute-start.25 = (bf16[768,768]{1,0:T(8,128)(2,1)}, bf16[768,768]{1,0:T(8,128)(2,1)S(1)}, u32[]{:S(2)}, u32[]{:S(2)}) collective-permute-start(bf16[768,768]{1,0:T(8,128)(2,1)} %collective-permute-done.23.refs_4_.refs_10_), channel_id=1, source_target_pairs={{0,1},{1,0},{2,3},{3,2},{4,5},{5,4},{6,7},{7,6},{8,9},{9,8},{10,11... | collective-permute-start | bytes 3538952 | tf_op jit(solution)/shard_map/ppermute | solution.py:28
  192.4 22.7 %collective-permute-start.34 = (bf16[2,192,768]{2,1,0:T(8,128)(2,1)}, bf16[2,192,768]{2,1,0:T(8,128)(2,1)S(1)}, u32[]{:S(2)}, u32[]{:S(2)}) collective-permute-start(bf16[2,192,768]{2,1,0:T(8,128)(2,1)} %get-tuple-element.287), channel_id=1, source_target_pairs={{0,1},{1,0},{2,3},{3,2},{4,5},{5,4},{6,7},{7,6},{8,9},{9,8},{10,11... | collective-permute-start | bytes 1769480 | tf_op jit(solution)/shard_map/ppermute | solution.py:28
  192.4 22.9 %collective-permute-start.35 = (bf16[2,192,768]{2,1,0:T(8,128)(2,1)}, bf16[2,192,768]{2,1,0:T(8,128)(2,1)S(1)}, u32[]{:S(2)}, u32[]{:S(2)}) collective-permute-start(bf16[2,192,768]{2,1,0:T(8,128)(2,1)} %get-tuple-element.288), channel_id=1, source_target_pairs={{0,1},{1,0},{2,3},{3,2},{4,5},{5,4},{6,7},{7,6},{8,9},{9,8},{10,11... | collective-permute-start | bytes 1769480 | tf_op jit(solution)/shard_map/ppermute | solution.py:28
  223.3 28.5 %collective-permute-start.40 = (bf16[2,384,768]{2,1,0:T(8,128)(2,1)}, bf16[2,384,768]{2,1,0:T(8,128)(2,1)S(1)}, u32[]{:S(2)}, u32[]{:S(2)}) collective-permute-start(bf16[2,384,768]{2,1,0:T(8,128)(2,1)} %get-tuple-element.300), channel_id=1, source_target_pairs={{0,4},{4,0},{8,12},{12,8},{16,20},{20,16},{24,28},{28,24},{1,5},{5... | collective-permute-start | bytes 3538952 | tf_op jit(solution)/shard_map/ppermute | solution.py:37
  225.0 28.2 %collective-permute-start.39 = (bf16[2,384,768]{2,1,0:T(8,128)(2,1)}, bf16[2,384,768]{2,1,0:T(8,128)(2,1)S(1)}, u32[]{:S(2)}, u32[]{:S(2)}) collective-permute-start(bf16[2,384,768]{2,1,0:T(8,128)(2,1)} %get-tuple-element.292.refs_32_), channel_id=1, source_target_pairs={{0,2},{2,0},{1,3},{3,1},{4,6},{6,4},{5,7},{7,5},{8,10},{10,8},{9,1... | collective-permute-start | bytes 3538952 | tf_op jit(solution)/shard_map/ppermute | solution.py:32
  247.3 33.6 %collective-permute-start.44 = (bf16[4,96,768]{2,1,0:T(8,128)(2,1)}, bf16[4,96,768]{2,1,0:T(8,128)(2,1)S(1)}, u32[]{:S(2)}, u32[]{:S(2)}) collective-permute-start(bf16[4,96,768]{2,1,0:T(8,128)(2,1)} %get-tuple-element.314), channel_id=1, source_target_pairs={{0,1},{1,0},{2,3},{3,2},{4,5},{5,4},{6,7},{7,6},{8,9},{9,8},{10,11... | collective-permute-start | bytes 1769480 | tf_op jit(solution)/shard_map/ppermute | solution.py:28
  247.6 33.4 %collective-permute-start.45 = (bf16[4,96,768]{2,1,0:T(8,128)(2,1)}, bf16[4,96,768]{2,1,0:T(8,128)(2,1)S(1)}, u32[]{:S(2)}, u32[]{:S(2)}) collective-permute-start(bf16[4,96,768]{2,1,0:T(8,128)(2,1)} %get-tuple-element.315), channel_id=1, source_target_pairs={{0,1},{1,0},{2,3},{3,2},{4,5},{5,4},{6,7},{7,6},{8,9},{9,8},{10,11... | collective-permute-start | bytes 1769480 | tf_op jit(solution)/shard_map/ppermute | solution.py:28
  251.8 29.7 %collective-permute-start.46 = (bf16[4,96,768]{2,1,0:T(8,128)(2,1)}, bf16[4,96,768]{2,1,0:T(8,128)(2,1)S(1)}, u32[]{:S(2)}, u32[]{:S(2)}) collective-permute-start(bf16[4,96,768]{2,1,0:T(8,128)(2,1)} %get-tuple-element.316), channel_id=1, source_target_pairs={{0,1},{1,0},{2,3},{3,2},{4,5},{5,4},{6,7},{7,6},{8,9},{9,8},{10,11... | collective-permute-start | bytes 1769480 | tf_op jit(solution)/shard_map/ppermute | solution.py:28
  258.5 23.1 %collective-permute-start.41 = (bf16[384,768]{1,0:T(8,128)(2,1)}, bf16[384,768]{1,0:T(8,128)(2,1)S(1)}, u32[]{:S(2)}, u32[]{:S(2)}) collective-permute-start(bf16[384,768]{1,0:T(8,128)(2,1)} %get-tuple-element.308), channel_id=1, source_target_pairs={{0,4},{4,0},{8,12},{12,8},{16,20},{20,16},{24,28},{28,24},{1,5},{5... | collective-permute-start | bytes 1769480 | tf_op jit(solution)/shard_map/ppermute | solution.py:37
  259.3 22.8 %collective-permute-start.42 = (bf16[384,768]{1,0:T(8,128)(2,1)}, bf16[384,768]{1,0:T(8,128)(2,1)S(1)}, u32[]{:S(2)}, u32[]{:S(2)}) collective-permute-start(bf16[384,768]{1,0:T(8,128)(2,1)} %get-tuple-element.310), channel_id=1, source_target_pairs={{0,2},{2,0},{1,3},{3,1},{4,6},{6,4},{5,7},{7,5},{8,10},{10,8},{9,1... | collective-permute-start | bytes 1769480 | tf_op jit(solution)/shard_map/ppermute | solution.py:32
  289.3 23.3 %collective-permute-start.60 = (bf16[2,192,768]{2,1,0:T(8,128)(2,1)}, bf16[2,192,768]{2,1,0:T(8,128)(2,1)S(1)}, u32[]{:S(2)}, u32[]{:S(2)}) collective-permute-start(bf16[2,192,768]{2,1,0:T(8,128)(2,1)} %get-tuple-element.346), channel_id=1, source_target_pairs={{0,1},{1,0},{2,3},{3,2},{4,5},{5,4},{6,7},{7,6},{8,9},{9,8},{10,11... | collective-permute-start | bytes 1769480 | tf_op jit(solution)/shard_map/ppermute | solution.py:28
  289.7 23.0 %collective-permute-start.61 = (bf16[2,192,768]{2,1,0:T(8,128)(2,1)}, bf16[2,192,768]{2,1,0:T(8,128)(2,1)S(1)}, u32[]{:S(2)}, u32[]{:S(2)}) collective-permute-start(bf16[2,192,768]{2,1,0:T(8,128)(2,1)} %get-tuple-element.347), channel_id=1, source_target_pairs={{0,1},{1,0},{2,3},{3,2},{4,5},{5,4},{6,7},{7,6},{8,9},{9,8},{10,11... | collective-permute-start | bytes 1769480 | tf_op jit(solution)/shard_map/ppermute | solution.py:28
  289.9 23.3 %collective-permute-start.51 = (bf16[384,768]{1,0:T(8,128)(2,1)}, bf16[384,768]{1,0:T(8,128)(2,1)S(1)}, u32[]{:S(2)}, u32[]{:S(2)}) collective-permute-start(bf16[384,768]{1,0:T(8,128)(2,1)} %get-tuple-element.333), channel_id=1, source_target_pairs={{0,8},{4,12},{8,0},{12,4},{16,24},{20,28},{24,16},{28,20},{1,9},{5... | collective-permute-start | bytes 1769480 | tf_op jit(solution)/shard_map/ppermute | solution.py:37
  361.3 33.0 %collective-permute-start.71 = (bf16[2,384,768]{2,1,0:T(8,128)(2,1)}, bf16[2,384,768]{2,1,0:T(8,128)(2,1)S(1)}, u32[]{:S(2)}, u32[]{:S(2)}) collective-permute-start(bf16[2,384,768]{2,1,0:T(8,128)(2,1)} %get-tuple-element.366), channel_id=1, source_target_pairs={{0,2},{2,0},{1,3},{3,1},{4,6},{6,4},{5,7},{7,5},{8,10},{10,8},{9,1... | collective-permute-start | bytes 3538952 | tf_op jit(solution)/shard_map/ppermute | solution.py:32
  362.8 31.5 %collective-permute-start.72 = (bf16[2,384,768]{2,1,0:T(8,128)(2,1)}, bf16[2,384,768]{2,1,0:T(8,128)(2,1)S(1)}, u32[]{:S(2)}, u32[]{:S(2)}) collective-permute-start(bf16[2,384,768]{2,1,0:T(8,128)(2,1)} %get-tuple-element.368), channel_id=1, source_target_pairs={{0,4},{4,0},{8,12},{12,8},{16,20},{20,16},{24,28},{28,24},{1,5},{5... | collective-permute-start | bytes 3538952 | tf_op jit(solution)/shard_map/ppermute | solution.py:37
  370.5 31.5 %collective-permute-start.73 = (bf16[2,192,768]{2,1,0:T(8,128)(2,1)}, bf16[2,192,768]{2,1,0:T(8,128)(2,1)S(1)}, u32[]{:S(2)}, u32[]{:S(2)}) collective-permute-start(bf16[2,192,768]{2,1,0:T(8,128)(2,1)} %get-tuple-element.370), channel_id=1, source_target_pairs={{0,2},{2,0},{1,3},{3,1},{4,6},{6,4},{5,7},{7,5},{8,10},{10,8},{9,1... | collective-permute-start | bytes 1769480 | tf_op jit(solution)/shard_map/ppermute | solution.py:32
  371.3 32.2 %collective-permute-start.74 = (bf16[2,192,768]{2,1,0:T(8,128)(2,1)}, bf16[2,192,768]{2,1,0:T(8,128)(2,1)S(1)}, u32[]{:S(2)}, u32[]{:S(2)}) collective-permute-start(bf16[2,192,768]{2,1,0:T(8,128)(2,1)} %get-tuple-element.372), channel_id=1, source_target_pairs={{0,4},{4,0},{8,12},{12,8},{16,20},{20,16},{24,28},{28,24},{1,5},{5... | collective-permute-start | bytes 1769480 | tf_op jit(solution)/shard_map/ppermute | solution.py:37
  432.1 26.8 %collective-permute-start.86 = (bf16[768,768]{1,0:T(8,128)(2,1)S(1)}, bf16[768,768]{1,0:T(8,128)(2,1)S(1)}, u32[]{:S(2)}, u32[]{:S(2)}) collective-permute-start(bf16[768,768]{1,0:T(8,128)(2,1)S(1)} %get-tuple-element.390.refs_13_), channel_id=1, source_target_pairs={{0,4},{4,0},{8,12},{12,8},{16,20},{20,16},{24,28},{28,24},{1,5},{5... | collective-permute-start | bytes 3538952 | tf_op jit(solution)/shard_map/ppermute | solution.py:37
  433.6 25.3 %collective-permute-start.83 = (bf16[384,768]{1,0:T(8,128)(2,1)S(1)}, bf16[384,768]{1,0:T(8,128)(2,1)S(1)}, u32[]{:S(2)}, u32[]{:S(2)}) collective-permute-start(bf16[384,768]{1,0:T(8,128)(2,1)S(1)} %get-tuple-element.386), channel_id=1, source_target_pairs={{0,8},{4,12},{8,0},{12,4},{16,24},{20,28},{24,16},{28,20},{1,9},{5... | collective-permute-start | bytes 1769480 | tf_op jit(solution)/shard_map/ppermute | solution.py:37
  477.7 25.0 %collective-permute-start.91 = (bf16[192,768]{1,0:T(8,128)(2,1)S(1)}, bf16[192,768]{1,0:T(8,128)(2,1)S(1)}, u32[]{:S(2)}, u32[]{:S(2)}) collective-permute-start(bf16[192,768]{1,0:T(8,128)(2,1)S(1)} %get-tuple-element.397.refs_0_.refs_9_), channel_id=1, source_target_pairs={{0,16},{4,20},{8,24},{12,28},{16,0},{20,4},{24,8},{28,12},{1,17},{... | collective-permute-start | bytes 884744 | tf_op jit(solution)/shard_map/ppermute | solution.py:37
  477.8 24.9 %collective-permute-start.92 = (bf16[96,768]{1,0:T(8,128)(2,1)S(1)}, bf16[96,768]{1,0:T(8,128)(2,1)S(1)}, u32[]{:S(2)}, u32[]{:S(2)}) collective-permute-start(bf16[96,768]{1,0:T(8,128)(2,1)S(1)} %get-tuple-element.398.refs_2_), channel_id=1, source_target_pairs={{0,16},{4,20},{8,24},{12,28},{16,0},{20,4},{24,8},{28,12},{1,17},{... | collective-permute-start | bytes 442376 | tf_op jit(solution)/shard_map/ppermute | solution.py:37
  519.3 31.8 %collective-permute-start.99 = (bf16[768,768]{1,0:T(8,128)(2,1)S(1)}, bf16[768,768]{1,0:T(8,128)(2,1)}, u32[]{:S(2)}, u32[]{:S(2)}) collective-permute-start(bf16[768,768]{1,0:T(8,128)(2,1)S(1)} %get-tuple-element.414), channel_id=1, source_target_pairs={{0,4},{4,0},{8,12},{12,8},{16,20},{20,16},{24,28},{28,24},{1,5},{5... | collective-permute-start | bytes 3538952 | tf_op jit(solution)/shard_map/ppermute | solution.py:37
  520.3 26.8 %collective-permute-start.98 = (bf16[384,768]{1,0:T(8,128)(2,1)}, bf16[384,768]{1,0:T(8,128)(2,1)}, u32[]{:S(2)}, u32[]{:S(2)}) collective-permute-start(bf16[384,768]{1,0:T(8,128)(2,1)} %get-tuple-element.406.refs_2_), channel_id=1, source_target_pairs={{0,8},{4,12},{8,0},{12,4},{16,24},{20,28},{24,16},{28,20},{1,9},{5... | collective-permute-start | bytes 1769480 | tf_op jit(solution)/shard_map/ppermute | solution.py:37
  (152 other events, 1454.8 us)
